TPU v7x, 32 devices: a whole 2x2x4 slice. The times are simulated.
32 devices in a mesh: dp: 8 (over y, x, core), group: 4 (over z).
Axes of the slice: x: 2, y: 2, z: 4, core: 2. Of those that a mesh axis runs over, the one named last changes fastest.
Arguments:
- question_tokens: bfloat16 [512, 64, 768], P(('dp', 'group')), may hold values from -6 to 6
- question_lengths: int32 [512], P(('dp', 'group')), may hold values from 16 to 64
- passage_tokens: bfloat16 [128, 256, 768], P(('dp', 'group')), may hold values from -6 to 6
- passage_lengths: int32 [128, 4], P(('dp', 'group')), may hold values from 1 to 128, 256 in all within a row
- positives: int32 [512], P(('dp', 'group')), may hold values from 0 to 511
- w_qkv: bfloat16 [2, 768, 2304], replicated, may hold values from -0.21875 to 0.21875
- qv_bias: float32 [2, 2, 768], replicated, may hold values from -3 to 3
- w_out: bfloat16 [2, 768, 768], replicated, may hold values from -1.5 to 1.5
- out_bias: float32 [2, 768], replicated, may hold values from -3 to 3
- norm_gains: float32 [2, 2, 768], replicated, may hold values from 0.1 to 1.9
- norm_biases: float32 [2, 2, 768], replicated, may hold values from -3 to 3
- w_in: bfloat16 [2, 768, 3072], replicated, may hold values from -0.21875 to 0.21875
- in_bias: float32 [2, 3072], replicated, may hold values from -3 to 3
- w_back: bfloat16 [2, 3072, 768], replicated, may hold values from -0.109375 to 0.109375
- back_bias: float32 [2, 768], replicated, may hold values from -3 to 3
Outputs:
- question_vectors: bfloat16 [512, 768], P(('dp', 'group'))
- passage_vectors: bfloat16 [512, 768], P(('dp', 'group'))
- losses: float32 [512], P(('dp', 'group'))
- grad_question_tokens: float32 [512, 64, 768], P(('dp', 'group'))
- grad_passage_tokens: float32 [128, 256, 768], P(('dp', 'group'))
- grad_w_qkv: float32 [2, 768, 2304], P(None, 'dp')
- grad_qv_bias: float32 [2, 2, 768], replicated
- grad_w_out: float32 [2, 768, 768], P(None, 'dp')
- grad_out_bias: float32 [2, 768], replicated
- grad_norm_gains: float32 [2, 2, 768], replicated
- grad_norm_biases: float32 [2, 2, 768], replicated
- grad_w_in: float32 [2, 768, 3072], P(None, 'dp')
- grad_in_bias: float32 [2, 3072], replicated
- grad_w_back: float32 [2, 3072, 768], P(None, 'dp')
- grad_back_bias: float32 [2, 768], replicated
Inputs may be any that keep to these rules, and one draw needn't show every extreme that they name: `question_lengths`: positions at and after a question's length are padding. `passage_lengths`: the 4 lengths of a row sum to 256. `positives`: index among all 512 passages.
All inputs are finite; a program needn't handle non-finite values.
Results may differ from a plain program's by a relative error of at most 0.018.
Values may be sent and summed in bfloat16 or wider, within the bound.
No kernel may reach another device: no remote copies, remote signals or barrier semaphores. Data moves between devices by JAX's collectives and lax.ppermute only.
A program may use at most 384 MiB of HBM per device.

v0:
```python
import functools
import math

import jax
import jax.numpy as jnp
from jax import lax
from jax.experimental import pallas as pl
from jax.experimental.pallas import tpu as pltpu
from jax.sharding import PartitionSpec as P

HEAD_DIM = 64
EPSILON = 1e-12
MASKED = -1000000000.0
EXTRA = 128
BF = jnp.bfloat16
F32 = jnp.float32

NT = (((1,), (1,)), ((), ()))
TN = (((0,), (0,)), ((), ()))
NN = (((1,), (0,)), ((), ()))


def mm(left, right, dims=NN):
    return lax.dot_general(left, right, dims, preferred_element_type=F32)


def row_bounds(packed, len_ref, rows, length):
    bounds = []
    for r in range(rows):
        if packed:
            row, k = r // packed, r % packed
            start = row * length
            for earlier in range(k):
                start = start + len_ref[row, earlier]
            bounds.append((start, start + len_ref[row, k]))
        else:
            bounds.append((r * length, r * length + len_ref[r]))
    return bounds


def column(values, rows):
    at = lax.broadcasted_iota(jnp.int32, (rows, 1), 0)
    result = jnp.zeros((rows, 1), jnp.int32)
    for r, value in enumerate(values):
        result = jnp.where(at == r, value, result)
    return result


def head_mask(rows, heads, width):
    row_head = lax.broadcasted_iota(jnp.int32, (rows * heads, width), 0) // rows
    col_head = lax.broadcasted_iota(jnp.int32, (rows * heads, width), 1) // HEAD_DIM
    return row_head == col_head


def spread_heads(values, heads, mask):
    tiled = jnp.concatenate([values] * heads, axis=0)
    return jnp.where(mask, tiled, jnp.zeros_like(tiled))


def gather_heads(full, heads, rows, mask):
    kept = jnp.where(mask, full, jnp.zeros_like(full))
    return jnp.sum(kept.reshape(heads, rows, full.shape[1]), axis=0)


def start_all(copies):
    for copy in copies:
        copy.start()


def order_of(positives, rows, depth):
    owner = positives // rows
    dp = owner // depth
    return ((dp // 2 * depth + owner % depth) * 2 + dp % 2) * rows + positives % rows


def attend_kernel(pack, lengths, rows, heads, chips, depth, ids, qlen_ref, plen_ref, pos_ref, xq_hbm, xp_hbm, w_hbm, wo_hbm,
                  bias_ref, ob_ref, pack_mine, pack_other, early_mine, early_other, a_ref, p_ref, x_buf, w_buf, wo_buf, sems):
    c, j = ids[0], ids[1]
    width = wo_buf.shape[2]
    part = width // chips
    tokens = x_buf.shape[1]
    copies = []
    for e in range(2):
        own = [pltpu.make_async_copy(xq_hbm if e == 0 else xp_hbm, x_buf.at[e], sems.at[e * 5])]
        for k in range(3):
            span = pl.ds(k * width, width)
            own.append(pltpu.make_async_copy(w_hbm.at[e, :, span], w_buf.at[e, :, span], sems.at[e * 5 + 1 + k]))
        own.append(pltpu.make_async_copy(wo_hbm.at[e], wo_buf.at[e], sems.at[e * 5 + 4]))
        copies.append(own)
    start_all(copies[0] + copies[1])
    mask = head_mask(rows, heads, width)
    pos = order_of(column([pos_ref[r] for r in range(rows)], rows), rows, depth)
    for e in range(2):
        wait = copies[e]
        bounds = row_bounds(pack if e else 0, plen_ref if e else qlen_ref, rows, lengths[e])
        start = column([b[0] for b in bounds], rows)
        stop = column([b[1] for b in bounds], rows)
        lane = lax.broadcasted_iota(jnp.int32, (rows, tokens), 1)
        bias = bias_ref[e]
        wait[0].wait()
        x = x_buf[e]
        x_cls = mm(jnp.where(lane == start, 1.0, 0.0).astype(BF), x)
        xc = x_cls.astype(BF)
        wait[1].wait()
        q = (mm(xc, w_buf[e, :, 0:width]) + bias[0:1, :]).astype(BF)
        wait[2].wait()
        a_low = mm(spread_heads(q, heads, mask), w_buf[e, :, width:2 * width], NT).astype(BF)
        a_ref[e] = a_low
        scores = mm(a_low, x, NT) * 0.125
        lane_all = lax.broadcasted_iota(jnp.int32, scores.shape, 1)
        starts = jnp.concatenate([start] * heads, axis=0)
        stops = jnp.concatenate([stop] * heads, axis=0)
        scores = jnp.where((lane_all >= starts) & (lane_all < stops), scores, MASKED)
        peak = jnp.max(scores, axis=1, keepdims=True)
        shifted = jnp.exp(scores - peak)
        p = shifted / jnp.sum(shifted, axis=1, keepdims=True)
        p_ref[e] = p
        p_low = p.astype(BF)
        sums = jnp.sum(p_low.astype(F32), axis=1, keepdims=True)
        pooled = mm(p_low, x).astype(BF)
        wait[3].wait()
        full = mm(pooled, w_buf[e, :, 2 * width:3 * width]) + sums * bias[1:2, :]
        ctx = gather_heads(full, heads, rows, mask).astype(BF)
        wait[4].wait()
        hidden = x_cls + mm(ctx, wo_buf[e]) + ob_ref[e:e + 1, :]
        mean = jnp.mean(hidden, axis=1, keepdims=True)
        centred = hidden - mean
        rstd = lax.rsqrt(jnp.mean(centred * centred, axis=1, keepdims=True) + EPSILON)
        hat = (centred * rstd).astype(BF)
        rstd_high = rstd.astype(BF).astype(F32)
        lanes = lax.broadcasted_iota(jnp.int32, (rows, EXTRA), 1)
        extra = jnp.where(lanes == 0, rstd_high, 0.0)
        extra = jnp.where(lanes == 1, rstd - rstd_high, extra)
        extra = jnp.where(lanes == 2, (pos // 32).astype(F32), extra)
        extra = jnp.where(lanes == 3, (pos % 32).astype(F32), extra)
        for h in range(heads):
            extra = jnp.where(lanes == 16 + h, sums[h * rows:(h + 1) * rows] - 1.0, extra)
        extra = extra.astype(BF)

        def put(pack_ref, early_ref):
            pack_ref[:, 0:width] = hat
            pack_ref[:, width:] = extra
            for chip in range(chips):
                slot = lax.rem(chip - j + chips, chips)
                cut = slice(chip * part, (chip + 1) * part)
                pieces = [pooled[h * rows:(h + 1) * rows, cut] for h in range(heads)] + [xc[:, cut], ctx[:, cut], q]
                early_ref[slot] = jnp.concatenate(pieces, axis=1)

        @pl.when(c == e)
        def keep():
            put(pack_mine, early_mine)

        @pl.when(c != e)
        def give():
            put(pack_other, early_other)


def gelu_parts(x):
    bell = jnp.exp(-0.5 * x * x)
    t = 1.0 / (1.0 + (0.3275911 * math.sqrt(0.5)) * jnp.abs(x))
    tail = 1.061405429 * 0.5
    for factor in (-1.453152027, 1.421413741, -0.284496736, 0.254829592):
        tail = tail * t + factor * 0.5
    tail = tail * t * bell
    cdf = jnp.where(x >= 0.0, 1.0 - tail, tail)
    return x * cdf, cdf + x * bell * (1.0 / math.sqrt(2.0 * math.pi))


def relative_places(chips, depth, rows, c, j, z):
    for kx in range(chips):
        for kz in range(depth):
            for kc in range(2):
                core = c if kc == 0 else 1 - c
                place = ((lax.rem(j - kx + chips, chips) * depth + lax.rem(z - kz + depth, depth)) * 2 + core) * rows
                yield kx, kz, kc, pl.multiple_of(place, rows)


def doubling(n, masks):
    found = [0]
    for mask in masks:
        found = found + [k ^ mask for k in found]
    assert sorted(found) == list(range(n))
    return found


def depth_masks(depth):
    return [(1 << k) - 1 for k in range(1, depth.bit_length())]


def chip_masks(chips):
    return [1 << k for k in range(chips.bit_length() - 1)]


def place_of(chip, deep, core, depth, rows):
    return pl.multiple_of(((chip * depth + deep) * 2 + core) * rows, rows)


def crossed_blocks(refs, chips, depth, rows, c, j, z, part):
    near = depth // 2
    for at, dz in enumerate(doubling(depth, depth_masks(depth))):
        for kc in range(2):
            core = c if kc == 0 else 1 - c
            first = ((at % near) * 2 + kc) * rows
            for kx in range(chips):
                place = place_of(lax.rem(j - kx + chips, chips), jnp.bitwise_xor(z, dz), core, depth, rows)
                yield refs[at // near], first, 2 * kx * part, place


def over_rows(count, tile, work):
    if tile == count:
        work(pl.ds(0, count))
    else:
        def one(t, carry):
            work(pl.ds(pl.multiple_of(t * tile, tile), tile))
            return carry

        lax.fori_loop(0, count // tile, one, 0)


def forward_kernel(chips, depth, rows, steps, tile, part, ids, *refs):
    blocks = refs[:chips]
    gain_ref, shift_ref, win_ref, inb_ref, wback_ref, backb_ref = refs[chips:chips + 6]
    act_ref, slope_ref, vec_ref, hat2_ref, ex_ref, cut_ref, hat1_ref, total, nl = refs[chips + 6:]
    c, j, z = ids[0], ids[1], ids[2]
    width = vec_ref.shape[1]
    step = pl.program_id(0)

    @pl.when(step == 0)
    def start():
        for kx, kz, kc, place in relative_places(chips, depth, rows, c, j, z):
            at = (kz * 2 + kc) * rows
            hat1_ref[pl.ds(place, rows), :] = blocks[kx][at:at + rows, 0:width]
            ex_ref[pl.ds(place, rows), :] = blocks[kx][at:at + rows, width:].astype(F32)
        gain = gain_ref[c]
        shift = shift_ref[c]
        normed = hat1_ref[...].astype(F32) * gain[0:1, :] + shift[0:1, :]
        low = normed.astype(BF)
        nl[...] = low
        total[...] = normed + backb_ref[pl.ds(c, 1), :]
        source = lax.broadcasted_iota(jnp.int32, (width, part), 0)
        target = lax.broadcasted_iota(jnp.int32, (width, part), 1) + j * part
        cut_ref[...] = mm(low, jnp.where(source == target, 1.0, 0.0).astype(BF)).astype(BF)

    columns = win_ref.shape[2]
    pre = mm(nl[...], win_ref[0]) + inb_ref[pl.ds(c, 1), pl.ds(pl.multiple_of(step * columns, columns), columns)]
    active, slope = gelu_parts(pre)
    active = active.astype(BF)
    fpart = act_ref.shape[2]
    for s in range(columns // fpart):
        act_ref[s] = active[:, s * fpart:(s + 1) * fpart]
    slope_ref[...] = slope.astype(BF)
    total[...] += mm(active, wback_ref[0])

    @pl.when(step == steps - 1)
    def finish():
        gain = gain_ref[c]
        shift = shift_ref[c]

        def normalise(part):
            second = total[part, :]
            mean = jnp.mean(second, axis=1, keepdims=True)
            centred = second - mean
            rstd = lax.rsqrt(jnp.mean(centred * centred, axis=1, keepdims=True) + EPSILON)
            hat = centred * rstd
            hat2_ref[part, :] = hat.astype(BF)
            vec_ref[part, :] = (hat * gain[1:2, :] + shift[1:2, :]).astype(BF)
            ex = ex_ref[part, :]
            lanes = lax.broadcasted_iota(jnp.int32, ex.shape, 1)
            pos = ex[:, 2:3] * 32.0 + ex[:, 3:4]
            ex_ref[part, :] = jnp.where(
                lanes == 0, ex[:, 0:1] + ex[:, 1:2], jnp.where(lanes == 1, rstd, jnp.where(lanes == 2, pos, ex)))

        over_rows(total.shape[0], tile, normalise)


def norm_back(grad, hat, rstd, gain):
    scaled = grad * gain
    inner = jnp.mean(scaled * hat, axis=1, keepdims=True)
    return rstd * (scaled - jnp.mean(scaled, axis=1, keepdims=True) - hat * inner)


def loss_kernel(depth, rows, tile, ids, own_ref, other_ref, ex_ref, hat2_ref, hat1_ref, slope_ref, gain_ref,
                wback_hbm, win_hbm, wout_hbm, second_ref, loss_ref, mine_ref, sib_ref, small_ref, qvec_ref, pvec_ref,
                wide_loss, wback, win, wout, sems):
    c, j, z = ids[0], ids[1], ids[2]
    count, width = own_ref.shape
    scale = 2.0 / math.sqrt(width)
    copies = [pltpu.make_async_copy(wback_hbm.at[c], wback, sems.at[0]),
              pltpu.make_async_copy(win_hbm.at[c], win, sems.at[1]),
              pltpu.make_async_copy(wout_hbm.at[c], wout, sems.at[2])]
    start_all(copies)
    own_at = pl.multiple_of(((j * depth + z) * 2 + c) * rows, rows)

    def softmax_part(questions, passages, pos):
        scores = mm(questions, passages, NT) * scale
        peak = jnp.max(scores, axis=1, keepdims=True)
        shifted = jnp.exp(scores - peak)
        totals = jnp.sum(shifted, axis=1, keepdims=True)
        hit = lax.broadcasted_iota(jnp.int32, scores.shape, 1) == pos.astype(jnp.int32)
        loss = peak + jnp.log(totals) - jnp.sum(jnp.where(hit, scores, 0.0), axis=1, keepdims=True)
        grad = (shifted / totals - jnp.where(hit, 1.0, 0.0)) * scale
        high = grad.astype(BF)
        return loss, high, (grad - high.astype(F32)).astype(BF)

    @pl.when(c == 0)
    def question_side():
        qvec_ref[...] = own_ref[pl.ds(own_at, rows), :]
        pvec_ref[...] = other_ref[pl.ds(own_at, rows), :]

        def work(part):
            loss, high, low = softmax_part(own_ref[part, :], other_ref[...], ex_ref[part, 2:3])
            wide_loss[part, :] = jnp.broadcast_to(loss, (tile, wide_loss.shape[1]))
            second_ref[part, :] = mm(high, other_ref[...]) + mm(low, other_ref[...])

        over_rows(count, tile, work)

    @pl.when(c == 1)
    def passage_side():
        pvec_ref[...] = own_ref[pl.ds(own_at, rows), :]
        qvec_ref[...] = other_ref[pl.ds(own_at, rows), :]
        if tile < count:
            second_ref[...] = jnp.zeros_like(second_ref)

        def work(part):
            loss, high, low = softmax_part(other_ref[part, :], own_ref[...], ex_ref[part, 2:3])
            wide_loss[part, :] = jnp.broadcast_to(loss, (tile, wide_loss.shape[1]))
            piece = mm(high, other_ref[part, :], TN) + mm(low, other_ref[part, :], TN)
            second_ref[...] = piece if tile == count else second_ref[...] + piece

        over_rows(count, tile, work)

    small_ref[...] = jnp.zeros_like(small_ref)
    loss_ref[...] = wide_loss[pl.ds(own_at, rows), :]

    def late_norm(part):
        grad = second_ref[part, :]
        hat = hat2_ref[part, :].astype(F32)
        small_ref[1:2, :] += jnp.sum(grad * hat, axis=0, keepdims=True)
        small_ref[3:4, :] += jnp.sum(grad, axis=0, keepdims=True)
        second = norm_back(grad, hat, ex_ref[part, 1:2], gain_ref[c][1:2, :])
        small_ref[5:6, :] += jnp.sum(second, axis=0, keepdims=True)
        second_ref[part, :] = second

    over_rows(count, tile, late_norm)

    chip_at = pl.multiple_of((j * depth + z) * 2 * rows, 2 * rows)
    second = second_ref[pl.ds(chip_at, 2 * rows), :]
    copies[0].wait()
    pre = (mm(second.astype(BF), wback[...], NT) * slope_ref[...].astype(F32)).astype(BF)
    copies[1].wait()
    normed = second + mm(pre, win[...], NT)
    hidden = norm_back(normed, hat1_ref[...].astype(F32), ex_ref[pl.ds(chip_at, 2 * rows), 0:1], gain_ref[c][0:1, :])
    copies[2].wait()
    ctx = mm(hidden.astype(BF), wout[...], NT).astype(BF).astype(F32)
    both = jnp.concatenate([hidden, ctx], axis=1)
    is_low = c == 0
    mine_ref[...] = jnp.where(is_low, both[:rows], both[rows:])
    sib_ref[...] = jnp.where(is_low, both[rows:], both[:rows])


def split_halves(value, scratch, c, own_ref_set, sib_ref_set):
    half = value.shape[0] // 2
    scratch[...] = value
    own_ref_set(scratch[pl.ds(pl.multiple_of(c * half, half), half), :])
    sib_ref_set(scratch[pl.ds(pl.multiple_of((1 - c) * half, half), half), :].astype(BF))


def backward_kernel(chips, depth, rows, steps, tile, ids, after_ref, second_ref, ex_ref, hat1_ref, slope_ref, wback_ref, win_ref,
                    gain_ref, wout_ref, small_in, gpl_ref, low_ref, hidden_ref, inb_ref, plane_ref, small_ref, acc, gfull):
    c, j, z = ids[0], ids[1], ids[2]
    count, width = second_ref.shape
    step = pl.program_id(0)

    @pl.when(step == 0)
    def start():
        acc[...] = second_ref[...]
        low_ref[...] = second_ref[...].astype(BF)
        small_ref[...] = small_in[...]

    pre = mm(low_ref[...], wback_ref[0], NT) * slope_ref[...].astype(F32)
    inb_ref[...] = jnp.sum(pre, axis=0, keepdims=True)
    pre_low = pre.astype(BF)
    gpl_ref[...] = pre_low
    acc[...] += mm(pre_low, win_ref[0], NT)

    @pl.when(step == steps - 1)
    def finish():
        lanes = lax.broadcasted_iota(jnp.int32, (EXTRA, width), 0)
        heads_of = lax.broadcasted_iota(jnp.int32, (EXTRA, width), 1) // HEAD_DIM
        expand = jnp.where(lanes == heads_of + 16, 1.0, 0.0).astype(BF)

        def early_norm(part):
            grad = acc[part, :]
            hat = hat1_ref[part, :].astype(F32)
            small_ref[0:1, :] += jnp.sum(grad * hat, axis=0, keepdims=True)
            small_ref[2:3, :] += jnp.sum(grad, axis=0, keepdims=True)
            hidden = norm_back(grad, hat, ex_ref[part, 0:1], gain_ref[c][0:1, :])
            small_ref[4:5, :] += jnp.sum(hidden, axis=0, keepdims=True)
            hidden_low = hidden.astype(BF)
            hidden_ref[part, :] = hidden_low
            ctx = mm(hidden_low, wout_ref[0], NT).astype(BF)
            sums = mm(ex_ref[part, :].astype(BF), expand) + 1.0
            small_ref[6:7, :] += jnp.sum(sums * ctx.astype(F32), axis=0, keepdims=True)
            gfull[part, :] = ctx

        over_rows(count, tile, early_norm)
        for kx in range(chips):
            for kc in range(2):
                core = c if kc == 0 else 1 - c
                place = pl.multiple_of(((lax.rem(j - kx + chips, chips) * depth + z) * 2 + core) * rows, rows)
                at = (kx * 2 + kc) * rows
                plane_ref[at:at + rows, :] = gfull[pl.ds(place, rows), :]


def weight_kernel(chips, depth, rows, part, steps, ids, after_ref, near_ref, far_ref, gpl_ref, low_ref, hidden_ref, act_ref, cut_ref,
                  gin_ref, gback_ref, gout_ref, sib_ref, ctx_all, in_scr, back_scr, out_scr):
    c, j, z = ids[0], ids[1], ids[2]
    step = pl.program_id(0)
    width = low_ref.shape[1]
    half = part // 2
    ghalf = back_scr.shape[0] // 2
    columns = gpl_ref.shape[1]
    in_rows = half * (columns * steps // width)

    def set_own(ref):
        def setter(value):
            ref[0] = value
        return setter

    def set_sib(at, rows, lane, lanes):
        def setter(value):
            sib_ref[at:at + rows, lane:lane + lanes] = value
        return setter

    @pl.when(step == 0)
    def start():
        split_halves(mm(act_ref[0], low_ref[...], TN), back_scr, c, set_own(gback_ref), set_sib(in_rows, ghalf, 0, width))
        for ref, first, lane, place in crossed_blocks((near_ref, far_ref), chips, depth, rows, c, j, z, part):
            ctx_all[pl.ds(place, rows), :] = ref[first:first + rows, lane + part:lane + 2 * part]
        split_halves(mm(ctx_all[...], hidden_ref[...], TN), out_scr, c, set_own(gout_ref), set_sib(in_rows + ghalf, half, 0, width))

    piece = mm(cut_ref[...], gpl_ref[...], TN)
    in_scr[...] = piece
    gin_ref[0] = in_scr[pl.ds(pl.multiple_of(c * half, half), half), :]
    other = in_scr[pl.ds(pl.multiple_of((1 - c) * half, half), half), :].astype(BF)
    for s in range(steps):
        @pl.when(step == s)
        def keep():
            set_sib((s * columns // width) * half, half, s * columns % width, columns)(other)


def attend_back_kernel(rows, heads, chips, ids, mine_ref, far_ref, xq_hbm, xp_hbm, w_hbm, bias_ref, p_ref, *refs):
    early = refs[:chips]
    late_mine, late_other, att_ref, b_ref, first_ref, cross_ref, x_buf, w_buf, sems = refs[chips:]
    c, j = ids[0], ids[1]
    width = bias_ref.shape[2]
    part = width // chips
    copies = []
    for e in range(2):
        own = [pltpu.make_async_copy(w_hbm.at[e, :, pl.ds(k * width, width)], w_buf.at[e, k], sems.at[e * 4 + k])
               for k in (2, 1, 0)]
        own.insert(1, pltpu.make_async_copy(xq_hbm if e == 0 else xp_hbm, x_buf.at[e], sems.at[e * 4 + 3]))
        copies.append(own)
    start_all(copies[0] + copies[1])
    cross_ref[...] = jnp.concatenate([b[:, heads * part:(heads + 2) * part] for b in early], axis=1)
    mask = head_mask(rows, heads, width)
    for e in range(2):
        wait = copies[e]
        gg = jnp.where(c == e, mine_ref[...], far_ref[...])
        blocks = spread_heads(gg[:, width:], heads, mask)
        constant = jnp.sum(blocks * bias_ref[e][1:2, :], axis=1, keepdims=True)
        wait[0].wait()
        b_low = mm(blocks.astype(BF), w_buf[e, 2], NT).astype(BF)
        b_ref[e] = b_low
        p = p_ref[e]
        wait[1].wait()
        x = x_buf[e]
        probs = mm(b_low, x, NT) + constant
        att = (p * (probs - jnp.sum(probs * p, axis=1, keepdims=True))).astype(BF)
        att_ref[e] = att
        y_low = mm(att, x).astype(BF)
        wait[2].wait()
        gq_low = (gather_heads(mm(y_low, w_buf[e, 1]), heads, rows, mask) * 0.125).astype(BF)

        def put(late_ref):
            for chip in range(chips):
                slot = lax.rem(chip - j + chips, chips)
                cut = slice(chip * part, (chip + 1) * part)
                late_ref[slot] = jnp.concatenate([y_low[h * rows:(h + 1) * rows, cut] for h in range(heads)] + [gq_low], axis=1)

        @pl.when(c == e)
        def keep():
            put(late_mine)

        @pl.when(c != e)
        def give():
            put(late_other)

        wait[3].wait()
        first_ref[e] = gg[:, 0:width] + mm(gq_low, w_buf[e, 0], NT)


def token_grad_kernel(pack, lengths, rows, heads, ids, after_ref, qlen_ref, plen_ref, att_ref, p_ref, a_ref, b_ref, first_ref,
                      gq_ref, gp_ref):
    tile = gq_ref.shape[0]
    at = pl.program_id(0) * tile
    lane = lax.broadcasted_iota(jnp.int32, (rows, tile), 1) + at
    for e in range(2):
        bounds = row_bounds(pack if e else 0, plen_ref if e else qlen_ref, rows, lengths[e])
        pick = jnp.where(lane == column([b[0] for b in bounds], rows), 1.0, 0.0).astype(BF)
        first = first_ref[e]
        high = first.astype(BF)
        rest = first - high.astype(F32)
        middle = rest.astype(BF)
        last = (rest - middle.astype(F32)).astype(BF)
        left = jnp.concatenate([att_ref[e], p_ref[e].astype(BF), pick, pick, pick], axis=0)
        right = jnp.concatenate([a_ref[e] * jnp.asarray(0.125, BF), b_ref[e], high, middle, last], axis=0)
        out = gp_ref if e else gq_ref
        out[...] = mm(left, right, TN)


def head_sums(factor, vectors, heads, part):
    width = vectors.shape[1]
    full = mm(factor, vectors, TN)
    row_head = lax.broadcasted_iota(jnp.int32, full.shape, 0) // part
    col_head = lax.broadcasted_iota(jnp.int32, full.shape, 1) // HEAD_DIM
    kept = jnp.where(row_head == col_head, full, 0.0)
    return jnp.sum(kept.reshape(heads, part, width), axis=0)


def share_kernel(heads, chips, depth, part, ids, *refs):
    late = refs[:chips]
    early = refs[chips:2 * chips]
    plane_ref = refs[2 * chips]
    outs = refs[2 * chips + 1:2 * chips + 1 + depth]
    scratch = refs[2 * chips + 1 + depth]
    z = ids[2]
    width = plane_ref.shape[1]
    hp = heads * part
    y = jnp.concatenate([b[:, 0:hp] for b in late], axis=0)
    pooled = jnp.concatenate([b[:, 0:hp] for b in early], axis=0)
    q = jnp.concatenate([b[:, hp + 2 * part:] for b in early], axis=0)
    scratch[:, 0:width] = head_sums(y, q, heads, part) * 0.125
    scratch[:, width:] = head_sums(pooled, plane_ref[...], heads, part)
    span = 2 * width // depth
    for k in range(depth):
        at = pl.multiple_of(lax.rem(z + k, depth) * span, span)
        outs[k][...] = scratch[:, pl.ds(at, span)].astype(BF)


def query_kernel(chips, depth, rows, part, ids, after_ref, near_ref, far_ref, low_chips, high_chips, *refs):
    shares = refs[:depth]
    gw_ref, keep_ref, send_ref, bias_ref, x_all, gq_all, q_scr, share_scr = refs[depth:]
    c, j, z = ids[0], ids[1], ids[2]
    for ref, first, lane, place in crossed_blocks((near_ref, far_ref), chips, depth, rows, c, j, z, part):
        x_all[pl.ds(place, rows), :] = ref[first:first + rows, lane:lane + part]
    few = chips // 2
    for at_chip, dx in enumerate(doubling(chips, chip_masks(chips))):
        for at_depth, dz in enumerate(doubling(depth, depth_masks(depth))):
            for kc in range(2):
                core = c if kc == 0 else 1 - c
                place = place_of(jnp.bitwise_xor(j, dx), jnp.bitwise_xor(z, dz), core, depth, rows)
                at = (((at_chip % few) * depth + at_depth) * 2 + kc) * rows
                gq_all[pl.ds(place, rows), :] = (low_chips, high_chips)[at_chip // few][at:at + rows, :]
    gq = gq_all[...]
    half = part // 2
    width = gq.shape[1]
    span = shares[0].shape[1]
    bias = jnp.sum(gq.astype(F32), axis=0, keepdims=True)
    bias_ref[...] = jnp.broadcast_to(bias, bias_ref.shape)
    total = shares[0][...].astype(F32)
    for k in range(1, depth):
        total = total + shares[k][...].astype(F32)
    share_scr[...] = total
    q_scr[...] = mm(x_all[...], gq, TN)
    own = pl.ds(pl.multiple_of(c * half, half), half)
    sib = pl.ds(pl.multiple_of((1 - c) * half, half), half)
    keep_ref[...] = share_scr[own, :].astype(BF)
    gw_ref[...] = q_scr[own, :]
    send_ref[:, 0:span] = share_scr[sib, :].astype(BF)
    send_ref[:, span:] = q_scr[sib, :].astype(BF)


def assemble_kernel(depth, ids, after_ref, *refs):
    shards = refs[:depth]
    own_ref, far_ref, out_ref = refs[depth:]
    c, z = ids[0], ids[2]
    half, width = own_ref.shape
    span = shards[0].shape[1]
    out_ref[c, :, 0:width] = own_ref[...]
    out_ref[1 - c, :, 0:width] = far_ref[:, span:].astype(F32)
    for k in range(depth):
        at = pl.multiple_of(width + lax.rem(z - k + depth, depth) * span, 128)
        out_ref[c, :, pl.ds(at, span)] = shards[k][0:half, :].astype(F32)
        out_ref[1 - c, :, pl.ds(at, span)] = shards[k][half:, :].astype(F32)


def fill_kernel(in_rows, ids, after_ref, in_hbm, back_hbm, out_hbm, sib_ref, gin_ref, gback_ref, gout_ref):
    half, width = gout_ref.shape[1], gout_ref.shape[2]
    ghalf = gback_ref.shape[1]
    for k in range(in_rows // half):
        gin_ref[0, :, k * width:(k + 1) * width] = sib_ref[k * half:(k + 1) * half, :].astype(F32)
    gback_ref[0] = sib_ref[in_rows:in_rows + ghalf, :].astype(F32)
    gout_ref[0] = sib_ref[in_rows + ghalf:, :].astype(F32)


def full_spec(shape):
    return pl.BlockSpec(tuple(shape), lambda *_: (0,) * len(shape))


def shape_of(shape, dtype):
    return jax.ShapeDtypeStruct(tuple(shape), dtype)


ANY = pl.BlockSpec(memory_space=pl.ANY)
SMEM = pl.BlockSpec(memory_space=pltpu.SMEM)


def kernel_call(name, kernel, ids, args, specs, outs, out_specs, scratch=(), grid=(1,), work=(0, 0), aliases=None, vmem=60):
    specs = [full_spec(a.shape) if s is None else s for a, s in zip(args, specs)]
    out_specs = [full_spec(o.shape) if s is None else s for o, s in zip(outs, out_specs)]
    return pl.pallas_call(
        kernel,
        grid_spec=pltpu.PrefetchScalarGridSpec(num_scalar_prefetch=1, grid=grid, in_specs=specs, out_specs=out_specs,
                                               scratch_shapes=list(scratch)),
        out_shape=list(outs),
        input_output_aliases=aliases or {},
        compiler_params=pltpu.CompilerParams(vmem_limit_bytes=vmem * 1024 * 1024),
        cost_estimate=pl.CostEstimate(flops=int(work[0]), bytes_accessed=int(work[1]), transcendentals=0),
        name=name,
    )(ids, *args)


def body(question_tokens, question_lengths, passage_tokens, passage_lengths, positives, w_qkv, qv_bias, w_out, out_bias,
         norm_gains, norm_biases, w_in, in_bias, w_back, back_bias, *, n_dp, depth):
    width = question_tokens.shape[2]
    heads = width // HEAD_DIM
    rows = question_tokens.shape[0]
    pack = passage_lengths.shape[1]
    lengths = (question_tokens.shape[1], passage_tokens.shape[1])
    tokens = rows * lengths[0]
    ff = w_in.shape[2]
    chips = n_dp // 2
    count = n_dp * depth * rows
    part = width // chips
    half = part // 2
    fpart = ff // chips
    hr = heads * rows
    i = lax.axis_index("dp")
    z = lax.axis_index("group")
    c, j = i % 2, i // 2
    ids = jnp.stack([c, j, z]).astype(jnp.int32)
    first = c == 0
    vm = pltpu.VMEM
    dma = pltpu.SemaphoreType.DMA

    def swap(x):
        return lax.ppermute(x, "dp", [(k, k ^ 1) for k in range(n_dp)])

    def to_chip(x, k):
        return lax.ppermute(x, "dp", [(s, ((s // 2 + k) % chips) * 2 + s % 2) for s in range(n_dp)])

    def to_depth(x, k):
        return lax.ppermute(x, "group", [(s, (s + k) % depth) for s in range(depth)])

    def over_depth(x):
        return [x] + [to_depth(x, k) for k in range(1, depth)]

    def over_plane(x):
        return [x] + [to_chip(x, k) for k in range(1, chips)]

    xq = question_tokens.reshape(tokens, width)
    xp = passage_tokens.reshape(tokens, width)

    wide = (heads + 2) * part + width
    pack_mine, pack_other, early_mine, early_other, a_low, probs = kernel_call(
        "attend", functools.partial(attend_kernel, pack, lengths, rows, heads, chips, depth), ids,
        [question_lengths, passage_lengths, positives, xq, xp, w_qkv, w_out, qv_bias, out_bias],
        [SMEM, SMEM, SMEM, ANY, ANY, ANY, ANY, None, None],
        [shape_of((rows, width + EXTRA), BF)] * 2 + [shape_of((chips, rows, wide), BF)] * 2 + [
            shape_of((2, hr, width), BF), shape_of((2, hr, tokens), F32)],
        [None] * 6,
        [vm((2, tokens, width), BF), vm((2, width, 3 * width), BF), vm((2, width, width), BF), dma((10,))],
        work=(6e9, 13e6))

    pair = jnp.concatenate([pack_mine, swap(pack_other)], axis=0)
    plane = over_plane(jnp.concatenate(over_depth(pair), axis=0))

    fc = max(fpart, 384)
    sub = fc // fpart
    steps = ff // fc
    tile = count if count <= 1024 else 128
    row = lambda w: full_spec((count, w))
    act, slope, vec, hat2, ex, cut, hat1 = kernel_call(
        "forward", functools.partial(forward_kernel, chips, depth, rows, steps, tile, part), ids,
        plane + [norm_gains, norm_biases, w_in, in_bias, w_back, back_bias],
        [None] * chips + [None, None, pl.BlockSpec((1, width, fc), lambda s, ids: (ids[0], 0, s)), None,
                          pl.BlockSpec((1, fc, width), lambda s, ids: (ids[0], s, 0)), None],
        [shape_of((chips, count, fpart), BF), shape_of((count, ff), BF), shape_of((count, width), BF),
         shape_of((count, width), BF), shape_of((count, EXTRA), F32), shape_of((count, part), BF), shape_of((count, width), BF)],
        [pl.BlockSpec((sub, count, fpart), lambda s, ids: (s, 0, 0)), pl.BlockSpec((count, fc), lambda s, ids: (0, s)),
         None, None, None, None, None],
        [vm((count, width), F32), vm((count, width), BF)], grid=(steps,), work=(10e9, 18e6))

    vec_other = swap(vec)
    hp = heads * part

    nothing = vec[0:1, 0:1] * jnp.asarray(0.0, BF)
    early_far = swap(early_other + nothing)
    payload = [jnp.concatenate([early_mine[k], early_far[k]], axis=0) for k in range(chips)]
    early = [payload[0]] + [to_chip(payload[k], k) for k in range(1, chips)]

    chip_block = lambda w: pl.BlockSpec((2 * rows, w), lambda s, ids: (ids[1] * depth + ids[2], 0))
    second, loss, gg_mine, gg_sib, small, q_vectors, p_vectors = kernel_call(
        "loss", functools.partial(loss_kernel, depth, rows, tile), ids,
        [vec, vec_other, ex, hat2, hat1, slope, norm_gains, w_back, w_in, w_out],
        [None, None, None, None, chip_block(width), chip_block(ff), None, ANY, ANY, ANY],
        [shape_of((count, width), F32), shape_of((rows, EXTRA), F32), shape_of((rows, 2 * width), F32),
         shape_of((rows, 2 * width), F32), shape_of((8, width), F32), shape_of((rows, width), BF), shape_of((rows, width), BF)],
        [None] * 7,
        [vm((count, EXTRA), F32), vm((ff, width), BF), vm((width, ff), BF), vm((width, width), BF), dma((3,))],
        work=(8e9, 16e6))

    late_mine, late_other, att, b_low, first_rows, crossed = kernel_call(
        "attend_back", functools.partial(attend_back_kernel, rows, heads, chips), ids,
        [gg_mine, swap(gg_sib), xq, xp, w_qkv, qv_bias, probs] + early,
        [None, None, ANY, ANY, ANY, None, None] + [None] * chips,
        [shape_of((chips, rows, hp + width), BF)] * 2 + [
            shape_of((2, hr, tokens), BF), shape_of((2, hr, width), BF), shape_of((2, rows, width), F32),
            shape_of((2 * rows, 2 * width), BF)],
        [None] * 6,
        [vm((2, tokens, width), BF), vm((2, 3, width, width), BF), dma((8,))], work=(6e9, 16e6))

    late_far = swap(late_other)
    payload = [jnp.concatenate([late_mine[k], late_far[k]], axis=0) for k in range(chips)]
    late = [payload[0]] + [to_chip(payload[k], k) for k in range(1, chips)]

    def xor_depth(x, mask):
        return lax.ppermute(x, "group", [(s, s ^ mask) for s in range(depth)])

    def xor_chip(x, mask):
        return lax.ppermute(x, "dp", [(s, s ^ (2 * mask)) for s in range(n_dp)])

    def double(x, step, masks):
        for mask in masks:
            x = jnp.concatenate([x, step(x, mask)], axis=0)
        return x

    near = double(crossed, xor_depth, depth_masks(depth)[:-1])
    far_z = xor_depth(near, depth_masks(depth)[-1])
    gq_column = double(payload[0][:, hp:], xor_depth, depth_masks(depth))
    gq_low = double(gq_column, xor_chip, chip_masks(chips)[:-1])
    gq_high = xor_chip(gq_low, chip_masks(chips)[-1])

    gpl, low, hidden_low, g_inb, g_plane, small = kernel_call(
        "backward", functools.partial(backward_kernel, chips, depth, rows, steps, tile), ids,
        [late_far, second, ex, hat1, slope, w_back, w_in, norm_gains, w_out, small],
        [ANY, None, None, None, pl.BlockSpec((count, fc), lambda s, ids: (0, s)),
         pl.BlockSpec((1, fc, width), lambda s, ids: (ids[0], s, 0)),
         pl.BlockSpec((1, width, fc), lambda s, ids: (ids[0], 0, s)), None,
         pl.BlockSpec((1, width, width), lambda s, ids: (ids[0], 0, 0)), None],
        [shape_of((count, ff), BF), shape_of((count, width), BF), shape_of((count, width), BF), shape_of((1, ff), F32),
         shape_of((chips * 2 * rows, width), BF), shape_of((8, width), F32)],
        [pl.BlockSpec((count, fc), lambda s, ids: (0, s)), None, None, pl.BlockSpec((1, fc), lambda s, ids: (0, s)), None, None],
        [vm((count, width), F32), vm((count, width), BF)], grid=(steps,), work=(12e9, 18e6))

    span = 2 * width // depth
    shares = kernel_call(
        "share", functools.partial(share_kernel, heads, chips, depth, part), ids,
        late + early + [g_plane], [None] * (2 * chips + 1),
        [shape_of((part, span), BF)] * depth, [None] * depth, [vm((part, 2 * width), F32)], work=(1e9, 3e6))
    shares = [shares[0]] + [to_depth(shares[k], k) for k in range(1, depth)]

    ghalf = fpart // 2
    out_block = lambda r, w: pl.BlockSpec((1, r, w), lambda s, ids: (ids[0], 0, 0))
    in_rows = half * ff // width
    gin, gback, gout, sib = kernel_call(
        "weight", functools.partial(weight_kernel, chips, depth, rows, part, steps), ids,
        [shares[0], near, far_z, gpl, low, hidden_low, act, cut],
        [ANY, None, None, pl.BlockSpec((count, fc), lambda s, ids: (0, s)), None, None,
         pl.BlockSpec((1, count, fpart), lambda s, ids: (ids[1], 0, 0)), None],
        [shape_of((2, half, ff), F32), shape_of((2, ghalf, width), F32), shape_of((2, half, width), F32),
         shape_of((in_rows + ghalf + half, width), BF)],
        [pl.BlockSpec((1, half, fc), lambda s, ids: (ids[0], 0, s)), out_block(ghalf, width), out_block(half, width), None],
        [vm((count, part), BF), vm((part, fc), F32), vm((fpart, width), F32), vm((part, width), F32)],
        grid=(steps,), vmem=28 if count <= 1024 else 60, work=(4e9, 12e6))
    sib_far = swap(sib)

    gw_q, keep, send, q_bias = kernel_call(
        "query", functools.partial(query_kernel, chips, depth, rows, part), ids,
        [sib, near, far_z, gq_low, gq_high] + shares, [ANY] + [None] * (depth + 4),
        [shape_of((half, width), F32), shape_of((half, span), BF), shape_of((half, span + width), BF), shape_of((8, width), F32)],
        [None] * 4,
        [vm((count, part), BF), vm((count, width), BF), vm((part, width), F32), vm((part, span), F32)], vmem=20 if count <= 1024 else 60, work=(1e9, 3e6))
    far = swap(send)
    shards = over_depth(jnp.concatenate([keep, far[:, 0:span]], axis=0))
    gx = kernel_call(
        "token_grad", functools.partial(token_grad_kernel, pack, lengths, rows, heads), ids,
        [far, question_lengths, passage_lengths, att, probs, a_low, b_low, first_rows],
        [ANY, SMEM, SMEM, pl.BlockSpec((2, hr, 256), lambda s, ids: (0, 0, s)),
         pl.BlockSpec((2, hr, 256), lambda s, ids: (0, 0, s)), None, None, None],
        [shape_of((tokens, width), F32)] * 2, [pl.BlockSpec((256, width), lambda s, ids: (s, 0))] * 2,
        grid=(tokens // 256,), vmem=24 if count <= 1024 else 60, work=(2e9, 9e6))

    gin, gback, gout = kernel_call(
        "fill", functools.partial(fill_kernel, in_rows), ids, [gx[0], gin, gback, gout, sib_far], [ANY, ANY, ANY, ANY, None],
        [shape_of(gin.shape, F32), shape_of(gback.shape, F32), shape_of(gout.shape, F32)],
        [pl.BlockSpec((1,) + a.shape[1:], lambda s, ids: (1 - ids[0], 0, 0)) for a in (gin, gback, gout)],
        aliases={2: 0, 3: 1, 4: 2}, vmem=20 if count <= 1024 else 60, work=(1e6, 8e6))

    (g_qkv,) = kernel_call(
        "assemble", functools.partial(assemble_kernel, depth), ids, [gout] + shards + [gw_q, far], [ANY] + [None] * (depth + 2),
        [shape_of((2, half, 3 * width), F32)], [None], vmem=20 if count <= 1024 else 60, work=(1e6, 3e6))

    n_in = ff // width
    small_all = jnp.concatenate([small, g_inb.reshape(-1, width), q_bias[0:4]], axis=0)
    small_far = swap(small_all)
    small_all = jnp.stack([jnp.where(first, small_all, small_far), jnp.where(first, small_far, small_all)])
    return (
        q_vectors,
        p_vectors,
        loss[:, 0],
        gx[0].reshape(question_tokens.shape),
        gx[1].reshape(passage_tokens.shape),
        g_qkv,
        jnp.stack([small_all[:, 8 + n_in], small_all[:, 6]], axis=1),
        gout,
        small_all[:, 4],
        small_all[:, 0:2],
        small_all[:, 2:4],
        gin,
        small_all[:, 8:8 + n_in].reshape(2, ff),
        gback,
        small_all[:, 5],
    )


def solution(mesh):
    split = P(("dp", "group"))
    return jax.shard_map(
        functools.partial(body, n_dp=mesh.shape["dp"], depth=mesh.shape["group"]),
        mesh=mesh,
        in_specs=(split, split, split, split, split) + (P(),) * 10,
        out_specs=(split, split, split, split, split, P(None, "dp", None), P(), P(None, "dp", None), P(), P(), P(),
                   P(None, "dp", None), P(), P(None, "dp", None), P()),
        check_vma=False,
    )
```

profile of v0, /device:TPU:0, one launch (start us, length us, event | category | flops | bytes accessed | tf_op | source)
XLA Modules:
  0.0 173.4 jit_solution(16724782332245751793)
XLA Ops:
  1.3 11.7 %attend.1 = (bf16[16,896]{1,0:T(8,128)(2,1)}, bf16[16,896]{1,0:T(8,128)(2,1)}, bf16[4,16,3456]{2,1,0:T(8,128)(2,1)}, bf16[4,16,3456]{2,1,0:T(8,128)(2,1)}, bf16[...) custom-call(s32[3]{0:T(128)} %pad_add_fusion.ids, s32[16]{0:T(128)} %qlen_ref.3, s32[4,4]{1,0:T(4,128)} %plen_ref.3, ...), custom_call_target="tpu_custom_call" | custom-call | flops 6000000000 | bytes 13000000 | tf_op jit(solution)/shard_map/attend/pallas_call | solution.py:622
  14.5 3.0 %collective-permute-start.1 = (bf16[32,896]{1,0:T(8,128)(2,1)S(1)}, bf16[32,896]{1,0:T(8,128)(2,1)S(1)}, u32[]{:S(2)}, u32[]{:S(2)}) collective-permute-start(bf16[32,896]{1,0:T(8,128)(2,1)S(1)} %get-tuple-element.136), channel_id=1, source_target_pairs={{0,1},{1,2},{2,3},{3,0},{4,5},{5,6},{6,7},{7,4},{8,9},{9,10},{10,1... | collective-permute-start | bytes 172040 | tf_op jit(solution)/shard_map/ppermute | solution.py:664
  17.5 2.1 %collective-permute-start.3 = (bf16[32,896]{1,0:T(8,128)(2,1)S(1)}, bf16[32,896]{1,0:T(8,128)(2,1)S(1)}, u32[]{:S(2)}, u32[]{:S(2)}) collective-permute-start(bf16[32,896]{1,0:T(8,128)(2,1)S(1)} %get-tuple-element.136), channel_id=1, source_target_pairs={{0,3},{1,0},{2,1},{3,2},{4,7},{5,4},{6,5},{7,6},{8,11},{9,8},{10,9... | collective-permute-start | bytes 172040 | tf_op jit(solution)/shard_map/ppermute | solution.py:664
  21.9 3.5 %collective-permute-done.2 = bf16[32,896]{1,0:T(8,128)(2,1)S(1)} collective-permute-done((bf16[32,896]{1,0:T(8,128)(2,1)S(1)}, bf16[32,896]{1,0:T(8,128)(2,1)S(1)}, u32[]{:S(2)}, u32[]{:S(2)}) %collective-permute-start.2) | collective-permute-done | bytes 57376 | tf_op jit(solution)/shard_map/ppermute | solution.py:664
  25.5 2.5 %collective-permute-start.6 = (bf16[128,896]{1,0:T(8,128)(2,1)S(1)}, bf16[128,896]{1,0:T(8,128)(2,1)S(1)}, u32[]{:S(2)}, u32[]{:S(2)}) collective-permute-start(bf16[128,896]{1,0:T(8,128)(2,1)S(1)} %constant_dynamic-update-slice_fusion.2.refs_0_), channel_id=1, source_target_pairs={{0,24},{4,28},{8,0},{12,4},{16,8},{20,12},{24,16},{28,20},{1,25},{... | collective-permute-start | bytes 688136 | tf_op jit(solution)/shard_map/ppermute | solution.py:661
  29.1 4.9 %collective-permute-done.6.refs_3_ = bf16[128,896]{1,0:T(8,128)(2,1)S(1)} collective-permute-done((bf16[128,896]{1,0:T(8,128)(2,1)S(1)}, bf16[128,896]{1,0:T(8,128)(2,1)S(1)}, u32[]{:S(2)}, u32[]{:S(2)}) %collective-permute-start.6) | collective-permute-done | bytes 229408 | tf_op jit(solution)/shard_map/ppermute | solution.py:661
  34.0 5.9 %collective-permute-done.5.refs_2_ = bf16[128,896]{1,0:T(8,128)(2,1)S(1)} collective-permute-done((bf16[128,896]{1,0:T(8,128)(2,1)S(1)}, bf16[128,896]{1,0:T(8,128)(2,1)S(1)}, u32[]{:S(2)}, u32[]{:S(2)}) %collective-permute-start.5) | collective-permute-done | bytes 229408 | tf_op jit(solution)/shard_map/ppermute | solution.py:661
  41.3 16.1 %forward.1 = (bf16[4,512,768]{2,1,0:T(8,128)(2,1)}, bf16[512,3072]{1,0:T(8,128)(2,1)}, bf16[512,768]{1,0:T(8,128)(2,1)}, bf16[512,768]{1,0:T(8,128)(2,1)}, f32[5...) custom-call(s32[3]{0:T(128)} %pad_add_fusion.ids, bf16[128,896]{1,0:T(8,128)(2,1)} %copy-done.21, ...), custom_call_target="tpu_custom_call" | custom-call | flops 10000000000 | bytes 18000000 | tf_op jit(solution)/shard_map/forward/pallas_call | solution.py:622
  62.5 2.4 %collective-permute-start.12 = (bf16[32,3456]{1,0:T(8,128)(2,1)S(1)}, bf16[32,3456]{1,0:T(8,128)(2,1)S(1)}, u32[]{:S(2)}, u32[]{:S(2)}) collective-permute-start(bf16[32,3456]{1,0:T(8,128)(2,1)S(1)} %pad_maximum_fusion.5), channel_id=1, source_target_pairs={{0,24},{4,28},{8,0},{12,4},{16,8},{20,12},{24,16},{28,20},{1,25},{... | collective-permute-start | bytes 663560 | tf_op jit(solution)/shard_map/ppermute | solution.py:661
  65.7 10.9 %loss.1 = (f32[512,768]{1,0:T(8,128)}, f32[16,128]{1,0:T(8,128)}, f32[16,1536]{1,0:T(8,128)}, f32[16,1536]{1,0:T(8,128)}, f32[8,768]{1,0:T(8,128)}, /*index=5*/bf16[16,768]{1,0:T(8,128)(2,1)}, bf16[16,768]{1,0:T(8,128)(2,1)}) custom-call(s32[3]{0:T(128)} %pad_add_fusion.ids, bf16[512,768]{1,0:T(8,128)(2,1)} %get-tuple-element.66.own_ref, ...), custom_call_target="tpu_custom_call" | custom-call | flops 8000000000 | bytes 16000000 | tf_op jit(solution)/shard_map/loss/pallas_call | solution.py:622
  78.8 10.7 %attend_back.1 = (bf16[4,16,3072]{2,1,0:T(8,128)(2,1)}, bf16[4,16,3072]{2,1,0:T(8,128)(2,1)}, bf16[2,192,1024]{2,1,0:T(8,128)(2,1)}, bf16[2,192,768]{2,1,0:T(8,1...) custom-call(s32[3]{0:T(128)} %pad_add_fusion.ids, f32[16,1536]{1,0:T(8,128)} %get-tuple-element.74.mine_ref, ...), custom_call_target="tpu_custom_call" | custom-call | flops 6000000000 | bytes 16000000 | tf_op jit(solution)/shard_map/attend_back/pallas_call | solution.py:622
  91.8 3.9 %collective-permute-done.17 = bf16[32,1536]{1,0:T(8,128)(2,1)S(1)} collective-permute-done((bf16[32,1536]{1,0:T(8,128)(2,1)}, bf16[32,1536]{1,0:T(8,128)(2,1)S(1)}, u32[]{:S(2)}, u32[]{:S(2)}) %collective-permute-start.17) | collective-permute-done | bytes 98336 | tf_op jit(solution)/shard_map/ppermute | solution.py:739
  95.7 2.7 %collective-permute-start.18 = (bf16[64,1536]{1,0:T(8,128)(2,1)S(1)}, bf16[64,1536]{1,0:T(8,128)(2,1)S(1)}, u32[]{:S(2)}, u32[]{:S(2)}) collective-permute-start(bf16[64,1536]{1,0:T(8,128)(2,1)S(1)} %constant_dynamic-update-slice_fusion.7.near_ref), channel_id=1, source_target_pairs={{0,3},{1,2},{2,1},{3,0},{4,7},{5,6},{6,5},{7,4},{8,11},{9,10},{10,... | collective-permute-start | bytes 589832 | tf_op jit(solution)/shard_map/ppermute | solution.py:739
  100.3 3.2 %collective-permute-start.16 = (bf16[32,3072]{1,0:T(8,128)(2,1)S(1)}, bf16[32,3072]{1,0:T(8,128)(2,1)}, u32[]{:S(2)}, u32[]{:S(2)}) collective-permute-start(bf16[32,3072]{1,0:T(8,128)(2,1)S(1)} %pad_maximum_fusion.8), channel_id=1, source_target_pairs={{0,24},{4,28},{8,0},{12,4},{16,8},{20,12},{24,16},{28,20},{1,25},{... | collective-permute-start | bytes 589832 | tf_op jit(solution)/shard_map/ppermute | solution.py:661
  106.4 14.3 %backward.1 = (bf16[512,3072]{1,0:T(8,128)(2,1)}, bf16[512,768]{1,0:T(8,128)(2,1)}, bf16[512,768]{1,0:T(8,128)(2,1)}, f32[1,3072]{1,0:T(1,128)}, bf16[128,768]{1,0:T(8,128)(2,1)}, /*index=5*/f32[8,768]{1,0:T(8,128)}) custom-call(s32[3]{0:T(128)} %pad_add_fusion.ids, bf16[4,16,3072]{2,1,0:T(8,128)(2,1)} %copy-done.18, ...), custom_call_target="tpu_custom_call" | custom-call | flops 12000000000 | bytes 18000000 | tf_op jit(solution)/shard_map/backward/pallas_call | solution.py:622
  123.6 3.0 %collective-permute-done.21 = bf16[128,768]{1,0:T(8,128)(2,1)} collective-permute-done((bf16[128,768]{1,0:T(8,128)(2,1)S(1)}, bf16[128,768]{1,0:T(8,128)(2,1)}, u32[]{:S(2)}, u32[]{:S(2)}) %collective-permute-start.21) | collective-permute-done | bytes 196640 | tf_op jit(solution)/shard_map/ppermute | solution.py:742
  129.2 5.3 %share.1 = (bf16[192,384]{1,0:T(8,128)(2,1)}, bf16[192,384]{1,0:T(8,128)(2,1)}, bf16[192,384]{1,0:T(8,128)(2,1)}, bf16[192,384]{1,0:T(8,128)(2,1)}) custom-call(s32[3]{0:T(128)} %pad_add_fusion.ids, bf16[32,3072]{1,0:T(8,128)(2,1)} %pad_maximum_fusion.1.refs_0_, bf16[32,3072]{1,0:T(8,128)(2,1)} %collective-permute-done.14.refs_1_, ...), custom_call_target="tpu_custom_call" | custom-call | flops 1000000000 | bytes 3000000 | tf_op jit(solution)/shard_map/share/pallas_call | solution.py:622
  134.5 3.9 %collective-permute-start.24 = (bf16[192,384]{1,0:T(8,128)(2,1)}, bf16[192,384]{1,0:T(8,128)(2,1)S(1)}, u32[]{:S(2)}, u32[]{:S(2)}) collective-permute-start(bf16[192,384]{1,0:T(8,128)(2,1)} %get-tuple-element.93), channel_id=1, source_target_pairs={{0,2},{1,3},{2,0},{3,1},{4,6},{5,7},{6,4},{7,5},{8,10},{9,11},{10,... | collective-permute-start | bytes 442376 | tf_op jit(solution)/shard_map/ppermute | solution.py:664
  143.2 5.2 %weight.1 = (f32[2,96,3072]{2,1,0:T(8,128)}, f32[2,384,768]{2,1,0:T(8,128)}, f32[2,96,768]{2,1,0:T(8,128)}, bf16[864,768]{1,0:T(8,128)(2,1)S(1)}) custom-call(s32[3]{0:T(128)S(1)} %copy-done.2, bf16[192,384]{1,0:T(8,128)(2,1)S(1)} %copy-done.5, bf16[64,1536]{1,0:T(8,128)(2,1)S(1)} %constant_dynamic-update-slice_fusion.7.near_ref, ...), custom_call_target="tpu_custom_call" | custom-call | flops 4000000000 | bytes 12000000 | tf_op jit(solution)/shard_map/weight/pallas_call | solution.py:622
  153.6 1.9 %collective-permute-start.30 = (bf16[192,384]{1,0:T(8,128)(2,1)S(1)}, bf16[192,384]{1,0:T(8,128)(2,1)S(1)}, u32[]{:S(2)}, u32[]{:S(2)}) collective-permute-start(bf16[192,384]{1,0:T(8,128)(2,1)S(1)} %pad_maximum_fusion.10.refs_0_), channel_id=1, source_target_pairs={{0,3},{1,0},{2,1},{3,2},{4,7},{5,4},{6,5},{7,6},{8,11},{9,8},{10,9... | collective-permute-start | bytes 442376 | tf_op jit(solution)/shard_map/ppermute | solution.py:664
  157.6 5.1 %token_grad.1 = (f32[1024,768]{1,0:T(8,128)}, f32[1024,768]{1,0:T(8,128)}) custom-call(s32[3]{0:T(128)S(1)} %copy-done.2, bf16[96,1152]{1,0:T(8,128)(2,1)S(1)} %collective-permute-done.26.after_ref.refs_5_, s32[16]{0:T(128)S(1)} %copy-done.4, s32[4,4]{1,0:T(4,128)S(1)} %copy-done.3, bf16[2,192,1024]{2,1,0:T(8,128)(2,1)S(1)} %copy-done.9, ...), custom_call_target="tpu_custom_call" | custom-call | flops 2000000000 | bytes 9000000 | tf_op jit(solution)/shard_map/token_grad/pallas_call | solution.py:622
  162.7 1.9 %copy-done = f32[1024,768]{1,0:T(8,128)S(1)} copy-done((f32[1024,768]{1,0:T(8,128)S(1)}, f32[1024,768]{1,0:T(8,128)}, u32[]{:S(2)}) %copy-start) | copy-done | bytes 3145752
  164.6 2.1 %fill.1 = (f32[2,96,3072]{2,1,0:T(8,128)}, f32[2,384,768]{2,1,0:T(8,128)}, f32[2,96,768]{2,1,0:T(8,128)}) custom-call(s32[3]{0:T(128)S(1)} %copy-done.2, f32[1024,768]{1,0:T(8,128)S(1)} %copy-done, f32[2,96,3072]{2,1,0:T(8,128)} %get-tuple-element.102.in_hbm, ...), custom_call_target="tpu_custom_call", output_to_operand_aliasing={{0}: (2, {}), {1}: (3, {}), {2}: (4, {})} | custom-call | flops 1000000 | bytes 8000000 | tf_op jit(solution)/shard_map/fill/pallas_call | solution.py:622
  166.7 3.7 %collective-permute-done.29.refs_2_ = bf16[192,384]{1,0:T(8,128)(2,1)S(1)} collective-permute-done((bf16[192,384]{1,0:T(8,128)(2,1)S(1)}, bf16[192,384]{1,0:T(8,128)(2,1)S(1)}, u32[]{:S(2)}, u32[]{:S(2)}) %collective-permute-start.29) | collective-permute-done | bytes 147488 | tf_op jit(solution)/shard_map/ppermute | solution.py:664
  (151 shorter events, 41.6 us)
Async XLA Ops:
  14.5 7.3 %collective-permute-start.1 = (bf16[32,896]{1,0:T(8,128)(2,1)S(1)}, bf16[32,896]{1,0:T(8,128)(2,1)S(1)}, u32[]{:S(2)}, u32[]{:S(2)}) collective-permute-start(bf16[32,896]{1,0:T(8,128)(2,1)S(1)} %get-tuple-element.136), channel_id=1, source_target_pairs={{0,1},{1,2},{2,3},{3,0},{4,5},{5,6},{6,7},{7,4},{8,9},{9,10},{10,1... | collective-permute-start | bytes 172040 | tf_op jit(solution)/shard_map/ppermute | solution.py:664
  17.5 7.9 %collective-permute-start.3 = (bf16[32,896]{1,0:T(8,128)(2,1)S(1)}, bf16[32,896]{1,0:T(8,128)(2,1)S(1)}, u32[]{:S(2)}, u32[]{:S(2)}) collective-permute-start(bf16[32,896]{1,0:T(8,128)(2,1)S(1)} %get-tuple-element.136), channel_id=1, source_target_pairs={{0,3},{1,0},{2,1},{3,2},{4,7},{5,4},{6,5},{7,6},{8,11},{9,8},{10,9... | collective-permute-start | bytes 172040 | tf_op jit(solution)/shard_map/ppermute | solution.py:664
  25.5 8.5 %collective-permute-start.6 = (bf16[128,896]{1,0:T(8,128)(2,1)S(1)}, bf16[128,896]{1,0:T(8,128)(2,1)S(1)}, u32[]{:S(2)}, u32[]{:S(2)}) collective-permute-start(bf16[128,896]{1,0:T(8,128)(2,1)S(1)} %constant_dynamic-update-slice_fusion.2.refs_0_), channel_id=1, source_target_pairs={{0,24},{4,28},{8,0},{12,4},{16,8},{20,12},{24,16},{28,20},{1,25},{... | collective-permute-start | bytes 688136 | tf_op jit(solution)/shard_map/ppermute | solution.py:661
  28.0 11.9 %collective-permute-start.5 = (bf16[128,896]{1,0:T(8,128)(2,1)S(1)}, bf16[128,896]{1,0:T(8,128)(2,1)S(1)}, u32[]{:S(2)}, u32[]{:S(2)}) collective-permute-start(bf16[128,896]{1,0:T(8,128)(2,1)S(1)} %constant_dynamic-update-slice_fusion.2.refs_0_), channel_id=1, source_target_pairs={{0,16},{4,20},{8,24},{12,28},{16,0},{20,4},{24,8},{28,12},{1,17},{... | collective-permute-start | bytes 688136 | tf_op jit(solution)/shard_map/ppermute | solution.py:661
  28.5 11.4 %collective-permute-start.4 = (bf16[128,896]{1,0:T(8,128)(2,1)S(1)}, bf16[128,896]{1,0:T(8,128)(2,1)S(1)}, u32[]{:S(2)}, u32[]{:S(2)}) collective-permute-start(bf16[128,896]{1,0:T(8,128)(2,1)S(1)} %constant_dynamic-update-slice_fusion.2.refs_0_), channel_id=1, source_target_pairs={{0,8},{4,12},{8,16},{12,20},{16,24},{20,28},{24,0},{28,4},{1,9},{5... | collective-permute-start | bytes 688136 | tf_op jit(solution)/shard_map/ppermute | solution.py:661
  61.2 16.2 %collective-permute-start.10 = (bf16[32,3456]{1,0:T(8,128)(2,1)S(1)}, bf16[32,3456]{1,0:T(8,128)(2,1)S(1)}, u32[]{:S(2)}, u32[]{:S(2)}) collective-permute-start(bf16[32,3456]{1,0:T(8,128)(2,1)S(1)} %pad_maximum_fusion.3), channel_id=1, source_target_pairs={{0,8},{4,12},{8,16},{12,20},{16,24},{20,28},{24,0},{28,4},{1,9},{5... | collective-permute-start | bytes 663560 | tf_op jit(solution)/shard_map/ppermute | solution.py:661
  61.3 16.1 %collective-permute-start.11 = (bf16[32,3456]{1,0:T(8,128)(2,1)S(1)}, bf16[32,3456]{1,0:T(8,128)(2,1)S(1)}, u32[]{:S(2)}, u32[]{:S(2)}) collective-permute-start(bf16[32,3456]{1,0:T(8,128)(2,1)S(1)} %pad_maximum_fusion.4), channel_id=1, source_target_pairs={{0,16},{4,20},{8,24},{12,28},{16,0},{20,4},{24,8},{28,12},{1,17},{... | collective-permute-start | bytes 663560 | tf_op jit(solution)/shard_map/ppermute | solution.py:661
  62.5 15.0 %collective-permute-start.12 = (bf16[32,3456]{1,0:T(8,128)(2,1)S(1)}, bf16[32,3456]{1,0:T(8,128)(2,1)S(1)}, u32[]{:S(2)}, u32[]{:S(2)}) collective-permute-start(bf16[32,3456]{1,0:T(8,128)(2,1)S(1)} %pad_maximum_fusion.5), channel_id=1, source_target_pairs={{0,24},{4,28},{8,0},{12,4},{16,8},{20,12},{24,16},{28,20},{1,25},{... | collective-permute-start | bytes 663560 | tf_op jit(solution)/shard_map/ppermute | solution.py:661
  90.7 7.7 %collective-permute-start.13 = (bf16[4,16,3072]{2,1,0:T(8,128)(2,1)}, bf16[4,16,3072]{2,1,0:T(8,128)(2,1)S(1)}, u32[]{:S(2)}, u32[]{:S(2)}) collective-permute-start(bf16[4,16,3072]{2,1,0:T(8,128)(2,1)} %get-tuple-element.80), channel_id=1, source_target_pairs={{0,4},{4,0},{8,12},{12,8},{16,20},{20,16},{24,28},{28,24},{1,5},{5... | collective-permute-start | bytes 1179656 | tf_op jit(solution)/shard_map/ppermute | solution.py:658
  95.7 42.7 %collective-permute-start.18 = (bf16[64,1536]{1,0:T(8,128)(2,1)S(1)}, bf16[64,1536]{1,0:T(8,128)(2,1)S(1)}, u32[]{:S(2)}, u32[]{:S(2)}) collective-permute-start(bf16[64,1536]{1,0:T(8,128)(2,1)S(1)} %constant_dynamic-update-slice_fusion.7.near_ref), channel_id=1, source_target_pairs={{0,3},{1,2},{2,1},{3,0},{4,7},{5,6},{6,5},{7,4},{8,11},{9,10},{10,... | collective-permute-start | bytes 589832 | tf_op jit(solution)/shard_map/ppermute | solution.py:739
  98.5 6.4 %collective-permute-start.19 = (bf16[32,768]{1,0:T(8,128)(2,1)S(1)}, bf16[32,768]{1,0:T(8,128)(2,1)S(1)}, u32[]{:S(2)}, u32[]{:S(2)}) collective-permute-start(bf16[32,768]{1,0:T(8,128)(2,1)S(1)} %fusion), channel_id=1, source_target_pairs={{0,1},{1,0},{2,3},{3,2},{4,5},{5,4},{6,7},{7,6},{8,9},{9,8},{10,11... | collective-permute-start | bytes 147464 | tf_op jit(solution)/shard_map/ppermute | solution.py:739
  98.6 30.6 %collective-permute-start.14 = (bf16[32,3072]{1,0:T(8,128)(2,1)S(1)}, bf16[32,3072]{1,0:T(8,128)(2,1)}, u32[]{:S(2)}, u32[]{:S(2)}) collective-permute-start(bf16[32,3072]{1,0:T(8,128)(2,1)S(1)} %pad_maximum_fusion.6), channel_id=1, source_target_pairs={{0,8},{4,12},{8,16},{12,20},{16,24},{20,28},{24,0},{28,4},{1,9},{5... | collective-permute-start | bytes 589832 | tf_op jit(solution)/shard_map/ppermute | solution.py:661
  98.7 30.5 %collective-permute-start.15 = (bf16[32,3072]{1,0:T(8,128)(2,1)S(1)}, bf16[32,3072]{1,0:T(8,128)(2,1)}, u32[]{:S(2)}, u32[]{:S(2)}) collective-permute-start(bf16[32,3072]{1,0:T(8,128)(2,1)S(1)} %pad_maximum_fusion.7), channel_id=1, source_target_pairs={{0,16},{4,20},{8,24},{12,28},{16,0},{20,4},{24,8},{28,12},{1,17},{... | collective-permute-start | bytes 589832 | tf_op jit(solution)/shard_map/ppermute | solution.py:661
  100.3 28.9 %collective-permute-start.16 = (bf16[32,3072]{1,0:T(8,128)(2,1)S(1)}, bf16[32,3072]{1,0:T(8,128)(2,1)}, u32[]{:S(2)}, u32[]{:S(2)}) collective-permute-start(bf16[32,3072]{1,0:T(8,128)(2,1)S(1)} %pad_maximum_fusion.8), channel_id=1, source_target_pairs={{0,24},{4,28},{8,0},{12,4},{16,8},{20,12},{24,16},{28,20},{1,25},{... | collective-permute-start | bytes 589832 | tf_op jit(solution)/shard_map/ppermute | solution.py:661
  104.9 15.9 %collective-permute-start.20 = (bf16[64,768]{1,0:T(8,128)(2,1)S(1)}, bf16[64,768]{1,0:T(8,128)(2,1)S(1)}, u32[]{:S(2)}, u32[]{:S(2)}) collective-permute-start(bf16[64,768]{1,0:T(8,128)(2,1)S(1)} %pad_maximum_fusion.11), channel_id=1, source_target_pairs={{0,3},{1,2},{2,1},{3,0},{4,7},{5,6},{6,5},{7,4},{8,11},{9,10},{10,... | collective-permute-start | bytes 294920 | tf_op jit(solution)/shard_map/ppermute | solution.py:739
  120.8 5.8 %collective-permute-start.21 = (bf16[128,768]{1,0:T(8,128)(2,1)S(1)}, bf16[128,768]{1,0:T(8,128)(2,1)}, u32[]{:S(2)}, u32[]{:S(2)}) collective-permute-start(bf16[128,768]{1,0:T(8,128)(2,1)S(1)} %pad_maximum_fusion.9), channel_id=1, source_target_pairs={{0,8},{4,12},{8,0},{12,4},{16,24},{20,28},{24,16},{28,20},{1,9},{5... | collective-permute-start | bytes 589832 | tf_op jit(solution)/shard_map/ppermute | solution.py:742
  127.6 20.9 %collective-permute-start.22 = (bf16[256,768]{1,0:T(8,128)(2,1)S(1)}, bf16[256,768]{1,0:T(8,128)(2,1)S(1)}, u32[]{:S(2)}, u32[]{:S(2)}) collective-permute-start(bf16[256,768]{1,0:T(8,128)(2,1)S(1)} %pad_maximum_fusion.low_chips), channel_id=1, source_target_pairs={{0,16},{4,20},{8,24},{12,28},{16,0},{20,4},{24,8},{28,12},{1,17},{... | collective-permute-start | bytes 1179656 | tf_op jit(solution)/shard_map/ppermute | solution.py:742
  134.5 14.0 %collective-permute-start.23 = (bf16[192,384]{1,0:T(8,128)(2,1)}, bf16[192,384]{1,0:T(8,128)(2,1)S(1)}, u32[]{:S(2)}, u32[]{:S(2)}) collective-permute-start(bf16[192,384]{1,0:T(8,128)(2,1)} %get-tuple-element.92), channel_id=1, source_target_pairs={{0,1},{1,2},{2,3},{3,0},{4,5},{5,6},{6,7},{7,4},{8,9},{9,10},{10,1... | collective-permute-start | bytes 442376 | tf_op jit(solution)/shard_map/ppermute | solution.py:664
  134.5 14.0 %collective-permute-start.24 = (bf16[192,384]{1,0:T(8,128)(2,1)}, bf16[192,384]{1,0:T(8,128)(2,1)S(1)}, u32[]{:S(2)}, u32[]{:S(2)}) collective-permute-start(bf16[192,384]{1,0:T(8,128)(2,1)} %get-tuple-element.93), channel_id=1, source_target_pairs={{0,2},{1,3},{2,0},{3,1},{4,6},{5,7},{6,4},{7,5},{8,10},{9,11},{10,... | collective-permute-start | bytes 442376 | tf_op jit(solution)/shard_map/ppermute | solution.py:664
  138.4 10.1 %collective-permute-start.25 = (bf16[192,384]{1,0:T(8,128)(2,1)}, bf16[192,384]{1,0:T(8,128)(2,1)S(1)}, u32[]{:S(2)}, u32[]{:S(2)}) collective-permute-start(bf16[192,384]{1,0:T(8,128)(2,1)} %get-tuple-element.94), channel_id=1, source_target_pairs={{0,3},{1,0},{2,1},{3,2},{4,7},{5,4},{6,5},{7,6},{8,11},{9,8},{10,9... | collective-permute-start | bytes 442376 | tf_op jit(solution)/shard_map/ppermute | solution.py:664
  148.4 14.3 %collective-permute-start.27 = (bf16[864,768]{1,0:T(8,128)(2,1)S(1)}, bf16[864,768]{1,0:T(8,128)(2,1)S(1)}, u32[]{:S(2)}, u32[]{:S(2)}) collective-permute-start(bf16[864,768]{1,0:T(8,128)(2,1)S(1)} %get-tuple-element.91.after_ref), channel_id=1, source_target_pairs={{0,4},{4,0},{8,12},{12,8},{16,20},{20,16},{24,28},{28,24},{1,5},{5... | collective-permute-start | bytes 3981320 | tf_op jit(solution)/shard_map/ppermute | solution.py:658
  153.6 13.2 %collective-permute-start.30 = (bf16[192,384]{1,0:T(8,128)(2,1)S(1)}, bf16[192,384]{1,0:T(8,128)(2,1)S(1)}, u32[]{:S(2)}, u32[]{:S(2)}) collective-permute-start(bf16[192,384]{1,0:T(8,128)(2,1)S(1)} %pad_maximum_fusion.10.refs_0_), channel_id=1, source_target_pairs={{0,3},{1,0},{2,1},{3,2},{4,7},{5,4},{6,5},{7,6},{8,11},{9,8},{10,9... | collective-permute-start | bytes 442376 | tf_op jit(solution)/shard_map/ppermute | solution.py:664
  155.5 15.0 %collective-permute-start.29 = (bf16[192,384]{1,0:T(8,128)(2,1)S(1)}, bf16[192,384]{1,0:T(8,128)(2,1)S(1)}, u32[]{:S(2)}, u32[]{:S(2)}) collective-permute-start(bf16[192,384]{1,0:T(8,128)(2,1)S(1)} %pad_maximum_fusion.10.refs_0_), channel_id=1, source_target_pairs={{0,2},{1,3},{2,0},{3,1},{4,6},{5,7},{6,4},{7,5},{8,10},{9,11},{10,... | collective-permute-start | bytes 442376 | tf_op jit(solution)/shard_map/ppermute | solution.py:664
  157.1 13.3 %collective-permute-start.28 = (bf16[192,384]{1,0:T(8,128)(2,1)S(1)}, bf16[192,384]{1,0:T(8,128)(2,1)S(1)}, u32[]{:S(2)}, u32[]{:S(2)}) collective-permute-start(bf16[192,384]{1,0:T(8,128)(2,1)S(1)} %pad_maximum_fusion.10.refs_0_), channel_id=1, source_target_pairs={{0,1},{1,2},{2,3},{3,0},{4,5},{5,6},{6,7},{7,4},{8,9},{9,10},{10,1... | collective-permute-start | bytes 442376 | tf_op jit(solution)/shard_map/ppermute | solution.py:664
  (38 other events, 269.8 us)
where the time goes:
time: 174 us; the launch traced here: 173 us
  Pallas kernels  84.3 us (48%)
  starting transfers between devices  34.1 us (20%)
  waiting for transfers between devices  30.8 us (18%)
  local copies, waits for them, and re-layouts  17.1 us (10%)
  other arithmetic  5.24 us (3%)
  between operations  1.85 us (1%)
    pallas_call x11, Pallas kernels, kernel_call(): pl.pallas_call(kernel, grid_spec=pltpu.PrefetchScalarGridSpec(num_scalar_...  84.3 us
    ppermute x9, starting transfers between devices, to_depth(): lax.ppermute(x, 'group', [(s, (s + k) % depth) for s in range(depth)])  13.9 us
    unnamed x66, local copies, waits for them, and re-layouts  13.5 us
    ppermute x9, starting transfers between devices, to_chip(): lax.ppermute(x, 'dp', [(s, (s // 2 + k) % chips * 2 + s % 2) for s in ran...  12 us
    ppermute x9, waiting for transfers between devices, to_chip(): lax.ppermute(x, 'dp', [(s, (s // 2 + k) % chips * 2 + s % 2) for s in ran...  10.8 us
    ppermute x9, waiting for transfers between devices, to_depth(): lax.ppermute(x, 'group', [(s, (s + k) % depth) for s in range(depth)])  8.56 us
    ppermute x4, waiting for transfers between devices, xor_depth(): return lax.ppermute(x, 'group', [(s, s ^ mask) for s in range(depth)])  5.4 us
    ppermute x4, starting transfers between devices, xor_depth(): return lax.ppermute(x, 'group', [(s, s ^ mask) for s in range(depth)])  4.33 us
  transfers between devices with their start and end apart: 32, of which 12 were waited for; matrix products, arithmetic and copies ran while one was open for 5% of the time, Pallas kernels for 25%

commit v1 on v0

--- a/solution.py
+++ b/solution.py
@@ -81,30 +81,34 @@
     tokens = x_buf.shape[1]
     copies = []
     for e in range(2):
-        own = [pltpu.make_async_copy(xq_hbm if e == 0 else xp_hbm, x_buf.at[e], sems.at[e * 5])]
+        copies.append(pltpu.make_async_copy(xq_hbm if e == 0 else xp_hbm, x_buf.at[e], sems.at[e * 5]))
         for k in range(3):
-            span = pl.ds(k * width, width)
-            own.append(pltpu.make_async_copy(w_hbm.at[e, :, span], w_buf.at[e, :, span], sems.at[e * 5 + 1 + k]))
-        own.append(pltpu.make_async_copy(wo_hbm.at[e], wo_buf.at[e], sems.at[e * 5 + 4]))
-        copies.append(own)
-    start_all(copies[0] + copies[1])
+            copies.append(pltpu.make_async_copy(w_hbm.at[e, :, pl.ds(k * width, width)], w_buf.at[e, k], sems.at[e * 5 + 1 + k]))
+        copies.append(pltpu.make_async_copy(wo_hbm.at[e], wo_buf.at[e], sems.at[e * 5 + 4]))
+    ahead = 4
+    start_all(copies[:ahead])
+
+    def arrive(k):
+        copies[k].wait()
+        if k + ahead < len(copies):
+            copies[k + ahead].start()
+
     mask = head_mask(rows, heads, width)
     pos = order_of(column([pos_ref[r] for r in range(rows)], rows), rows, depth)
     for e in range(2):
-        wait = copies[e]
         bounds = row_bounds(pack if e else 0, plen_ref if e else qlen_ref, rows, lengths[e])
         start = column([b[0] for b in bounds], rows)
         stop = column([b[1] for b in bounds], rows)
         lane = lax.broadcasted_iota(jnp.int32, (rows, tokens), 1)
         bias = bias_ref[e]
-        wait[0].wait()
+        arrive(e * 5 + 0)
         x = x_buf[e]
         x_cls = mm(jnp.where(lane == start, 1.0, 0.0).astype(BF), x)
         xc = x_cls.astype(BF)
-        wait[1].wait()
-        q = (mm(xc, w_buf[e, :, 0:width]) + bias[0:1, :]).astype(BF)
-        wait[2].wait()
-        a_low = mm(spread_heads(q, heads, mask), w_buf[e, :, width:2 * width], NT).astype(BF)
+        arrive(e * 5 + 1)
+        q = (mm(xc, w_buf[e, 0]) + bias[0:1, :]).astype(BF)
+        arrive(e * 5 + 2)
+        a_low = mm(spread_heads(q, heads, mask), w_buf[e, 1], NT).astype(BF)
         a_ref[e] = a_low
         scores = mm(a_low, x, NT) * 0.125
         lane_all = lax.broadcasted_iota(jnp.int32, scores.shape, 1)
@@ -118,10 +122,10 @@
         p_low = p.astype(BF)
         sums = jnp.sum(p_low.astype(F32), axis=1, keepdims=True)
         pooled = mm(p_low, x).astype(BF)
-        wait[3].wait()
-        full = mm(pooled, w_buf[e, :, 2 * width:3 * width]) + sums * bias[1:2, :]
+        arrive(e * 5 + 3)
+        full = mm(pooled, w_buf[e, 2]) + sums * bias[1:2, :]
         ctx = gather_heads(full, heads, rows, mask).astype(BF)
-        wait[4].wait()
+        arrive(e * 5 + 4)
         hidden = x_cls + mm(ctx, wo_buf[e]) + ob_ref[e:e + 1, :]
         mean = jnp.mean(hidden, axis=1, keepdims=True)
         centred = hidden - mean
@@ -155,6 +159,20 @@
             put(pack_other, early_other)
 
 
+def stage_kernel(ids, after_ref, win_hbm, wback_hbm, wout_hbm, xq_hbm, xp_hbm, w_hbm, win, wback, wout, x_buf, w_buf, sems):
+    c = ids[0]
+    width = wout.shape[0]
+    copies = [pltpu.make_async_copy(win_hbm.at[c], win, sems.at[0]), pltpu.make_async_copy(wback_hbm.at[c], wback, sems.at[1]),
+              pltpu.make_async_copy(wout_hbm.at[c], wout, sems.at[2]), pltpu.make_async_copy(xq_hbm, x_buf.at[0], sems.at[3]),
+              pltpu.make_async_copy(xp_hbm, x_buf.at[1], sems.at[4])]
+    for e in range(2):
+        for k in range(3):
+            copies.append(pltpu.make_async_copy(w_hbm.at[e, :, pl.ds(k * width, width)], w_buf.at[e, k], sems.at[5 + 3 * e + k]))
+    start_all(copies)
+    for copy in copies:
+        copy.wait()
+
+
 def gelu_parts(x):
     bell = jnp.exp(-0.5 * x * x)
     t = 1.0 / (1.0 + (0.3275911 * math.sqrt(0.5)) * jnp.abs(x))
@@ -195,7 +213,7 @@
     return pl.multiple_of(((chip * depth + deep) * 2 + core) * rows, rows)
 
 
-def crossed_blocks(refs, chips, depth, rows, c, j, z, part):
+def crossed_blocks(refs, chips, depth, rows, c, j, z, part, lead):
     near = depth // 2
     for at, dz in enumerate(doubling(depth, depth_masks(depth))):
         for kc in range(2):
@@ -203,7 +221,7 @@
             first = ((at % near) * 2 + kc) * rows
             for kx in range(chips):
                 place = place_of(lax.rem(j - kx + chips, chips), jnp.bitwise_xor(z, dz), core, depth, rows)
-                yield refs[at // near], first, 2 * kx * part, place
+                yield refs[at // near], first, lead + 2 * kx * part, place
 
 
 def over_rows(count, tile, work):
@@ -220,7 +238,7 @@
 def forward_kernel(chips, depth, rows, steps, tile, part, ids, *refs):
     blocks = refs[:chips]
     gain_ref, shift_ref, win_ref, inb_ref, wback_ref, backb_ref = refs[chips:chips + 6]
-    act_ref, slope_ref, vec_ref, hat2_ref, ex_ref, cut_ref, hat1_ref, total, nl = refs[chips + 6:]
+    _, act_ref, slope_ref, vec_ref, hat2_ref, ex_ref, cut_ref, hat1_ref, _, total, nl, chunk = refs[chips + 6:]
     c, j, z = ids[0], ids[1], ids[2]
     width = vec_ref.shape[1]
     step = pl.program_id(0)
@@ -241,15 +259,33 @@
         target = lax.broadcasted_iota(jnp.int32, (width, part), 1) + j * part
         cut_ref[...] = mm(low, jnp.where(source == target, 1.0, 0.0).astype(BF)).astype(BF)
 
-    columns = win_ref.shape[2]
-    pre = mm(nl[...], win_ref[0]) + inb_ref[pl.ds(c, 1), pl.ds(pl.multiple_of(step * columns, columns), columns)]
-    active, slope = gelu_parts(pre)
-    active = active.astype(BF)
-    fpart = act_ref.shape[2]
-    for s in range(columns // fpart):
-        act_ref[s] = active[:, s * fpart:(s + 1) * fpart]
-    slope_ref[...] = slope.astype(BF)
-    total[...] += mm(active, wback_ref[0])
+    columns = slope_ref.shape[1]
+    at = pl.multiple_of(step * columns, columns)
+    fpart = act_ref.shape[1]
+    bias = inb_ref[pl.ds(c, 1), pl.ds(at, columns)]
+    strips = 2
+    strip = nl.shape[0] // strips
+    spans = [slice(k * strip, (k + 1) * strip) for k in range(strips)]
+
+    def up(span):
+        return mm(nl[span, :], win_ref[:, pl.ds(at, columns)]) + bias
+
+    def down(span, pre):
+        active, slope = gelu_parts(pre)
+        active = active.astype(BF)
+        chunk[span, :] = active
+        slope_ref[span, :] = slope.astype(BF)
+        total[span, :] += mm(active, wback_ref[pl.ds(at, columns), :])
+
+    pre = up(spans[0])
+    for k in range(strips):
+        following = up(spans[k + 1]) if k + 1 < strips else None
+        down(spans[k], pre)
+        pre = following
+    for q in range(columns // fpart):
+        @pl.when(step * (columns // fpart) + q == j)
+        def keep():
+            act_ref[...] = chunk[:, q * fpart:(q + 1) * fpart]
 
     @pl.when(step == steps - 1)
     def finish():
@@ -280,15 +316,11 @@
 
 
 def loss_kernel(depth, rows, tile, ids, own_ref, other_ref, ex_ref, hat2_ref, hat1_ref, slope_ref, gain_ref,
-                wback_hbm, win_hbm, wout_hbm, second_ref, loss_ref, mine_ref, sib_ref, small_ref, qvec_ref, pvec_ref,
-                wide_loss, wback, win, wout, sems):
+                wback, win, wout, second_ref, loss_ref, mine_ref, sib_ref, small_ref, qvec_ref, pvec_ref,
+                wide_loss):
     c, j, z = ids[0], ids[1], ids[2]
     count, width = own_ref.shape
     scale = 2.0 / math.sqrt(width)
-    copies = [pltpu.make_async_copy(wback_hbm.at[c], wback, sems.at[0]),
-              pltpu.make_async_copy(win_hbm.at[c], win, sems.at[1]),
-              pltpu.make_async_copy(wout_hbm.at[c], wout, sems.at[2])]
-    start_all(copies)
     own_at = pl.multiple_of(((j * depth + z) * 2 + c) * rows, rows)
 
     def softmax_part(questions, passages, pos):
@@ -330,7 +362,9 @@
         over_rows(count, tile, work)
 
     small_ref[...] = jnp.zeros_like(small_ref)
-    loss_ref[...] = wide_loss[pl.ds(own_at, rows), :]
+    losses = wide_loss[pl.ds(own_at, rows), :]
+    diagonal = lax.broadcasted_iota(jnp.int32, losses.shape, 0) == lax.broadcasted_iota(jnp.int32, losses.shape, 1)
+    loss_ref[...] = jnp.sum(jnp.where(diagonal, losses, 0.0), axis=0, keepdims=True)[:, 0:rows]
 
     def late_norm(part):
         grad = second_ref[part, :]
@@ -345,12 +379,9 @@
 
     chip_at = pl.multiple_of((j * depth + z) * 2 * rows, 2 * rows)
     second = second_ref[pl.ds(chip_at, 2 * rows), :]
-    copies[0].wait()
     pre = (mm(second.astype(BF), wback[...], NT) * slope_ref[...].astype(F32)).astype(BF)
-    copies[1].wait()
     normed = second + mm(pre, win[...], NT)
     hidden = norm_back(normed, hat1_ref[...].astype(F32), ex_ref[pl.ds(chip_at, 2 * rows), 0:1], gain_ref[c][0:1, :])
-    copies[2].wait()
     ctx = mm(hidden.astype(BF), wout[...], NT).astype(BF).astype(F32)
     both = jnp.concatenate([hidden, ctx], axis=1)
     is_low = c == 0
@@ -365,8 +396,8 @@
     sib_ref_set(scratch[pl.ds(pl.multiple_of((1 - c) * half, half), half), :].astype(BF))
 
 
-def backward_kernel(chips, depth, rows, steps, tile, ids, after_ref, second_ref, ex_ref, hat1_ref, slope_ref, wback_ref, win_ref,
-                    gain_ref, wout_ref, small_in, gpl_ref, low_ref, hidden_ref, inb_ref, plane_ref, small_ref, acc, gfull):
+def backward_kernel(chips, depth, rows, steps, tile, ids, near_ref, second_ref, ex_ref, hat1_ref, slope_ref, wback_ref, win_ref,
+                    gain_ref, wout_ref, small_in, gpl_ref, low_ref, hidden_ref, plane_ref, small_ref, column_ref, acc, gfull):
     c, j, z = ids[0], ids[1], ids[2]
     count, width = second_ref.shape
     step = pl.program_id(0)
@@ -375,13 +406,22 @@
     def start():
         acc[...] = second_ref[...]
         low_ref[...] = second_ref[...].astype(BF)
-        small_ref[...] = small_in[...]
-
-    pre = mm(low_ref[...], wback_ref[0], NT) * slope_ref[...].astype(F32)
-    inb_ref[...] = jnp.sum(pre, axis=0, keepdims=True)
+        column_ref[...] = near_ref[:, 0:width]
+        small_ref[0:8, :] = small_in[...]
+        small_ref[8:, :] = jnp.zeros((8, width), F32)
+
+    columns = slope_ref.shape[1]
+    at = pl.multiple_of(step * columns, columns)
+    pre = mm(low_ref[...], wback_ref[pl.ds(at, columns), :], NT) * slope_ref[...].astype(F32)
+    bias = jnp.sum(pre, axis=0, keepdims=True)
     pre_low = pre.astype(BF)
     gpl_ref[...] = pre_low
-    acc[...] += mm(pre_low, win_ref[0], NT)
+    acc[...] += mm(pre_low, win_ref[:, pl.ds(at, columns)], NT)
+    for s in range(steps):
+        @pl.when(step == s)
+        def keep_bias():
+            line, lane = 8 + s * columns // width, s * columns % width
+            small_ref[line:line + 1, lane:lane + columns] = bias
 
     @pl.when(step == steps - 1)
     def finish():
@@ -398,7 +438,7 @@
             small_ref[4:5, :] += jnp.sum(hidden, axis=0, keepdims=True)
             hidden_low = hidden.astype(BF)
             hidden_ref[part, :] = hidden_low
-            ctx = mm(hidden_low, wout_ref[0], NT).astype(BF)
+            ctx = mm(hidden_low, wout_ref[...], NT).astype(BF)
             sums = mm(ex_ref[part, :].astype(BF), expand) + 1.0
             small_ref[6:7, :] += jnp.sum(sums * ctx.astype(F32), axis=0, keepdims=True)
             gfull[part, :] = ctx
@@ -434,8 +474,8 @@
 
     @pl.when(step == 0)
     def start():
-        split_halves(mm(act_ref[0], low_ref[...], TN), back_scr, c, set_own(gback_ref), set_sib(in_rows, ghalf, 0, width))
-        for ref, first, lane, place in crossed_blocks((near_ref, far_ref), chips, depth, rows, c, j, z, part):
+        split_halves(mm(act_ref[...], low_ref[...], TN), back_scr, c, set_own(gback_ref), set_sib(in_rows, ghalf, 0, width))
+        for ref, first, lane, place in crossed_blocks((near_ref, far_ref), chips, depth, rows, c, j, z, part, chips * part):
             ctx_all[pl.ds(place, rows), :] = ref[first:first + rows, lane + part:lane + 2 * part]
         split_halves(mm(ctx_all[...], hidden_ref[...], TN), out_scr, c, set_own(gout_ref), set_sib(in_rows + ghalf, half, 0, width))
 
@@ -449,37 +489,26 @@
             set_sib((s * columns // width) * half, half, s * columns % width, columns)(other)
 
 
-def attend_back_kernel(rows, heads, chips, ids, mine_ref, far_ref, xq_hbm, xp_hbm, w_hbm, bias_ref, p_ref, *refs):
+def attend_back_kernel(rows, heads, chips, ids, mine_ref, far_ref, x_buf, w_buf, bias_ref, p_ref, *refs):
     early = refs[:chips]
-    late_mine, late_other, att_ref, b_ref, first_ref, cross_ref, x_buf, w_buf, sems = refs[chips:]
+    late_mine, late_other, att_ref, b_ref, first_ref, cross_ref = refs[chips:]
     c, j = ids[0], ids[1]
     width = bias_ref.shape[2]
     part = width // chips
-    copies = []
-    for e in range(2):
-        own = [pltpu.make_async_copy(w_hbm.at[e, :, pl.ds(k * width, width)], w_buf.at[e, k], sems.at[e * 4 + k])
-               for k in (2, 1, 0)]
-        own.insert(1, pltpu.make_async_copy(xq_hbm if e == 0 else xp_hbm, x_buf.at[e], sems.at[e * 4 + 3]))
-        copies.append(own)
-    start_all(copies[0] + copies[1])
     cross_ref[...] = jnp.concatenate([b[:, heads * part:(heads + 2) * part] for b in early], axis=1)
     mask = head_mask(rows, heads, width)
     for e in range(2):
-        wait = copies[e]
         gg = jnp.where(c == e, mine_ref[...], far_ref[...])
         blocks = spread_heads(gg[:, width:], heads, mask)
         constant = jnp.sum(blocks * bias_ref[e][1:2, :], axis=1, keepdims=True)
-        wait[0].wait()
         b_low = mm(blocks.astype(BF), w_buf[e, 2], NT).astype(BF)
         b_ref[e] = b_low
         p = p_ref[e]
-        wait[1].wait()
         x = x_buf[e]
         probs = mm(b_low, x, NT) + constant
         att = (p * (probs - jnp.sum(probs * p, axis=1, keepdims=True))).astype(BF)
         att_ref[e] = att
         y_low = mm(att, x).astype(BF)
-        wait[2].wait()
         gq_low = (gather_heads(mm(y_low, w_buf[e, 1]), heads, rows, mask) * 0.125).astype(BF)
 
         def put(late_ref):
@@ -496,7 +525,6 @@
         def give():
             put(late_other)
 
-        wait[3].wait()
         first_ref[e] = gg[:, 0:width] + mm(gq_low, w_buf[e, 0], NT)
 
 
@@ -532,8 +560,9 @@
     late = refs[:chips]
     early = refs[chips:2 * chips]
     plane_ref = refs[2 * chips]
-    outs = refs[2 * chips + 1:2 * chips + 1 + depth]
-    scratch = refs[2 * chips + 1 + depth]
+    outs = refs[2 * chips + 2:2 * chips + 2 + depth]
+    column_ref, scratch = refs[-2:]
+    column_ref[...] = refs[2 * chips + 1][...]
     z = ids[2]
     width = plane_ref.shape[1]
     hp = heads * part
@@ -548,11 +577,11 @@
         outs[k][...] = scratch[:, pl.ds(at, span)].astype(BF)
 
 
-def query_kernel(chips, depth, rows, part, ids, after_ref, near_ref, far_ref, low_chips, high_chips, *refs):
+def query_kernel(chips, depth, rows, part, ids, sib_in, near_ref, far_ref, low_chips, high_chips, *refs):
     shares = refs[:depth]
-    gw_ref, keep_ref, send_ref, bias_ref, x_all, gq_all, q_scr, share_scr = refs[depth:]
+    small_in, gw_ref, keep_ref, send_ref, small_ref, sib_out, x_all, gq_all, q_scr, share_scr = refs[depth:]
     c, j, z = ids[0], ids[1], ids[2]
-    for ref, first, lane, place in crossed_blocks((near_ref, far_ref), chips, depth, rows, c, j, z, part):
+    for ref, first, lane, place in crossed_blocks((near_ref, far_ref), chips, depth, rows, c, j, z, part, chips * part):
         x_all[pl.ds(place, rows), :] = ref[first:first + rows, lane:lane + part]
     few = chips // 2
     for at_chip, dx in enumerate(doubling(chips, chip_masks(chips))):
@@ -567,7 +596,8 @@
     width = gq.shape[1]
     span = shares[0].shape[1]
     bias = jnp.sum(gq.astype(F32), axis=0, keepdims=True)
-    bias_ref[...] = jnp.broadcast_to(bias, bias_ref.shape)
+    small_ref[...] = small_in[...]
+    small_ref[7:8, :] = bias
     total = shares[0][...].astype(F32)
     for k in range(1, depth):
         total = total + shares[k][...].astype(F32)
@@ -595,13 +625,25 @@
         out_ref[1 - c, :, pl.ds(at, span)] = shards[k][half:, :].astype(F32)
 
 
-def fill_kernel(in_rows, ids, after_ref, in_hbm, back_hbm, out_hbm, sib_ref, gin_ref, gback_ref, gout_ref):
+def fill_kernel(in_rows, ids, after_ref, in_hbm, back_hbm, out_hbm, sib_ref, own_ref, other_ref, gin_ref, gback_ref, gout_ref,
+                qv_ref, outb_ref, gains_ref, shifts_ref, inb_ref, backb_ref):
+    c = ids[0]
     half, width = gout_ref.shape[1], gout_ref.shape[2]
     ghalf = gback_ref.shape[1]
     for k in range(in_rows // half):
         gin_ref[0, :, k * width:(k + 1) * width] = sib_ref[k * half:(k + 1) * half, :].astype(F32)
     gback_ref[0] = sib_ref[in_rows:in_rows + ghalf, :].astype(F32)
     gout_ref[0] = sib_ref[in_rows + ghalf:, :].astype(F32)
+    for e in range(2):
+        small = jnp.where(c == e, own_ref[...], other_ref[...])
+        gains_ref[e] = small[0:2]
+        shifts_ref[e] = small[2:4]
+        outb_ref[e:e + 1, :] = small[4:5]
+        backb_ref[e:e + 1, :] = small[5:6]
+        qv_ref[e, 0:1, :] = small[7:8]
+        qv_ref[e, 1:2, :] = small[6:7]
+        for k in range(inb_ref.shape[1] // width):
+            inb_ref[e:e + 1, k * width:(k + 1) * width] = small[8 + k:9 + k]
 
 
 def full_spec(shape):
@@ -650,7 +692,6 @@
     z = lax.axis_index("group")
     c, j = i % 2, i // 2
     ids = jnp.stack([c, j, z]).astype(jnp.int32)
-    first = c == 0
     vm = pltpu.VMEM
     dma = pltpu.SemaphoreType.DMA
 
@@ -668,6 +709,10 @@
 
     def over_plane(x):
         return [x] + [to_chip(x, k) for k in range(1, chips)]
+
+    small_enough = count <= 1024
+    kept = pl.BlockSpec(memory_space=pltpu.VMEM) if small_enough else None
+    keep_shape = (lambda shape: pltpu.VMEM(shape, BF)) if small_enough else (lambda shape: shape_of(shape, BF))
 
     xq = question_tokens.reshape(tokens, width)
     xp = passage_tokens.reshape(tokens, width)
@@ -680,56 +725,60 @@
         [shape_of((rows, width + EXTRA), BF)] * 2 + [shape_of((chips, rows, wide), BF)] * 2 + [
             shape_of((2, hr, width), BF), shape_of((2, hr, tokens), F32)],
         [None] * 6,
-        [vm((2, tokens, width), BF), vm((2, width, 3 * width), BF), vm((2, width, width), BF), dma((10,))],
-        work=(6e9, 13e6))
+        [vm((2, tokens, width), BF), vm((2, 3, width, width), BF), vm((2, width, width), BF), dma((10,))],
+        vmem=60 if count <= 1024 else 60, work=(6e9, 13e6))
 
     pair = jnp.concatenate([pack_mine, swap(pack_other)], axis=0)
-    plane = over_plane(jnp.concatenate(over_depth(pair), axis=0))
+    column_rows = jnp.concatenate(over_depth(pair), axis=0)
+    plane = over_plane(column_rows)
+    win_kept, wback_kept, wout_kept, x_kept, w_kept = kernel_call(
+        "stage", stage_kernel, ids, [column_rows, w_in, w_back, w_out, xq, xp, w_qkv], [ANY] * 7,
+        [keep_shape((width, ff)), keep_shape((ff, width)), keep_shape((width, width)), keep_shape((2, tokens, width)),
+         keep_shape((2, 3, width, width))], [kept] * 5, [dma((11,))],
+        vmem=24 if count <= 1024 else 60, work=(5e9, 10e6))
 
     fc = max(fpart, 384)
-    sub = fc // fpart
     steps = ff // fc
     tile = count if count <= 1024 else 128
     row = lambda w: full_spec((count, w))
-    act, slope, vec, hat2, ex, cut, hat1 = kernel_call(
+    act, slope, vec, hat2, ex, cut, hat1, early_other = kernel_call(
         "forward", functools.partial(forward_kernel, chips, depth, rows, steps, tile, part), ids,
-        plane + [norm_gains, norm_biases, w_in, in_bias, w_back, back_bias],
-        [None] * chips + [None, None, pl.BlockSpec((1, width, fc), lambda s, ids: (ids[0], 0, s)), None,
-                          pl.BlockSpec((1, fc, width), lambda s, ids: (ids[0], s, 0)), None],
-        [shape_of((chips, count, fpart), BF), shape_of((count, ff), BF), shape_of((count, width), BF),
-         shape_of((count, width), BF), shape_of((count, EXTRA), F32), shape_of((count, part), BF), shape_of((count, width), BF)],
-        [pl.BlockSpec((sub, count, fpart), lambda s, ids: (s, 0, 0)), pl.BlockSpec((count, fc), lambda s, ids: (0, s)),
-         None, None, None, None, None],
-        [vm((count, width), F32), vm((count, width), BF)], grid=(steps,), work=(10e9, 18e6))
+        plane + [norm_gains, norm_biases, win_kept, in_bias, wback_kept, back_bias, early_other],
+        [None] * chips + [None, None, kept, None, kept, None, ANY],
+        [shape_of((count, fpart), BF), shape_of((count, ff), BF), shape_of((count, width), BF),
+         shape_of((count, width), BF), shape_of((count, EXTRA), F32), shape_of((count, part), BF), shape_of((count, width), BF),
+         shape_of(early_other.shape, BF)],
+        [None, pl.BlockSpec((count, fc), lambda s, ids: (0, s)), None, None, None, None, None, ANY],
+        [vm((count, width), F32), vm((count, width), BF), vm((count, fc), BF)], grid=(steps,), vmem=24 if count <= 1024 else 60, work=(10e9, 18e6),
+        aliases={1 + chips + 6: 7})
 
     vec_other = swap(vec)
     hp = heads * part
 
-    nothing = vec[0:1, 0:1] * jnp.asarray(0.0, BF)
-    early_far = swap(early_other + nothing)
+    early_far = swap(early_other)
     payload = [jnp.concatenate([early_mine[k], early_far[k]], axis=0) for k in range(chips)]
     early = [payload[0]] + [to_chip(payload[k], k) for k in range(1, chips)]
 
     chip_block = lambda w: pl.BlockSpec((2 * rows, w), lambda s, ids: (ids[1] * depth + ids[2], 0))
     second, loss, gg_mine, gg_sib, small, q_vectors, p_vectors = kernel_call(
         "loss", functools.partial(loss_kernel, depth, rows, tile), ids,
-        [vec, vec_other, ex, hat2, hat1, slope, norm_gains, w_back, w_in, w_out],
-        [None, None, None, None, chip_block(width), chip_block(ff), None, ANY, ANY, ANY],
-        [shape_of((count, width), F32), shape_of((rows, EXTRA), F32), shape_of((rows, 2 * width), F32),
+        [vec, vec_other, ex, hat2, hat1, slope, norm_gains, wback_kept, win_kept, wout_kept],
+        [None, None, None, None, chip_block(width), chip_block(ff), None, kept, kept, kept],
+        [shape_of((count, width), F32), shape_of((1, rows), F32), shape_of((rows, 2 * width), F32),
          shape_of((rows, 2 * width), F32), shape_of((8, width), F32), shape_of((rows, width), BF), shape_of((rows, width), BF)],
         [None] * 7,
-        [vm((count, EXTRA), F32), vm((ff, width), BF), vm((width, ff), BF), vm((width, width), BF), dma((3,))],
-        work=(8e9, 16e6))
+        [vm((count, EXTRA), F32)],
+        vmem=24 if count <= 1024 else 60, work=(8e9, 16e6))
 
     late_mine, late_other, att, b_low, first_rows, crossed = kernel_call(
         "attend_back", functools.partial(attend_back_kernel, rows, heads, chips), ids,
-        [gg_mine, swap(gg_sib), xq, xp, w_qkv, qv_bias, probs] + early,
-        [None, None, ANY, ANY, ANY, None, None] + [None] * chips,
+        [gg_mine, swap(gg_sib), x_kept, w_kept, qv_bias, probs] + early,
+        [None, None, kept, kept, None, None] + [None] * chips,
         [shape_of((chips, rows, hp + width), BF)] * 2 + [
             shape_of((2, hr, tokens), BF), shape_of((2, hr, width), BF), shape_of((2, rows, width), F32),
             shape_of((2 * rows, 2 * width), BF)],
         [None] * 6,
-        [vm((2, tokens, width), BF), vm((2, 3, width, width), BF), dma((8,))], work=(6e9, 16e6))
+        vmem=24 if count <= 1024 else 60, work=(6e9, 16e6))
 
     late_far = swap(late_other)
     payload = [jnp.concatenate([late_mine[k], late_far[k]], axis=0) for k in range(chips)]
@@ -746,29 +795,30 @@
             x = jnp.concatenate([x, step(x, mask)], axis=0)
         return x
 
-    near = double(crossed, xor_depth, depth_masks(depth)[:-1])
+    near = double(jnp.concatenate([payload[0][:, hp:], crossed], axis=1), xor_depth, depth_masks(depth)[:-1])
     far_z = xor_depth(near, depth_masks(depth)[-1])
-    gq_column = double(payload[0][:, hp:], xor_depth, depth_masks(depth))
-    gq_low = double(gq_column, xor_chip, chip_masks(chips)[:-1])
-    gq_high = xor_chip(gq_low, chip_masks(chips)[-1])
-
-    gpl, low, hidden_low, g_inb, g_plane, small = kernel_call(
+    gpl, low, hidden_low, g_plane, small, gq_near = kernel_call(
         "backward", functools.partial(backward_kernel, chips, depth, rows, steps, tile), ids,
-        [late_far, second, ex, hat1, slope, w_back, w_in, norm_gains, w_out, small],
-        [ANY, None, None, None, pl.BlockSpec((count, fc), lambda s, ids: (0, s)),
-         pl.BlockSpec((1, fc, width), lambda s, ids: (ids[0], s, 0)),
-         pl.BlockSpec((1, width, fc), lambda s, ids: (ids[0], 0, s)), None,
-         pl.BlockSpec((1, width, width), lambda s, ids: (ids[0], 0, 0)), None],
-        [shape_of((count, ff), BF), shape_of((count, width), BF), shape_of((count, width), BF), shape_of((1, ff), F32),
-         shape_of((chips * 2 * rows, width), BF), shape_of((8, width), F32)],
-        [pl.BlockSpec((count, fc), lambda s, ids: (0, s)), None, None, pl.BlockSpec((1, fc), lambda s, ids: (0, s)), None, None],
-        [vm((count, width), F32), vm((count, width), BF)], grid=(steps,), work=(12e9, 18e6))
+        [near, second, ex, hat1, slope, wback_kept, win_kept, norm_gains, wout_kept, small],
+        [None, None, None, None, pl.BlockSpec((count, fc), lambda s, ids: (0, s)),
+         kept, kept, None, kept, None],
+        [shape_of((count, ff), BF), shape_of((count, width), BF), shape_of((count, width), BF),
+         shape_of((chips * 2 * rows, width), BF), shape_of((16, width), F32), shape_of((near.shape[0], width), BF)],
+        [pl.BlockSpec((count, fc), lambda s, ids: (0, s)), None, None, None, None, None],
+        [vm((count, width), F32), vm((count, width), BF)], grid=(steps,), vmem=36 if count <= 1024 else 60, work=(12e9, 18e6))
+
+    gq_column = jnp.concatenate([gq_near, far_z[:, 0:width]], axis=0)
 
     span = 2 * width // depth
-    shares = kernel_call(
+    *shares, gq_first = kernel_call(
         "share", functools.partial(share_kernel, heads, chips, depth, part), ids,
-        late + early + [g_plane], [None] * (2 * chips + 1),
-        [shape_of((part, span), BF)] * depth, [None] * depth, [vm((part, 2 * width), F32)], work=(1e9, 3e6))
+        late + early + [g_plane, gq_column], [None] * (2 * chips + 2),
+        [shape_of((part, span), BF)] * depth + [shape_of(gq_column.shape, BF)], [None] * (depth + 1),
+        [vm((part, 2 * width), F32)], vmem=40 if count <= 1024 else 60, work=(1e9, 3e6))
+    masks = chip_masks(chips)
+    gq_low = jnp.concatenate([gq_first, xor_chip(gq_column, masks[0])], axis=0)
+    gq_low = double(gq_low, xor_chip, masks[1:-1])
+    gq_high = xor_chip(gq_low, masks[-1])
     shares = [shares[0]] + [to_depth(shares[k], k) for k in range(1, depth)]
 
     ghalf = fpart // 2
@@ -778,20 +828,20 @@
         "weight", functools.partial(weight_kernel, chips, depth, rows, part, steps), ids,
         [shares[0], near, far_z, gpl, low, hidden_low, act, cut],
         [ANY, None, None, pl.BlockSpec((count, fc), lambda s, ids: (0, s)), None, None,
-         pl.BlockSpec((1, count, fpart), lambda s, ids: (ids[1], 0, 0)), None],
+         None, None],
         [shape_of((2, half, ff), F32), shape_of((2, ghalf, width), F32), shape_of((2, half, width), F32),
          shape_of((in_rows + ghalf + half, width), BF)],
         [pl.BlockSpec((1, half, fc), lambda s, ids: (ids[0], 0, s)), out_block(ghalf, width), out_block(half, width), None],
         [vm((count, part), BF), vm((part, fc), F32), vm((fpart, width), F32), vm((part, width), F32)],
-        grid=(steps,), vmem=28 if count <= 1024 else 60, work=(4e9, 12e6))
+        grid=(steps,), vmem=44 if count <= 1024 else 60, work=(4e9, 12e6))
+    gw_q, keep, send, small, sib = kernel_call(
+        "query", functools.partial(query_kernel, chips, depth, rows, part), ids,
+        [sib, near, far_z, gq_low, gq_high] + shares + [small], [ANY] + [None] * (depth + 5),
+        [shape_of((half, width), F32), shape_of((half, span), BF), shape_of((half, span + width), BF), shape_of((16, width), F32),
+         shape_of(sib.shape, BF)],
+        [None] * 4 + [ANY],
+        [vm((count, part), BF), vm((count, width), BF), vm((part, width), F32), vm((part, span), F32)], vmem=20 if count <= 1024 else 60, aliases={1: 4}, work=(1e9, 3e6))
     sib_far = swap(sib)
-
-    gw_q, keep, send, q_bias = kernel_call(
-        "query", functools.partial(query_kernel, chips, depth, rows, part), ids,
-        [sib, near, far_z, gq_low, gq_high] + shares, [ANY] + [None] * (depth + 4),
-        [shape_of((half, width), F32), shape_of((half, span), BF), shape_of((half, span + width), BF), shape_of((8, width), F32)],
-        [None] * 4,
-        [vm((count, part), BF), vm((count, width), BF), vm((part, width), F32), vm((part, span), F32)], vmem=20 if count <= 1024 else 60, work=(1e9, 3e6))
     far = swap(send)
     shards = over_depth(jnp.concatenate([keep, far[:, 0:span]], axis=0))
     gx = kernel_call(
@@ -802,36 +852,35 @@
         [shape_of((tokens, width), F32)] * 2, [pl.BlockSpec((256, width), lambda s, ids: (s, 0))] * 2,
         grid=(tokens // 256,), vmem=24 if count <= 1024 else 60, work=(2e9, 9e6))
 
-    gin, gback, gout = kernel_call(
-        "fill", functools.partial(fill_kernel, in_rows), ids, [gx[0], gin, gback, gout, sib_far], [ANY, ANY, ANY, ANY, None],
-        [shape_of(gin.shape, F32), shape_of(gback.shape, F32), shape_of(gout.shape, F32)],
-        [pl.BlockSpec((1,) + a.shape[1:], lambda s, ids: (1 - ids[0], 0, 0)) for a in (gin, gback, gout)],
+    gin, gback, gout, g_qv, g_outb, g_gains, g_shifts, g_inb, g_backb = kernel_call(
+        "fill", functools.partial(fill_kernel, in_rows), ids, [gx[0], gin, gback, gout, sib_far, small, swap(small)],
+        [ANY, ANY, ANY, ANY, None, None, None],
+        [shape_of(gin.shape, F32), shape_of(gback.shape, F32), shape_of(gout.shape, F32), shape_of((2, 2, width), F32),
+         shape_of((2, width), F32), shape_of((2, 2, width), F32), shape_of((2, 2, width), F32), shape_of((2, ff), F32),
+         shape_of((2, width), F32)],
+        [pl.BlockSpec((1,) + a.shape[1:], lambda s, ids: (1 - ids[0], 0, 0)) for a in (gin, gback, gout)] + [None] * 6,
         aliases={2: 0, 3: 1, 4: 2}, vmem=20 if count <= 1024 else 60, work=(1e6, 8e6))
 
     (g_qkv,) = kernel_call(
         "assemble", functools.partial(assemble_kernel, depth), ids, [gout] + shards + [gw_q, far], [ANY] + [None] * (depth + 2),
         [shape_of((2, half, 3 * width), F32)], [None], vmem=20 if count <= 1024 else 60, work=(1e6, 3e6))
 
-    n_in = ff // width
-    small_all = jnp.concatenate([small, g_inb.reshape(-1, width), q_bias[0:4]], axis=0)
-    small_far = swap(small_all)
-    small_all = jnp.stack([jnp.where(first, small_all, small_far), jnp.where(first, small_far, small_all)])
     return (
         q_vectors,
         p_vectors,
-        loss[:, 0],
+        loss.reshape(rows),
         gx[0].reshape(question_tokens.shape),
         gx[1].reshape(passage_tokens.shape),
         g_qkv,
-        jnp.stack([small_all[:, 8 + n_in], small_all[:, 6]], axis=1),
+        g_qv,
         gout,
-        small_all[:, 4],
-        small_all[:, 0:2],
-        small_all[:, 2:4],
+        g_outb,
+        g_gains,
+        g_shifts,
         gin,
-        small_all[:, 8:8 + n_in].reshape(2, ff),
+        g_inb,
         gback,
-        small_all[:, 5],
+        g_backb,
     )
 
 

time: 174 us -> 141 us (0.81)
  Pallas kernels: 84.3 us -> 73.6 us
  local copies, waits for them, and re-layouts: 17.1 us -> 6.62 us
  waiting for transfers between devices: 30.8 us -> 24.7 us
  other arithmetic: 5.24 us -> 0.79 us
    pallas_call x11 -> x12, Pallas kernels: 84.3 us -> 73.6 us  [kernel_call(): pl.pallas_call(kernel, grid_spec=pltpu.PrefetchScalarGridSpec(num_scalar_...]
    ppermute x9, waiting for transfers between devices: 10.8 us -> 2.84 us  [to_chip(): lax.ppermute(x, 'dp', [(s, (s // 2 + k) % chips * 2 + s % 2) for s in ran...]
    unnamed x66, local copies, waits for them, and re-layouts: 13.5 us -> 6.45 us
    ppermute x4 -> x2, waiting for transfers between devices: 5.4 us -> 1.01 us  [xor_depth(): return lax.ppermute(x, 'group', [(s, s ^ mask) for s in range(depth)])]
    ppermute x8, waiting for transfers between devices: 2.92 us -> 7.06 us  [swap(): return lax.ppermute(x, 'dp', [(k, k ^ 1) for k in range(n_dp)])]
    ppermute x9, waiting for transfers between devices: 8.56 us -> 10.9 us  [to_depth(): lax.ppermute(x, 'group', [(s, (s + k) % depth) for s in range(depth)])]
    slice x3 -> x1, local copies, waits for them, and re-layouts: 1.82 us -> 0.01 us  [body(): gq_column = jnp.concatenate([gq_near, far_z[:, 0:width]], axis=0)]
    ppermute x4 -> x2, starting transfers between devices: 4.33 us -> 2.74 us  [xor_depth(): return lax.ppermute(x, 'group', [(s, s ^ mask) for s in range(depth)])]
  transfers between devices with their start and end apart: 32 -> 30, of which waited for: 12 -> 12; matrix products, arithmetic and copies ran while one was open for 5% -> 1% of each run, Pallas kernels for 25% -> 30%
where the time goes in v1:
time: 141 us; the launch traced here: 140 us
  Pallas kernels  73.6 us (52%)
  starting transfers between devices  33.6 us (24%)
  waiting for transfers between devices  24.7 us (18%)
  local copies, waits for them, and re-layouts  6.62 us (5%)
    pallas_call x12, Pallas kernels, kernel_call(): pl.pallas_call(kernel, grid_spec=pltpu.PrefetchScalarGridSpec(num_scalar_...  73.6 us
    ppermute x9, starting transfers between devices, to_depth(): lax.ppermute(x, 'group', [(s, (s + k) % depth) for s in range(depth)])  15 us
    ppermute x9, starting transfers between devices, to_chip(): lax.ppermute(x, 'dp', [(s, (s // 2 + k) % chips * 2 + s % 2) for s in ran...  12 us
    ppermute x9, waiting for transfers between devices, to_depth(): lax.ppermute(x, 'group', [(s, (s + k) % depth) for s in range(depth)])  10.9 us
    ppermute x8, waiting for transfers between devices, swap(): return lax.ppermute(x, 'dp', [(k, k ^ 1) for k in range(n_dp)])  7.06 us
    unnamed x66, local copies, waits for them, and re-layouts  6.45 us
    ppermute x2, waiting for transfers between devices, xor_chip(): return lax.ppermute(x, 'dp', [(s, s ^ 2 * mask) for s in range(n_dp)])  2.86 us
    ppermute x9, waiting for transfers between devices, to_chip(): lax.ppermute(x, 'dp', [(s, (s // 2 + k) % chips * 2 + s % 2) for s in ran...  2.84 us
  transfers between devices with their start and end apart: 30, of which 12 were waited for; matrix products, arithmetic and copies ran while one was open for 1% of the time, Pallas kernels for 30%

profile of v1, /device:TPU:0, one launch (start us, length us, event | category | flops | bytes accessed | tf_op | source)
XLA Modules:
  0.0 140.5 jit_solution(654432619180043242)
XLA Ops:
  1.3 12.2 %attend.1 = (bf16[16,896]{1,0:T(8,128)(2,1)}, bf16[16,896]{1,0:T(8,128)(2,1)}, bf16[4,16,3456]{2,1,0:T(8,128)(2,1)}, bf16[4,16,3456]{2,1,0:T(8,128)(2,1)}, bf16[...) custom-call(s32[3]{0:T(128)} %pad_add_fusion.ids, s32[16]{0:T(128)} %qlen_ref.3, s32[4,4]{1,0:T(4,128)} %plen_ref.3, ...), custom_call_target="tpu_custom_call" | custom-call | flops 6000000000 | bytes 13000000 | tf_op jit(solution)/shard_map/attend/pallas_call | solution.py:664
  15.1 3.0 %collective-permute-start.1 = (bf16[32,896]{1,0:T(8,128)(2,1)S(1)}, bf16[32,896]{1,0:T(8,128)(2,1)S(1)}, u32[]{:S(2)}, u32[]{:S(2)}) collective-permute-start(bf16[32,896]{1,0:T(8,128)(2,1)S(1)} %get-tuple-element.157), channel_id=1, source_target_pairs={{0,1},{1,2},{2,3},{3,0},{4,5},{5,6},{6,7},{7,4},{8,9},{9,10},{10,1... | collective-permute-start | bytes 172040 | tf_op jit(solution)/shard_map/ppermute | solution.py:705
  18.0 2.1 %collective-permute-start.3 = (bf16[32,896]{1,0:T(8,128)(2,1)S(1)}, bf16[32,896]{1,0:T(8,128)(2,1)S(1)}, u32[]{:S(2)}, u32[]{:S(2)}) collective-permute-start(bf16[32,896]{1,0:T(8,128)(2,1)S(1)} %get-tuple-element.157), channel_id=1, source_target_pairs={{0,3},{1,0},{2,1},{3,2},{4,7},{5,4},{6,5},{7,6},{8,11},{9,8},{10,9... | collective-permute-start | bytes 172040 | tf_op jit(solution)/shard_map/ppermute | solution.py:705
  22.4 3.5 %collective-permute-done.2 = bf16[32,896]{1,0:T(8,128)(2,1)S(1)} collective-permute-done((bf16[32,896]{1,0:T(8,128)(2,1)S(1)}, bf16[32,896]{1,0:T(8,128)(2,1)S(1)}, u32[]{:S(2)}, u32[]{:S(2)}) %collective-permute-start.2) | collective-permute-done | bytes 57376 | tf_op jit(solution)/shard_map/ppermute | solution.py:705
  26.0 2.5 %collective-permute-start.6 = (bf16[128,896]{1,0:T(8,128)(2,1)S(1)}, bf16[128,896]{1,0:T(8,128)(2,1)S(1)}, u32[]{:S(2)}, u32[]{:S(2)}) collective-permute-start(bf16[128,896]{1,0:T(8,128)(2,1)S(1)} %constant_dynamic-update-slice_fusion.2.after_ref.refs_0_), channel_id=1, source_target_pairs={{0,24},{4,28},{8,0},{12,4},{16,8},{20,12},{24,16},{28,20},{1,25},{... | collective-permute-start | bytes 688136 | tf_op jit(solution)/shard_map/ppermute | solution.py:702
  31.0 6.5 %stage.1 = (bf16[768,3072]{1,0:T(8,128)(2,1)S(1)}, bf16[3072,768]{1,0:T(8,128)(2,1)S(1)}, bf16[768,768]{1,0:T(8,128)(2,1)S(1)}, bf16[2,1024,768]{2,1,0:T(8,128)(2,1)S(1)}, bf16[2,3,768,768]{3,2,1,0:T(8,128)(2,1)S(1)}) custom-call(s32[3]{0:T(128)S(1)} %copy-done.5, bf16[128,896]{1,0:T(8,128)(2,1)S(1)} %constant_dynamic-update-slice_fusion.2.after_ref.refs_0_, ...), custom_call_target="tpu_custom_call" | custom-call | flops 5000000000 | bytes 10000000 | tf_op jit(solution)/shard_map/stage/pallas_call | solution.py:664
  37.6 2.8 %collective-permute-done.5.refs_2_ = bf16[128,896]{1,0:T(8,128)(2,1)S(1)} collective-permute-done((bf16[128,896]{1,0:T(8,128)(2,1)S(1)}, bf16[128,896]{1,0:T(8,128)(2,1)S(1)}, u32[]{:S(2)}, u32[]{:S(2)}) %collective-permute-start.5) | collective-permute-done | bytes 229408 | tf_op jit(solution)/shard_map/ppermute | solution.py:702
  40.5 11.2 %forward.1 = (bf16[512,768]{1,0:T(8,128)(2,1)S(1)}, bf16[512,3072]{1,0:T(8,128)(2,1)S(1)}, bf16[512,768]{1,0:T(8,128)(2,1)S(1)}, bf16[512,768]{1,0:T(8,128)(2,1)...) custom-call(s32[3]{0:T(128)S(1)} %copy-done.5, ...), custom_call_target="tpu_custom_call", output_to_operand_aliasing={{7}: (11, {})} | custom-call | flops 10000000000 | bytes 18000000 | tf_op jit(solution)/shard_map/forward/pallas_call | solution.py:664
  54.9 2.4 %collective-permute-start.12 = (bf16[32,3456]{1,0:T(8,128)(2,1)S(1)}, bf16[32,3456]{1,0:T(8,128)(2,1)S(1)}, u32[]{:S(2)}, u32[]{:S(2)}) collective-permute-start(bf16[32,3456]{1,0:T(8,128)(2,1)S(1)} %pad_maximum_fusion.5), channel_id=1, source_target_pairs={{0,24},{4,28},{8,0},{12,4},{16,8},{20,12},{24,16},{28,20},{1,25},{... | collective-permute-start | bytes 663560 | tf_op jit(solution)/shard_map/ppermute | solution.py:702
  57.3 8.4 %loss.1 = (f32[512,768]{1,0:T(8,128)S(1)}, f32[1,16]{1,0:T(1,128)}, f32[16,1536]{1,0:T(8,128)S(1)}, f32[16,1536]{1,0:T(8,128)S(1)}, f32[8,768]{1,0:T(8,128)S(1)}...) custom-call(s32[3]{0:T(128)S(1)} %copy-done.5, bf16[512,768]{1,0:T(8,128)(2,1)S(1)} %get-tuple-element.83.own_ref, ...), custom_call_target="tpu_custom_call" | custom-call | flops 8000000000 | bytes 16000000 | tf_op jit(solution)/shard_map/loss/pallas_call | solution.py:664
  68.2 5.4 %attend_back.1 = (bf16[4,16,3072]{2,1,0:T(8,128)(2,1)S(1)}, bf16[4,16,3072]{2,1,0:T(8,128)(2,1)S(1)}, bf16[2,192,1024]{2,1,0:T(8,128)(2,1)S(1)}, bf16[2,192,768]...) custom-call(s32[3]{0:T(128)S(1)} %copy-done.5, ...), custom_call_target="tpu_custom_call" | custom-call | flops 6000000000 | bytes 16000000 | tf_op jit(solution)/shard_map/attend_back/pallas_call | solution.py:664
  77.3 3.2 %collective-permute-start.16 = (bf16[32,3072]{1,0:T(8,128)(2,1)S(1)}, bf16[32,3072]{1,0:T(8,128)(2,1)S(1)}, u32[]{:S(2)}, u32[]{:S(2)}) collective-permute-start(bf16[32,3072]{1,0:T(8,128)(2,1)S(1)} %pad_maximum_fusion.8), channel_id=1, source_target_pairs={{0,24},{4,28},{8,0},{12,4},{16,8},{20,12},{24,16},{28,20},{1,25},{... | collective-permute-start | bytes 589832 | tf_op jit(solution)/shard_map/ppermute | solution.py:702
  81.5 2.7 %collective-permute-start.18 = (bf16[64,2304]{1,0:T(8,128)(2,1)S(1)}, bf16[64,2304]{1,0:T(8,128)(2,1)S(1)}, u32[]{:S(2)}, u32[]{:S(2)}) collective-permute-start(bf16[64,2304]{1,0:T(8,128)(2,1)S(1)} %pad_maximum_fusion.near_ref), channel_id=1, source_target_pairs={{0,3},{1,2},{2,1},{3,0},{4,7},{5,6},{6,5},{7,4},{8,11},{9,10},{10,... | collective-permute-start | bytes 884744 | tf_op jit(solution)/shard_map/ppermute | solution.py:788
  84.3 11.6 %backward.1 = (bf16[512,3072]{1,0:T(8,128)(2,1)S(1)}, bf16[512,768]{1,0:T(8,128)(2,1)S(1)}, bf16[512,768]{1,0:T(8,128)(2,1)S(1)}, bf16[128,768]{1,0:T(8,128)(2,1...) custom-call(s32[3]{0:T(128)S(1)} %copy-done.5, bf16[64,2304]{1,0:T(8,128)(2,1)S(1)} %pad_maximum_fusion.near_ref, ...), custom_call_target="tpu_custom_call" | custom-call | flops 12000000000 | bytes 18000000 | tf_op jit(solution)/shard_map/backward/pallas_call | solution.py:664
  96.1 2.8 %share.1 = (bf16[192,384]{1,0:T(8,128)(2,1)S(1)}, bf16[192,384]{1,0:T(8,128)(2,1)S(1)}, bf16[192,384]{1,0:T(8,128)(2,1)S(1)}, bf16[192,384]{1,0:T(8,128)(2,1)S(1)}, bf16[128,768]{1,0:T(8,128)(2,1)S(1)}) custom-call(s32[3]{0:T(128)S(1)} %copy-done.5, bf16[32,3072]{1,0:T(8,128)(2,1)S(1)} %pad_maximum_fusion.1.refs_0_, ...), custom_call_target="tpu_custom_call" | custom-call | flops 1000000000 | bytes 3000000 | tf_op jit(solution)/shard_map/share/pallas_call | solution.py:664
  99.0 2.9 %collective-permute-done.19 = bf16[128,768]{1,0:T(8,128)(2,1)S(1)} collective-permute-done((bf16[128,768]{1,0:T(8,128)(2,1)S(1)}, bf16[128,768]{1,0:T(8,128)(2,1)S(1)}, u32[]{:S(2)}, u32[]{:S(2)}) %collective-permute-start.19) | collective-permute-done | bytes 196640 | tf_op jit(solution)/shard_map/ppermute | solution.py:791
  105.3 2.9 %collective-permute-start.23 = (bf16[192,384]{1,0:T(8,128)(2,1)S(1)}, bf16[192,384]{1,0:T(8,128)(2,1)S(1)}, u32[]{:S(2)}, u32[]{:S(2)}) collective-permute-start(bf16[192,384]{1,0:T(8,128)(2,1)S(1)} %get-tuple-element.116), channel_id=1, source_target_pairs={{0,3},{1,0},{2,1},{3,2},{4,7},{5,4},{6,5},{7,6},{8,11},{9,8},{10,9... | collective-permute-start | bytes 442376 | tf_op jit(solution)/shard_map/ppermute | solution.py:705
  108.3 5.2 %weight.1 = (f32[2,96,3072]{2,1,0:T(8,128)}, f32[2,384,768]{2,1,0:T(8,128)}, f32[2,96,768]{2,1,0:T(8,128)}, bf16[864,768]{1,0:T(8,128)(2,1)S(1)}) custom-call(s32[3]{0:T(128)S(1)} %copy-done.5, bf16[192,384]{1,0:T(8,128)(2,1)S(1)} %get-tuple-element.106.after_ref.refs_0_, bf16[64,2304]{1,0:T(8,128)(2,1)S(1)} %pad_maximum_fusion.near_ref, ...), custom_call_target="tpu_custom_call" | custom-call | flops 4000000000 | bytes 12000000 | tf_op jit(solution)/shard_map/weight/pallas_call | solution.py:664
  113.5 1.9 %collective-permute-done.22.refs_2_ = bf16[192,384]{1,0:T(8,128)(2,1)S(1)} collective-permute-done((bf16[192,384]{1,0:T(8,128)(2,1)S(1)}, bf16[192,384]{1,0:T(8,128)(2,1)S(1)}, u32[]{:S(2)}, u32[]{:S(2)}) %collective-permute-start.22) | collective-permute-done | bytes 147488 | tf_op jit(solution)/shard_map/ppermute | solution.py:705
  117.2 2.8 %collective-permute-done.24.after_ref.refs_5_ = bf16[96,1152]{1,0:T(8,128)(2,1)S(1)} collective-permute-done((bf16[96,1152]{1,0:T(8,128)(2,1)S(1)}, bf16[96,1152]{1,0:T(8,128)(2,1)S(1)}, u32[]{:S(2)}, u32[]{:S(2)}) %collective-permute-start.24) | collective-permute-done | bytes 221216 | tf_op jit(solution)/shard_map/ppermute | solution.py:699
  120.0 3.5 %collective-permute-start.29 = (bf16[192,384]{1,0:T(8,128)(2,1)S(1)}, bf16[192,384]{1,0:T(8,128)(2,1)S(1)}, u32[]{:S(2)}, u32[]{:S(2)}) collective-permute-start(bf16[192,384]{1,0:T(8,128)(2,1)S(1)} %pad_maximum_fusion.11.refs_0_), channel_id=1, source_target_pairs={{0,3},{1,0},{2,1},{3,2},{4,7},{5,4},{6,5},{7,6},{8,11},{9,8},{10,9... | collective-permute-start | bytes 442376 | tf_op jit(solution)/shard_map/ppermute | solution.py:705
  124.2 5.1 %token_grad.1 = (f32[1024,768]{1,0:T(8,128)}, f32[1024,768]{1,0:T(8,128)}) custom-call(s32[3]{0:T(128)S(1)} %copy-done.5, bf16[96,1152]{1,0:T(8,128)(2,1)S(1)} %collective-permute-done.24.after_ref.refs_5_, s32[16]{0:T(128)S(1)} %copy-done.17, s32[4,4]{1,0:T(4,128)S(1)} %copy-done.16, bf16[2,192,1024]{2,1,0:T(8,128)(2,1)S(1)} %get-tuple-element.119.att_ref, ...), custom_call_target="tpu_custom_call" | custom-call | flops 2000000000 | bytes 9000000 | tf_op jit(solution)/shard_map/token_grad/pallas_call | solution.py:664
  131.2 2.2 %fill.1 = (f32[2,96,3072]{2,1,0:T(8,128)}, f32[2,384,768]{2,1,0:T(8,128)}, f32[2,96,768]{2,1,0:T(8,128)}, f32[2,2,768]{2,1,0:T(2,128)}, f32[2,768]{1,0:T(2,128)}...) custom-call(s32[3]{0:T(128)S(1)} %copy-done.5, ...), custom_call_target="tpu_custom_call", output_to_operand_aliasing={{0}: (2, {}), {1}: (3, {}), {2}: (4, {})} | custom-call | flops 1000000 | bytes 8000000 | tf_op jit(solution)/shard_map/fill/pallas_call | solution.py:664
  133.4 4.1 %collective-permute-done.28.refs_2_ = bf16[192,384]{1,0:T(8,128)(2,1)S(1)} collective-permute-done((bf16[192,384]{1,0:T(8,128)(2,1)S(1)}, bf16[192,384]{1,0:T(8,128)(2,1)S(1)}, u32[]{:S(2)}, u32[]{:S(2)}) %collective-permute-start.28) | collective-permute-done | bytes 147488 | tf_op jit(solution)/shard_map/ppermute | solution.py:705
  (138 shorter events, 28.4 us)
Async XLA Ops:
  15.1 7.3 %collective-permute-start.1 = (bf16[32,896]{1,0:T(8,128)(2,1)S(1)}, bf16[32,896]{1,0:T(8,128)(2,1)S(1)}, u32[]{:S(2)}, u32[]{:S(2)}) collective-permute-start(bf16[32,896]{1,0:T(8,128)(2,1)S(1)} %get-tuple-element.157), channel_id=1, source_target_pairs={{0,1},{1,2},{2,3},{3,0},{4,5},{5,6},{6,7},{7,4},{8,9},{9,10},{10,1... | collective-permute-start | bytes 172040 | tf_op jit(solution)/shard_map/ppermute | solution.py:705
  18.0 7.9 %collective-permute-start.3 = (bf16[32,896]{1,0:T(8,128)(2,1)S(1)}, bf16[32,896]{1,0:T(8,128)(2,1)S(1)}, u32[]{:S(2)}, u32[]{:S(2)}) collective-permute-start(bf16[32,896]{1,0:T(8,128)(2,1)S(1)} %get-tuple-element.157), channel_id=1, source_target_pairs={{0,3},{1,0},{2,1},{3,2},{4,7},{5,4},{6,5},{7,6},{8,11},{9,8},{10,9... | collective-permute-start | bytes 172040 | tf_op jit(solution)/shard_map/ppermute | solution.py:705
  20.1 5.8 %collective-permute-start.2 = (bf16[32,896]{1,0:T(8,128)(2,1)S(1)}, bf16[32,896]{1,0:T(8,128)(2,1)S(1)}, u32[]{:S(2)}, u32[]{:S(2)}) collective-permute-start(bf16[32,896]{1,0:T(8,128)(2,1)S(1)} %get-tuple-element.157), channel_id=1, source_target_pairs={{0,2},{1,3},{2,0},{3,1},{4,6},{5,7},{6,4},{7,5},{8,10},{9,11},{10,... | collective-permute-start | bytes 172040 | tf_op jit(solution)/shard_map/ppermute | solution.py:705
  26.0 11.6 %collective-permute-start.6 = (bf16[128,896]{1,0:T(8,128)(2,1)S(1)}, bf16[128,896]{1,0:T(8,128)(2,1)S(1)}, u32[]{:S(2)}, u32[]{:S(2)}) collective-permute-start(bf16[128,896]{1,0:T(8,128)(2,1)S(1)} %constant_dynamic-update-slice_fusion.2.after_ref.refs_0_), channel_id=1, source_target_pairs={{0,24},{4,28},{8,0},{12,4},{16,8},{20,12},{24,16},{28,20},{1,25},{... | collective-permute-start | bytes 688136 | tf_op jit(solution)/shard_map/ppermute | solution.py:702
  28.5 11.9 %collective-permute-start.5 = (bf16[128,896]{1,0:T(8,128)(2,1)S(1)}, bf16[128,896]{1,0:T(8,128)(2,1)S(1)}, u32[]{:S(2)}, u32[]{:S(2)}) collective-permute-start(bf16[128,896]{1,0:T(8,128)(2,1)S(1)} %constant_dynamic-update-slice_fusion.2.after_ref.refs_0_), channel_id=1, source_target_pairs={{0,16},{4,20},{8,24},{12,28},{16,0},{20,4},{24,8},{28,12},{1,17},{... | collective-permute-start | bytes 688136 | tf_op jit(solution)/shard_map/ppermute | solution.py:702
  29.0 11.4 %collective-permute-start.4 = (bf16[128,896]{1,0:T(8,128)(2,1)S(1)}, bf16[128,896]{1,0:T(8,128)(2,1)S(1)}, u32[]{:S(2)}, u32[]{:S(2)}) collective-permute-start(bf16[128,896]{1,0:T(8,128)(2,1)S(1)} %constant_dynamic-update-slice_fusion.2.after_ref.refs_0_), channel_id=1, source_target_pairs={{0,8},{4,12},{8,16},{12,20},{16,24},{20,28},{24,0},{28,4},{1,9},{5... | collective-permute-start | bytes 688136 | tf_op jit(solution)/shard_map/ppermute | solution.py:702
  53.6 13.3 %collective-permute-start.10 = (bf16[32,3456]{1,0:T(8,128)(2,1)S(1)}, bf16[32,3456]{1,0:T(8,128)(2,1)S(1)}, u32[]{:S(2)}, u32[]{:S(2)}) collective-permute-start(bf16[32,3456]{1,0:T(8,128)(2,1)S(1)} %pad_maximum_fusion.3), channel_id=1, source_target_pairs={{0,8},{4,12},{8,16},{12,20},{16,24},{20,28},{24,0},{28,4},{1,9},{5... | collective-permute-start | bytes 663560 | tf_op jit(solution)/shard_map/ppermute | solution.py:702
  54.0 12.9 %collective-permute-start.11 = (bf16[32,3456]{1,0:T(8,128)(2,1)S(1)}, bf16[32,3456]{1,0:T(8,128)(2,1)S(1)}, u32[]{:S(2)}, u32[]{:S(2)}) collective-permute-start(bf16[32,3456]{1,0:T(8,128)(2,1)S(1)} %pad_maximum_fusion.4), channel_id=1, source_target_pairs={{0,16},{4,20},{8,24},{12,28},{16,0},{20,4},{24,8},{28,12},{1,17},{... | collective-permute-start | bytes 663560 | tf_op jit(solution)/shard_map/ppermute | solution.py:702
  54.9 12.0 %collective-permute-start.12 = (bf16[32,3456]{1,0:T(8,128)(2,1)S(1)}, bf16[32,3456]{1,0:T(8,128)(2,1)S(1)}, u32[]{:S(2)}, u32[]{:S(2)}) collective-permute-start(bf16[32,3456]{1,0:T(8,128)(2,1)S(1)} %pad_maximum_fusion.5), channel_id=1, source_target_pairs={{0,24},{4,28},{8,0},{12,4},{16,8},{20,12},{24,16},{28,20},{1,25},{... | collective-permute-start | bytes 663560 | tf_op jit(solution)/shard_map/ppermute | solution.py:702
  75.5 6.0 %collective-permute-start.17 = (bf16[32,2304]{1,0:T(8,128)(2,1)S(1)}, bf16[32,2304]{1,0:T(8,128)(2,1)S(1)}, u32[]{:S(2)}, u32[]{:S(2)}) collective-permute-start(bf16[32,2304]{1,0:T(8,128)(2,1)S(1)} %pad_maximum_fusion.10), channel_id=1, source_target_pairs={{0,1},{1,0},{2,3},{3,2},{4,5},{5,4},{6,7},{7,6},{8,9},{9,8},{10,11... | collective-permute-start | bytes 442376 | tf_op jit(solution)/shard_map/ppermute | solution.py:788
  75.6 20.5 %collective-permute-start.14 = (bf16[32,3072]{1,0:T(8,128)(2,1)S(1)}, bf16[32,3072]{1,0:T(8,128)(2,1)S(1)}, u32[]{:S(2)}, u32[]{:S(2)}) collective-permute-start(bf16[32,3072]{1,0:T(8,128)(2,1)S(1)} %pad_maximum_fusion.6), channel_id=1, source_target_pairs={{0,8},{4,12},{8,16},{12,20},{16,24},{20,28},{24,0},{28,4},{1,9},{5... | collective-permute-start | bytes 589832 | tf_op jit(solution)/shard_map/ppermute | solution.py:702
  75.8 20.3 %collective-permute-start.15 = (bf16[32,3072]{1,0:T(8,128)(2,1)S(1)}, bf16[32,3072]{1,0:T(8,128)(2,1)S(1)}, u32[]{:S(2)}, u32[]{:S(2)}) collective-permute-start(bf16[32,3072]{1,0:T(8,128)(2,1)S(1)} %pad_maximum_fusion.7), channel_id=1, source_target_pairs={{0,16},{4,20},{8,24},{12,28},{16,0},{20,4},{24,8},{28,12},{1,17},{... | collective-permute-start | bytes 589832 | tf_op jit(solution)/shard_map/ppermute | solution.py:702
  77.3 18.8 %collective-permute-start.16 = (bf16[32,3072]{1,0:T(8,128)(2,1)S(1)}, bf16[32,3072]{1,0:T(8,128)(2,1)S(1)}, u32[]{:S(2)}, u32[]{:S(2)}) collective-permute-start(bf16[32,3072]{1,0:T(8,128)(2,1)S(1)} %pad_maximum_fusion.8), channel_id=1, source_target_pairs={{0,24},{4,28},{8,0},{12,4},{16,8},{20,12},{24,16},{28,20},{1,25},{... | collective-permute-start | bytes 589832 | tf_op jit(solution)/shard_map/ppermute | solution.py:702
  81.5 14.3 %collective-permute-start.18 = (bf16[64,2304]{1,0:T(8,128)(2,1)S(1)}, bf16[64,2304]{1,0:T(8,128)(2,1)S(1)}, u32[]{:S(2)}, u32[]{:S(2)}) collective-permute-start(bf16[64,2304]{1,0:T(8,128)(2,1)S(1)} %pad_maximum_fusion.near_ref), channel_id=1, source_target_pairs={{0,3},{1,2},{2,1},{3,0},{4,7},{5,6},{6,5},{7,4},{8,11},{9,10},{10,... | collective-permute-start | bytes 884744 | tf_op jit(solution)/shard_map/ppermute | solution.py:788
  95.9 5.9 %collective-permute-start.19 = (bf16[128,768]{1,0:T(8,128)(2,1)S(1)}, bf16[128,768]{1,0:T(8,128)(2,1)S(1)}, u32[]{:S(2)}, u32[]{:S(2)}) collective-permute-start(bf16[128,768]{1,0:T(8,128)(2,1)S(1)} %pad_maximum_fusion.9.refs_9_), channel_id=1, source_target_pairs={{0,8},{4,12},{8,0},{12,4},{16,24},{20,28},{24,16},{28,20},{1,9},{5... | collective-permute-start | bytes 589832 | tf_op jit(solution)/shard_map/ppermute | solution.py:791
  101.9 13.5 %collective-permute-start.20 = (bf16[256,768]{1,0:T(8,128)(2,1)S(1)}, bf16[256,768]{1,0:T(8,128)(2,1)S(1)}, u32[]{:S(2)}, u32[]{:S(2)}) collective-permute-start(bf16[256,768]{1,0:T(8,128)(2,1)S(1)} %constant_dynamic-update-slice_fusion.7.low_chips), channel_id=1, source_target_pairs={{0,16},{4,20},{8,24},{12,28},{16,0},{20,4},{24,8},{28,12},{1,17},{... | collective-permute-start | bytes 1179656 | tf_op jit(solution)/shard_map/ppermute | solution.py:791
  103.5 10.0 %collective-permute-start.21 = (bf16[192,384]{1,0:T(8,128)(2,1)S(1)}, bf16[192,384]{1,0:T(8,128)(2,1)S(1)}, u32[]{:S(2)}, u32[]{:S(2)}) collective-permute-start(bf16[192,384]{1,0:T(8,128)(2,1)S(1)} %get-tuple-element.114), channel_id=1, source_target_pairs={{0,1},{1,2},{2,3},{3,0},{4,5},{5,6},{6,7},{7,4},{8,9},{9,10},{10,1... | collective-permute-start | bytes 442376 | tf_op jit(solution)/shard_map/ppermute | solution.py:705
  104.2 11.2 %collective-permute-start.22 = (bf16[192,384]{1,0:T(8,128)(2,1)S(1)}, bf16[192,384]{1,0:T(8,128)(2,1)S(1)}, u32[]{:S(2)}, u32[]{:S(2)}) collective-permute-start(bf16[192,384]{1,0:T(8,128)(2,1)S(1)} %get-tuple-element.115), channel_id=1, source_target_pairs={{0,2},{1,3},{2,0},{3,1},{4,6},{5,7},{6,4},{7,5},{8,10},{9,11},{10,... | collective-permute-start | bytes 442376 | tf_op jit(solution)/shard_map/ppermute | solution.py:705
  105.3 10.0 %collective-permute-start.23 = (bf16[192,384]{1,0:T(8,128)(2,1)S(1)}, bf16[192,384]{1,0:T(8,128)(2,1)S(1)}, u32[]{:S(2)}, u32[]{:S(2)}) collective-permute-start(bf16[192,384]{1,0:T(8,128)(2,1)S(1)} %get-tuple-element.116), channel_id=1, source_target_pairs={{0,3},{1,0},{2,1},{3,2},{4,7},{5,4},{6,5},{7,6},{8,11},{9,8},{10,9... | collective-permute-start | bytes 442376 | tf_op jit(solution)/shard_map/ppermute | solution.py:705
  116.5 12.8 %collective-permute-start.25 = (bf16[864,768]{1,0:T(8,128)(2,1)S(1)}, bf16[864,768]{1,0:T(8,128)(2,1)S(1)}, u32[]{:S(2)}, u32[]{:S(2)}) collective-permute-start(bf16[864,768]{1,0:T(8,128)(2,1)S(1)} %get-tuple-element.128), channel_id=1, source_target_pairs={{0,4},{4,0},{8,12},{12,8},{16,20},{20,16},{24,28},{28,24},{1,5},{5... | collective-permute-start | bytes 3981320 | tf_op jit(solution)/shard_map/ppermute | solution.py:699
  117.1 12.2 %collective-permute-start.26 = (f32[16,768]{1,0:T(8,128)S(1)}, f32[16,768]{1,0:T(8,128)S(1)}, u32[]{:S(2)}, u32[]{:S(2)}) collective-permute-start(f32[16,768]{1,0:T(8,128)S(1)} %get-tuple-element.129.own_ref), channel_id=1, source_target_pairs={{0,4},{4,0},{8,12},{12,8},{16,20},{20,16},{24,28},{28,24},{1,5},{5... | collective-permute-start | bytes 147464 | tf_op jit(solution)/shard_map/ppermute | solution.py:699
  120.0 13.4 %collective-permute-start.29 = (bf16[192,384]{1,0:T(8,128)(2,1)S(1)}, bf16[192,384]{1,0:T(8,128)(2,1)S(1)}, u32[]{:S(2)}, u32[]{:S(2)}) collective-permute-start(bf16[192,384]{1,0:T(8,128)(2,1)S(1)} %pad_maximum_fusion.11.refs_0_), channel_id=1, source_target_pairs={{0,3},{1,0},{2,1},{3,2},{4,7},{5,4},{6,5},{7,6},{8,11},{9,8},{10,9... | collective-permute-start | bytes 442376 | tf_op jit(solution)/shard_map/ppermute | solution.py:705
  123.5 14.0 %collective-permute-start.28 = (bf16[192,384]{1,0:T(8,128)(2,1)S(1)}, bf16[192,384]{1,0:T(8,128)(2,1)S(1)}, u32[]{:S(2)}, u32[]{:S(2)}) collective-permute-start(bf16[192,384]{1,0:T(8,128)(2,1)S(1)} %pad_maximum_fusion.11.refs_0_), channel_id=1, source_target_pairs={{0,2},{1,3},{2,0},{3,1},{4,6},{5,7},{6,4},{7,5},{8,10},{9,11},{10,... | collective-permute-start | bytes 442376 | tf_op jit(solution)/shard_map/ppermute | solution.py:705
  124.2 13.3 %collective-permute-start.27 = (bf16[192,384]{1,0:T(8,128)(2,1)S(1)}, bf16[192,384]{1,0:T(8,128)(2,1)S(1)}, u32[]{:S(2)}, u32[]{:S(2)}) collective-permute-start(bf16[192,384]{1,0:T(8,128)(2,1)S(1)} %pad_maximum_fusion.11.refs_0_), channel_id=1, source_target_pairs={{0,1},{1,2},{2,3},{3,0},{4,5},{5,6},{6,7},{7,4},{8,9},{9,10},{10,1... | collective-permute-start | bytes 442376 | tf_op jit(solution)/shard_map/ppermute | solution.py:705
  (37 other events, 428.9 us)

commit v2 on v1

--- a/solution.py
+++ b/solution.py
@@ -73,19 +73,24 @@
     return ((dp // 2 * depth + owner % depth) * 2 + dp % 2) * rows + positives % rows
 
 
-def attend_kernel(pack, lengths, rows, heads, chips, depth, ids, qlen_ref, plen_ref, pos_ref, xq_hbm, xp_hbm, w_hbm, wo_hbm,
+def attend_kernel(pack, lengths, rows, heads, chips, depth, qlen_ref, plen_ref, pos_ref, xq_hbm, xp_hbm, w_hbm, wo_hbm,
                   bias_ref, ob_ref, pack_mine, pack_other, early_mine, early_other, a_ref, p_ref, x_buf, w_buf, wo_buf, sems):
-    c, j = ids[0], ids[1]
+    i = lax.axis_index("dp")
+    c, j = lax.rem(i, 2), i // 2
     width = wo_buf.shape[2]
     part = width // chips
     tokens = x_buf.shape[1]
+    both = range(2)
+
+    def weight_copy(e, k):
+        return pltpu.make_async_copy(w_hbm.at[e, :, pl.ds(k * width, width)], w_buf.at[e, k], sems.at[e * 5 + 1 + k])
+
     copies = []
-    for e in range(2):
-        copies.append(pltpu.make_async_copy(xq_hbm if e == 0 else xp_hbm, x_buf.at[e], sems.at[e * 5]))
-        for k in range(3):
-            copies.append(pltpu.make_async_copy(w_hbm.at[e, :, pl.ds(k * width, width)], w_buf.at[e, k], sems.at[e * 5 + 1 + k]))
-        copies.append(pltpu.make_async_copy(wo_hbm.at[e], wo_buf.at[e], sems.at[e * 5 + 4]))
-    ahead = 4
+    for e in both:
+        copies += [pltpu.make_async_copy(xq_hbm if e == 0 else xp_hbm, x_buf.at[e], sems.at[e * 5]), weight_copy(e, 0)]
+    copies += [weight_copy(e, k) for k in (1, 2) for e in both]
+    copies += [pltpu.make_async_copy(wo_hbm.at[e], wo_buf.at[e], sems.at[e * 5 + 4]) for e in both]
+    ahead = 10
     start_all(copies[:ahead])
 
     def arrive(k):
@@ -95,68 +100,75 @@
 
     mask = head_mask(rows, heads, width)
     pos = order_of(column([pos_ref[r] for r in range(rows)], rows), rows, depth)
-    for e in range(2):
-        bounds = row_bounds(pack if e else 0, plen_ref if e else qlen_ref, rows, lengths[e])
-        start = column([b[0] for b in bounds], rows)
-        stop = column([b[1] for b in bounds], rows)
-        lane = lax.broadcasted_iota(jnp.int32, (rows, tokens), 1)
-        bias = bias_ref[e]
-        arrive(e * 5 + 0)
-        x = x_buf[e]
-        x_cls = mm(jnp.where(lane == start, 1.0, 0.0).astype(BF), x)
-        xc = x_cls.astype(BF)
-        arrive(e * 5 + 1)
-        q = (mm(xc, w_buf[e, 0]) + bias[0:1, :]).astype(BF)
-        arrive(e * 5 + 2)
-        a_low = mm(spread_heads(q, heads, mask), w_buf[e, 1], NT).astype(BF)
-        a_ref[e] = a_low
-        scores = mm(a_low, x, NT) * 0.125
-        lane_all = lax.broadcasted_iota(jnp.int32, scores.shape, 1)
-        starts = jnp.concatenate([start] * heads, axis=0)
-        stops = jnp.concatenate([stop] * heads, axis=0)
-        scores = jnp.where((lane_all >= starts) & (lane_all < stops), scores, MASKED)
-        peak = jnp.max(scores, axis=1, keepdims=True)
-        shifted = jnp.exp(scores - peak)
+    bounds = [row_bounds(pack if e else 0, plen_ref if e else qlen_ref, rows, lengths[e]) for e in both]
+    start = [column([b[0] for b in bounds[e]], rows) for e in both]
+    stop = [column([b[1] for b in bounds[e]], rows) for e in both]
+    lane = lax.broadcasted_iota(jnp.int32, (rows, tokens), 1)
+    pick = [jnp.where(lane == start[e], 1.0, 0.0).astype(BF) for e in both]
+    x_cls, xc, q = [], [], []
+    for e in both:
+        arrive(2 * e)
+        x_cls.append(mm(pick[e], x_buf[e]))
+        xc.append(x_cls[e].astype(BF))
+        arrive(2 * e + 1)
+        q.append((mm(xc[e], w_buf[e, 0]) + bias_ref[e][0:1, :]).astype(BF))
+    arrive(4)
+    arrive(5)
+    a_low = [mm(spread_heads(q[e], heads, mask), w_buf[e, 1], NT).astype(BF) for e in both]
+    scores = [mm(a_low[e], x_buf[e], NT) * 0.125 for e in both]
+    p_low, sums = [], []
+    for e in both:
+        a_ref[e] = a_low[e]
+        lane_all = lax.broadcasted_iota(jnp.int32, scores[e].shape, 1)
+        starts = jnp.concatenate([start[e]] * heads, axis=0)
+        stops = jnp.concatenate([stop[e]] * heads, axis=0)
+        allowed = jnp.where((lane_all >= starts) & (lane_all < stops), scores[e], MASKED)
+        shifted = jnp.exp(allowed - jnp.max(allowed, axis=1, keepdims=True))
         p = shifted / jnp.sum(shifted, axis=1, keepdims=True)
         p_ref[e] = p
-        p_low = p.astype(BF)
-        sums = jnp.sum(p_low.astype(F32), axis=1, keepdims=True)
-        pooled = mm(p_low, x).astype(BF)
-        arrive(e * 5 + 3)
-        full = mm(pooled, w_buf[e, 2]) + sums * bias[1:2, :]
-        ctx = gather_heads(full, heads, rows, mask).astype(BF)
-        arrive(e * 5 + 4)
-        hidden = x_cls + mm(ctx, wo_buf[e]) + ob_ref[e:e + 1, :]
-        mean = jnp.mean(hidden, axis=1, keepdims=True)
-        centred = hidden - mean
+        p_low.append(p.astype(BF))
+        sums.append(jnp.sum(p_low[e].astype(F32), axis=1, keepdims=True))
+    pooled = [mm(p_low[e], x_buf[e]).astype(BF) for e in both]
+    arrive(6)
+    arrive(7)
+    full = [mm(pooled[e], w_buf[e, 2]) + sums[e] * bias_ref[e][1:2, :] for e in both]
+    ctx = [gather_heads(full[e], heads, rows, mask).astype(BF) for e in both]
+    arrive(8)
+    arrive(9)
+    hidden = [x_cls[e] + mm(ctx[e], wo_buf[e]) + ob_ref[e:e + 1, :] for e in both]
+    lanes = lax.broadcasted_iota(jnp.int32, (rows, EXTRA), 1)
+    hat, extra = [], []
+    for e in both:
+        centred = hidden[e] - jnp.mean(hidden[e], axis=1, keepdims=True)
         rstd = lax.rsqrt(jnp.mean(centred * centred, axis=1, keepdims=True) + EPSILON)
-        hat = (centred * rstd).astype(BF)
+        hat.append((centred * rstd).astype(BF))
         rstd_high = rstd.astype(BF).astype(F32)
-        lanes = lax.broadcasted_iota(jnp.int32, (rows, EXTRA), 1)
-        extra = jnp.where(lanes == 0, rstd_high, 0.0)
-        extra = jnp.where(lanes == 1, rstd - rstd_high, extra)
-        extra = jnp.where(lanes == 2, (pos // 32).astype(F32), extra)
-        extra = jnp.where(lanes == 3, (pos % 32).astype(F32), extra)
+        more = jnp.where(lanes == 0, rstd_high, 0.0)
+        more = jnp.where(lanes == 1, rstd - rstd_high, more)
+        more = jnp.where(lanes == 2, (pos // 32).astype(F32), more)
+        more = jnp.where(lanes == 3, (pos % 32).astype(F32), more)
         for h in range(heads):
-            extra = jnp.where(lanes == 16 + h, sums[h * rows:(h + 1) * rows] - 1.0, extra)
-        extra = extra.astype(BF)
-
-        def put(pack_ref, early_ref):
-            pack_ref[:, 0:width] = hat
-            pack_ref[:, width:] = extra
-            for chip in range(chips):
-                slot = lax.rem(chip - j + chips, chips)
-                cut = slice(chip * part, (chip + 1) * part)
-                pieces = [pooled[h * rows:(h + 1) * rows, cut] for h in range(heads)] + [xc[:, cut], ctx[:, cut], q]
-                early_ref[slot] = jnp.concatenate(pieces, axis=1)
-
-        @pl.when(c == e)
-        def keep():
-            put(pack_mine, early_mine)
-
-        @pl.when(c != e)
-        def give():
-            put(pack_other, early_other)
+            more = jnp.where(lanes == 16 + h, sums[e][h * rows:(h + 1) * rows] - 1.0, more)
+        extra.append(more.astype(BF))
+
+    def put(e, pack_ref, early_ref):
+        pack_ref[:, 0:width] = hat[e]
+        pack_ref[:, width:] = extra[e]
+        for chip in range(chips):
+            slot = lax.rem(chip - j + chips, chips)
+            cut = slice(chip * part, (chip + 1) * part)
+            pieces = [pooled[e][h * rows:(h + 1) * rows, cut] for h in range(heads)] + [xc[e][:, cut], ctx[e][:, cut], q[e]]
+            early_ref[slot] = jnp.concatenate(pieces, axis=1)
+
+    @pl.when(c == 0)
+    def even():
+        put(0, pack_mine, early_mine)
+        put(1, pack_other, early_other)
+
+    @pl.when(c == 1)
+    def odd():
+        put(1, pack_mine, early_mine)
+        put(0, pack_other, early_other)
 
 
 def stage_kernel(ids, after_ref, win_hbm, wback_hbm, wout_hbm, xq_hbm, xp_hbm, w_hbm, win, wback, wout, x_buf, w_buf, sems):
@@ -497,35 +509,39 @@
     part = width // chips
     cross_ref[...] = jnp.concatenate([b[:, heads * part:(heads + 2) * part] for b in early], axis=1)
     mask = head_mask(rows, heads, width)
-    for e in range(2):
-        gg = jnp.where(c == e, mine_ref[...], far_ref[...])
-        blocks = spread_heads(gg[:, width:], heads, mask)
-        constant = jnp.sum(blocks * bias_ref[e][1:2, :], axis=1, keepdims=True)
-        b_low = mm(blocks.astype(BF), w_buf[e, 2], NT).astype(BF)
-        b_ref[e] = b_low
+    both = range(2)
+    gg = [jnp.where(c == e, mine_ref[...], far_ref[...]) for e in both]
+    blocks = [spread_heads(gg[e][:, width:], heads, mask) for e in both]
+    constant = [jnp.sum(blocks[e] * bias_ref[e][1:2, :], axis=1, keepdims=True) for e in both]
+    b_low = [mm(blocks[e].astype(BF), w_buf[e, 2], NT).astype(BF) for e in both]
+    probs = [mm(b_low[e], x_buf[e], NT) + constant[e] for e in both]
+    att = []
+    for e in both:
+        b_ref[e] = b_low[e]
         p = p_ref[e]
-        x = x_buf[e]
-        probs = mm(b_low, x, NT) + constant
-        att = (p * (probs - jnp.sum(probs * p, axis=1, keepdims=True))).astype(BF)
-        att_ref[e] = att
-        y_low = mm(att, x).astype(BF)
-        gq_low = (gather_heads(mm(y_low, w_buf[e, 1]), heads, rows, mask) * 0.125).astype(BF)
-
-        def put(late_ref):
-            for chip in range(chips):
-                slot = lax.rem(chip - j + chips, chips)
-                cut = slice(chip * part, (chip + 1) * part)
-                late_ref[slot] = jnp.concatenate([y_low[h * rows:(h + 1) * rows, cut] for h in range(heads)] + [gq_low], axis=1)
-
-        @pl.when(c == e)
-        def keep():
-            put(late_mine)
-
-        @pl.when(c != e)
-        def give():
-            put(late_other)
-
-        first_ref[e] = gg[:, 0:width] + mm(gq_low, w_buf[e, 0], NT)
+        att.append((p * (probs[e] - jnp.sum(probs[e] * p, axis=1, keepdims=True))).astype(BF))
+        att_ref[e] = att[e]
+    y_low = [mm(att[e], x_buf[e]).astype(BF) for e in both]
+    gq_low = [(gather_heads(mm(y_low[e], w_buf[e, 1]), heads, rows, mask) * 0.125).astype(BF) for e in both]
+    for e in both:
+        first_ref[e] = gg[e][:, 0:width] + mm(gq_low[e], w_buf[e, 0], NT)
+
+    def put(e, late_ref):
+        for chip in range(chips):
+            slot = lax.rem(chip - j + chips, chips)
+            cut = slice(chip * part, (chip + 1) * part)
+            pieces = [y_low[e][h * rows:(h + 1) * rows, cut] for h in range(heads)] + [gq_low[e]]
+            late_ref[slot] = jnp.concatenate(pieces, axis=1)
+
+    @pl.when(c == 0)
+    def even():
+        put(0, late_mine)
+        put(1, late_other)
+
+    @pl.when(c == 1)
+    def odd():
+        put(1, late_mine)
+        put(0, late_other)
 
 
 def token_grad_kernel(pack, lengths, rows, heads, ids, after_ref, qlen_ref, plen_ref, att_ref, p_ref, a_ref, b_ref, first_ref,
@@ -719,9 +735,9 @@
 
     wide = (heads + 2) * part + width
     pack_mine, pack_other, early_mine, early_other, a_low, probs = kernel_call(
-        "attend", functools.partial(attend_kernel, pack, lengths, rows, heads, chips, depth), ids,
-        [question_lengths, passage_lengths, positives, xq, xp, w_qkv, w_out, qv_bias, out_bias],
-        [SMEM, SMEM, SMEM, ANY, ANY, ANY, ANY, None, None],
+        "attend", functools.partial(attend_kernel, pack, lengths, rows, heads, chips, depth), question_lengths,
+        [passage_lengths, positives, xq, xp, w_qkv, w_out, qv_bias, out_bias],
+        [SMEM, SMEM, ANY, ANY, ANY, ANY, None, None],
         [shape_of((rows, width + EXTRA), BF)] * 2 + [shape_of((chips, rows, wide), BF)] * 2 + [
             shape_of((2, hr, width), BF), shape_of((2, hr, tokens), F32)],
         [None] * 6,
@@ -805,7 +821,7 @@
         [shape_of((count, ff), BF), shape_of((count, width), BF), shape_of((count, width), BF),
          shape_of((chips * 2 * rows, width), BF), shape_of((16, width), F32), shape_of((near.shape[0], width), BF)],
         [pl.BlockSpec((count, fc), lambda s, ids: (0, s)), None, None, None, None, None],
-        [vm((count, width), F32), vm((count, width), BF)], grid=(steps,), vmem=36 if count <= 1024 else 60, work=(12e9, 18e6))
+        [vm((count, width), F32), vm((count, width), BF)], grid=(steps,), vmem=30 if count <= 1024 else 60, work=(12e9, 18e6))
 
     gq_column = jnp.concatenate([gq_near, far_z[:, 0:width]], axis=0)
 
@@ -814,7 +830,7 @@
         "share", functools.partial(share_kernel, heads, chips, depth, part), ids,
         late + early + [g_plane, gq_column], [None] * (2 * chips + 2),
         [shape_of((part, span), BF)] * depth + [shape_of(gq_column.shape, BF)], [None] * (depth + 1),
-        [vm((part, 2 * width), F32)], vmem=40 if count <= 1024 else 60, work=(1e9, 3e6))
+        [vm((part, 2 * width), F32)], vmem=28 if count <= 1024 else 60, work=(1e9, 3e6))
     masks = chip_masks(chips)
     gq_low = jnp.concatenate([gq_first, xor_chip(gq_column, masks[0])], axis=0)
     gq_low = double(gq_low, xor_chip, masks[1:-1])
@@ -833,7 +849,7 @@
          shape_of((in_rows + ghalf + half, width), BF)],
         [pl.BlockSpec((1, half, fc), lambda s, ids: (ids[0], 0, s)), out_block(ghalf, width), out_block(half, width), None],
         [vm((count, part), BF), vm((part, fc), F32), vm((fpart, width), F32), vm((part, width), F32)],
-        grid=(steps,), vmem=44 if count <= 1024 else 60, work=(4e9, 12e6))
+        grid=(steps,), vmem=28 if count <= 1024 else 60, work=(4e9, 12e6))
     gw_q, keep, send, small, sib = kernel_call(
         "query", functools.partial(query_kernel, chips, depth, rows, part), ids,
         [sib, near, far_z, gq_low, gq_high] + shares + [small], [ANY] + [None] * (depth + 5),

time: 141 us -> 136 us (0.965)
  Pallas kernels: 73.6 us -> 68.7 us
  waiting for transfers between devices: 24.7 us -> 20.6 us
  starting transfers between devices: 33.6 us -> 37.3 us
    pallas_call x12, Pallas kernels: 73.6 us -> 68.7 us  [kernel_call(): pl.pallas_call(kernel, grid_spec=pltpu.PrefetchScalarGridSpec(num_scalar_...]
    ppermute x9, starting transfers between devices: 15 us -> 18.6 us  [to_depth(): lax.ppermute(x, 'group', [(s, (s + k) % depth) for s in range(depth)])]
    ppermute x9, waiting for transfers between devices: 10.9 us -> 8.32 us  [to_depth(): lax.ppermute(x, 'group', [(s, (s + k) % depth) for s in range(depth)])]
    ppermute x9, waiting for transfers between devices: 2.84 us -> 1.32 us  [to_chip(): lax.ppermute(x, 'dp', [(s, (s // 2 + k) % chips * 2 + s % 2) for s in ran...]
    unnamed x66 -> x70, local copies, waits for them, and re-layouts: 6.45 us -> 7.84 us
  transfers between devices with their start and end apart: 30 -> 30, of which waited for: 12 -> 12; matrix products, arithmetic and copies ran while one was open for 1% -> 1% of each run, Pallas kernels for 30% -> 29%
where the time goes in v2:
time: 136 us
  Pallas kernels  68.7 us (51%)
  starting transfers between devices  37.3 us (27%)
  waiting for transfers between devices  20.6 us (15%)
  local copies, waits for them, and re-layouts  8.01 us (6%)
    pallas_call x12, Pallas kernels, kernel_call(): pl.pallas_call(kernel, grid_spec=pltpu.PrefetchScalarGridSpec(num_scalar_...  68.7 us
    ppermute x9, starting transfers between devices, to_depth(): lax.ppermute(x, 'group', [(s, (s + k) % depth) for s in range(depth)])  18.6 us
    ppermute x9, starting transfers between devices, to_chip(): lax.ppermute(x, 'dp', [(s, (s // 2 + k) % chips * 2 + s % 2) for s in ran...  12 us
    ppermute x9, waiting for transfers between devices, to_depth(): lax.ppermute(x, 'group', [(s, (s + k) % depth) for s in range(depth)])  8.32 us
    unnamed x70, local copies, waits for them, and re-layouts  7.84 us
    ppermute x8, waiting for transfers between devices, swap(): return lax.ppermute(x, 'dp', [(k, k ^ 1) for k in range(n_dp)])  7.07 us
    ppermute x2, starting transfers between devices, xor_depth(): return lax.ppermute(x, 'group', [(s, s ^ mask) for s in range(depth)])  2.89 us
    ppermute x2, waiting for transfers between devices, xor_chip(): return lax.ppermute(x, 'dp', [(s, s ^ 2 * mask) for s in range(n_dp)])  2.87 us
  transfers between devices with their start and end apart: 30, of which 12 were waited for; matrix products, arithmetic and copies ran while one was open for 1% of the time, Pallas kernels for 29%

profile of v2, /device:TPU:0, one launch (start us, length us, event | category | flops | bytes accessed | tf_op | source)
XLA Modules:
  0.0 136.1 jit_solution(15875178349630241680)
XLA Ops:
  0.7 10.7 %attend.1 = (bf16[16,896]{1,0:T(8,128)(2,1)}, bf16[16,896]{1,0:T(8,128)(2,1)}, bf16[4,16,3456]{2,1,0:T(8,128)(2,1)}, bf16[4,16,3456]{2,1,0:T(8,128)(2,1)}, bf16[...) custom-call(s32[16]{0:T(128)} %qlen_ref.3, s32[4,4]{1,0:T(4,128)} %plen_ref.3, s32[16]{0:T(128)} %pos_ref.1, ...), custom_call_target="tpu_custom_call" | custom-call | flops 6000000000 | bytes 13000000 | tf_op jit(solution)/shard_map/attend/pallas_call | solution.py:680
  13.0 3.0 %collective-permute-start.1 = (bf16[32,896]{1,0:T(8,128)(2,1)S(1)}, bf16[32,896]{1,0:T(8,128)(2,1)S(1)}, u32[]{:S(2)}, u32[]{:S(2)}) collective-permute-start(bf16[32,896]{1,0:T(8,128)(2,1)S(1)} %get-tuple-element.157), channel_id=1, source_target_pairs={{0,1},{1,2},{2,3},{3,0},{4,5},{5,6},{6,7},{7,4},{8,9},{9,10},{10,1... | collective-permute-start | bytes 172040 | tf_op jit(solution)/shard_map/ppermute | solution.py:721
  16.0 2.1 %collective-permute-start.3 = (bf16[32,896]{1,0:T(8,128)(2,1)S(1)}, bf16[32,896]{1,0:T(8,128)(2,1)S(1)}, u32[]{:S(2)}, u32[]{:S(2)}) collective-permute-start(bf16[32,896]{1,0:T(8,128)(2,1)S(1)} %get-tuple-element.157), channel_id=1, source_target_pairs={{0,3},{1,0},{2,1},{3,2},{4,7},{5,4},{6,5},{7,6},{8,11},{9,8},{10,9... | collective-permute-start | bytes 172040 | tf_op jit(solution)/shard_map/ppermute | solution.py:721
  20.3 3.5 %collective-permute-done.2 = bf16[32,896]{1,0:T(8,128)(2,1)S(1)} collective-permute-done((bf16[32,896]{1,0:T(8,128)(2,1)S(1)}, bf16[32,896]{1,0:T(8,128)(2,1)S(1)}, u32[]{:S(2)}, u32[]{:S(2)}) %collective-permute-start.2) | collective-permute-done | bytes 57376 | tf_op jit(solution)/shard_map/ppermute | solution.py:721
  23.9 2.5 %collective-permute-start.6 = (bf16[128,896]{1,0:T(8,128)(2,1)S(1)}, bf16[128,896]{1,0:T(8,128)(2,1)S(1)}, u32[]{:S(2)}, u32[]{:S(2)}) collective-permute-start(bf16[128,896]{1,0:T(8,128)(2,1)S(1)} %constant_dynamic-update-slice_fusion.2.after_ref.refs_0_), channel_id=1, source_target_pairs={{0,24},{4,28},{8,0},{12,4},{16,8},{20,12},{24,16},{28,20},{1,25},{... | collective-permute-start | bytes 688136 | tf_op jit(solution)/shard_map/ppermute | solution.py:718
  30.3 6.5 %stage.1 = (bf16[768,3072]{1,0:T(8,128)(2,1)S(1)}, bf16[3072,768]{1,0:T(8,128)(2,1)S(1)}, bf16[768,768]{1,0:T(8,128)(2,1)S(1)}, bf16[2,1024,768]{2,1,0:T(8,128)(2,1)S(1)}, bf16[2,3,768,768]{3,2,1,0:T(8,128)(2,1)S(1)}) custom-call(s32[3]{0:T(128)S(1)} %pad_add_fusion.ids, bf16[128,896]{1,0:T(8,128)(2,1)S(1)} %constant_dynamic-update-slice_fusion.2.after_ref.refs_0_, ...), custom_call_target="tpu_custom_call" | custom-call | flops 5000000000 | bytes 10000000 | tf_op jit(solution)/shard_map/stage/pallas_call | solution.py:680
  38.3 11.0 %forward.1 = (bf16[512,768]{1,0:T(8,128)(2,1)S(1)}, bf16[512,3072]{1,0:T(8,128)(2,1)S(1)}, bf16[512,768]{1,0:T(8,128)(2,1)S(1)}, bf16[512,768]{1,0:T(8,128)(2,1)...) custom-call(s32[3]{0:T(128)S(1)} %pad_add_fusion.ids, ...), custom_call_target="tpu_custom_call", output_to_operand_aliasing={{7}: (11, {})} | custom-call | flops 10000000000 | bytes 18000000 | tf_op jit(solution)/shard_map/forward/pallas_call | solution.py:680
  54.9 8.4 %loss.1 = (f32[512,768]{1,0:T(8,128)S(1)}, f32[1,16]{1,0:T(1,128)}, f32[16,1536]{1,0:T(8,128)S(1)}, f32[16,1536]{1,0:T(8,128)S(1)}, f32[8,768]{1,0:T(8,128)S(1)}...) custom-call(s32[3]{0:T(128)S(1)} %pad_add_fusion.ids, bf16[512,768]{1,0:T(8,128)(2,1)S(1)} %get-tuple-element.83.own_ref, ...), custom_call_target="tpu_custom_call" | custom-call | flops 8000000000 | bytes 16000000 | tf_op jit(solution)/shard_map/loss/pallas_call | solution.py:680
  65.8 4.6 %attend_back.1 = (bf16[4,16,3072]{2,1,0:T(8,128)(2,1)S(1)}, bf16[4,16,3072]{2,1,0:T(8,128)(2,1)S(1)}, bf16[2,192,1024]{2,1,0:T(8,128)(2,1)S(1)}, bf16[2,192,768]...) custom-call(s32[3]{0:T(128)S(1)} %pad_add_fusion.ids, ...), custom_call_target="tpu_custom_call" | custom-call | flops 6000000000 | bytes 16000000 | tf_op jit(solution)/shard_map/attend_back/pallas_call | solution.py:680
  74.3 3.0 %collective-permute-start.16 = (bf16[32,3072]{1,0:T(8,128)(2,1)S(1)}, bf16[32,3072]{1,0:T(8,128)(2,1)S(1)}, u32[]{:S(2)}, u32[]{:S(2)}) collective-permute-start(bf16[32,3072]{1,0:T(8,128)(2,1)S(1)} %pad_maximum_fusion.8), channel_id=1, source_target_pairs={{0,24},{4,28},{8,0},{12,4},{16,8},{20,12},{24,16},{28,20},{1,25},{... | collective-permute-start | bytes 589832 | tf_op jit(solution)/shard_map/ppermute | solution.py:718
  78.3 2.8 %collective-permute-start.18 = (bf16[64,2304]{1,0:T(8,128)(2,1)S(1)}, bf16[64,2304]{1,0:T(8,128)(2,1)S(1)}, u32[]{:S(2)}, u32[]{:S(2)}) collective-permute-start(bf16[64,2304]{1,0:T(8,128)(2,1)S(1)} %pad_maximum_fusion.near_ref), channel_id=1, source_target_pairs={{0,3},{1,2},{2,1},{3,0},{4,7},{5,6},{6,5},{7,4},{8,11},{9,10},{10,... | collective-permute-start | bytes 884744 | tf_op jit(solution)/shard_map/ppermute | solution.py:804
  81.2 9.3 %backward.1 = (bf16[512,3072]{1,0:T(8,128)(2,1)S(1)}, bf16[512,768]{1,0:T(8,128)(2,1)S(1)}, bf16[512,768]{1,0:T(8,128)(2,1)S(1)}, bf16[128,768]{1,0:T(8,128)(2,1...) custom-call(s32[3]{0:T(128)S(1)} %pad_add_fusion.ids, bf16[64,2304]{1,0:T(8,128)(2,1)S(1)} %pad_maximum_fusion.near_ref, ...), custom_call_target="tpu_custom_call" | custom-call | flops 12000000000 | bytes 18000000 | tf_op jit(solution)/shard_map/backward/pallas_call | solution.py:680
  90.7 2.8 %share.1 = (bf16[192,384]{1,0:T(8,128)(2,1)S(1)}, bf16[192,384]{1,0:T(8,128)(2,1)S(1)}, bf16[192,384]{1,0:T(8,128)(2,1)S(1)}, bf16[192,384]{1,0:T(8,128)(2,1)S(1)}, bf16[128,768]{1,0:T(8,128)(2,1)S(1)}) custom-call(s32[3]{0:T(128)S(1)} %pad_add_fusion.ids, bf16[32,3072]{1,0:T(8,128)(2,1)S(1)} %pad_maximum_fusion.1.refs_0_, ...), custom_call_target="tpu_custom_call" | custom-call | flops 1000000000 | bytes 3000000 | tf_op jit(solution)/shard_map/share/pallas_call | solution.py:680
  93.6 2.9 %collective-permute-done.19 = bf16[128,768]{1,0:T(8,128)(2,1)S(1)} collective-permute-done((bf16[128,768]{1,0:T(8,128)(2,1)S(1)}, bf16[128,768]{1,0:T(8,128)(2,1)S(1)}, u32[]{:S(2)}, u32[]{:S(2)}) %collective-permute-start.19) | collective-permute-done | bytes 196640 | tf_op jit(solution)/shard_map/ppermute | solution.py:807
  98.0 3.0 %collective-permute-start.21 = (bf16[192,384]{1,0:T(8,128)(2,1)S(1)}, bf16[192,384]{1,0:T(8,128)(2,1)S(1)}, u32[]{:S(2)}, u32[]{:S(2)}) collective-permute-start(bf16[192,384]{1,0:T(8,128)(2,1)S(1)} %get-tuple-element.114), channel_id=1, source_target_pairs={{0,1},{1,2},{2,3},{3,0},{4,5},{5,6},{6,7},{7,4},{8,9},{9,10},{10,1... | collective-permute-start | bytes 442376 | tf_op jit(solution)/shard_map/ppermute | solution.py:721
  102.2 2.9 %collective-permute-start.23 = (bf16[192,384]{1,0:T(8,128)(2,1)S(1)}, bf16[192,384]{1,0:T(8,128)(2,1)S(1)}, u32[]{:S(2)}, u32[]{:S(2)}) collective-permute-start(bf16[192,384]{1,0:T(8,128)(2,1)S(1)} %get-tuple-element.116), channel_id=1, source_target_pairs={{0,3},{1,0},{2,1},{3,2},{4,7},{5,4},{6,5},{7,6},{8,11},{9,8},{10,9... | collective-permute-start | bytes 442376 | tf_op jit(solution)/shard_map/ppermute | solution.py:721
  105.1 5.2 %weight.1 = (f32[2,96,3072]{2,1,0:T(8,128)}, f32[2,384,768]{2,1,0:T(8,128)}, f32[2,96,768]{2,1,0:T(8,128)}, bf16[864,768]{1,0:T(8,128)(2,1)S(1)}) custom-call(s32[3]{0:T(128)S(1)} %pad_add_fusion.ids, bf16[192,384]{1,0:T(8,128)(2,1)S(1)} %get-tuple-element.106.after_ref.refs_0_, bf16[64,2304]{1,0:T(8,128)(2,1)S(1)} %pad_maximum_fusion.near_ref, ...), custom_call_target="tpu_custom_call" | custom-call | flops 4000000000 | bytes 12000000 | tf_op jit(solution)/shard_map/weight/pallas_call | solution.py:680
  112.6 2.8 %collective-permute-done.24.after_ref.refs_5_ = bf16[96,1152]{1,0:T(8,128)(2,1)S(1)} collective-permute-done((bf16[96,1152]{1,0:T(8,128)(2,1)S(1)}, bf16[96,1152]{1,0:T(8,128)(2,1)S(1)}, u32[]{:S(2)}, u32[]{:S(2)}) %collective-permute-start.24) | collective-permute-done | bytes 221216 | tf_op jit(solution)/shard_map/ppermute | solution.py:715
  115.5 4.9 %collective-permute-start.29 = (bf16[192,384]{1,0:T(8,128)(2,1)S(1)}, bf16[192,384]{1,0:T(8,128)(2,1)S(1)}, u32[]{:S(2)}, u32[]{:S(2)}) collective-permute-start(bf16[192,384]{1,0:T(8,128)(2,1)S(1)} %pad_maximum_fusion.11.refs_0_), channel_id=1, source_target_pairs={{0,3},{1,0},{2,1},{3,2},{4,7},{5,4},{6,5},{7,6},{8,11},{9,8},{10,9... | collective-permute-start | bytes 442376 | tf_op jit(solution)/shard_map/ppermute | solution.py:721
  121.0 5.1 %token_grad.1 = (f32[1024,768]{1,0:T(8,128)}, f32[1024,768]{1,0:T(8,128)}) custom-call(s32[3]{0:T(128)S(1)} %pad_add_fusion.ids, bf16[96,1152]{1,0:T(8,128)(2,1)S(1)} %collective-permute-done.24.after_ref.refs_5_, s32[16]{0:T(128)S(1)} %copy-done.16, s32[4,4]{1,0:T(4,128)S(1)} %copy-done.15, bf16[2,192,1024]{2,1,0:T(8,128)(2,1)S(1)} %get-tuple-element.119.att_ref, ...), custom_call_target="tpu_custom_call" | custom-call | flops 2000000000 | bytes 9000000 | tf_op jit(solution)/shard_map/token_grad/pallas_call | solution.py:680
  126.1 1.9 %copy-done = f32[1024,768]{1,0:T(8,128)S(1)} copy-done((f32[1024,768]{1,0:T(8,128)S(1)}, f32[1024,768]{1,0:T(8,128)}, u32[]{:S(2)}) %copy-start) | copy-done | bytes 3145752
  128.0 2.2 %fill.1 = (f32[2,96,3072]{2,1,0:T(8,128)}, f32[2,384,768]{2,1,0:T(8,128)}, f32[2,96,768]{2,1,0:T(8,128)}, f32[2,2,768]{2,1,0:T(2,128)}, f32[2,768]{1,0:T(2,128)}...) custom-call(s32[3]{0:T(128)S(1)} %pad_add_fusion.ids, ...), custom_call_target="tpu_custom_call", output_to_operand_aliasing={{0}: (2, {}), {1}: (3, {}), {2}: (4, {})} | custom-call | flops 1000000 | bytes 8000000 | tf_op jit(solution)/shard_map/fill/pallas_call | solution.py:680
  130.1 3.0 %collective-permute-done.28.refs_2_ = bf16[192,384]{1,0:T(8,128)(2,1)S(1)} collective-permute-done((bf16[192,384]{1,0:T(8,128)(2,1)S(1)}, bf16[192,384]{1,0:T(8,128)(2,1)S(1)}, u32[]{:S(2)}, u32[]{:S(2)}) %collective-permute-start.28) | collective-permute-done | bytes 147488 | tf_op jit(solution)/shard_map/ppermute | solution.py:721
  134.2 1.9 %assemble.1 = f32[2,96,2304]{2,1,0:T(8,128)} custom-call(s32[3]{0:T(128)S(1)} %pad_add_fusion.ids, f32[2,96,768]{2,1,0:T(8,128)S(1)} %copy-done.2, bf16[192,384]{1,0:T(8,128)(2,1)S(1)} %pad_maximum_fusion.11.refs_0_, bf16[192,384]{1,0:T(8,128)(2,1)S(1)} %collective-permute-done.27.refs_1_, bf16[192,384]{1,0:T(8,128)(2,1)S(1)} %collective-permute-done.28.refs_2_, ...), custom_call_target="tpu_custom_call" | custom-call | flops 1000000 | bytes 3000000 | tf_op jit(solution)/shard_map/assemble/pallas_call | solution.py:680
  (143 shorter events, 29.1 us)
Async XLA Ops:
  13.0 7.3 %collective-permute-start.1 = (bf16[32,896]{1,0:T(8,128)(2,1)S(1)}, bf16[32,896]{1,0:T(8,128)(2,1)S(1)}, u32[]{:S(2)}, u32[]{:S(2)}) collective-permute-start(bf16[32,896]{1,0:T(8,128)(2,1)S(1)} %get-tuple-element.157), channel_id=1, source_target_pairs={{0,1},{1,2},{2,3},{3,0},{4,5},{5,6},{6,7},{7,4},{8,9},{9,10},{10,1... | collective-permute-start | bytes 172040 | tf_op jit(solution)/shard_map/ppermute | solution.py:721
  16.0 7.9 %collective-permute-start.3 = (bf16[32,896]{1,0:T(8,128)(2,1)S(1)}, bf16[32,896]{1,0:T(8,128)(2,1)S(1)}, u32[]{:S(2)}, u32[]{:S(2)}) collective-permute-start(bf16[32,896]{1,0:T(8,128)(2,1)S(1)} %get-tuple-element.157), channel_id=1, source_target_pairs={{0,3},{1,0},{2,1},{3,2},{4,7},{5,4},{6,5},{7,6},{8,11},{9,8},{10,9... | collective-permute-start | bytes 172040 | tf_op jit(solution)/shard_map/ppermute | solution.py:721
  18.0 5.8 %collective-permute-start.2 = (bf16[32,896]{1,0:T(8,128)(2,1)S(1)}, bf16[32,896]{1,0:T(8,128)(2,1)S(1)}, u32[]{:S(2)}, u32[]{:S(2)}) collective-permute-start(bf16[32,896]{1,0:T(8,128)(2,1)S(1)} %get-tuple-element.157), channel_id=1, source_target_pairs={{0,2},{1,3},{2,0},{3,1},{4,6},{5,7},{6,4},{7,5},{8,10},{9,11},{10,... | collective-permute-start | bytes 172040 | tf_op jit(solution)/shard_map/ppermute | solution.py:721
  23.9 13.0 %collective-permute-start.6 = (bf16[128,896]{1,0:T(8,128)(2,1)S(1)}, bf16[128,896]{1,0:T(8,128)(2,1)S(1)}, u32[]{:S(2)}, u32[]{:S(2)}) collective-permute-start(bf16[128,896]{1,0:T(8,128)(2,1)S(1)} %constant_dynamic-update-slice_fusion.2.after_ref.refs_0_), channel_id=1, source_target_pairs={{0,24},{4,28},{8,0},{12,4},{16,8},{20,12},{24,16},{28,20},{1,25},{... | collective-permute-start | bytes 688136 | tf_op jit(solution)/shard_map/ppermute | solution.py:718
  26.4 11.8 %collective-permute-start.5 = (bf16[128,896]{1,0:T(8,128)(2,1)S(1)}, bf16[128,896]{1,0:T(8,128)(2,1)S(1)}, u32[]{:S(2)}, u32[]{:S(2)}) collective-permute-start(bf16[128,896]{1,0:T(8,128)(2,1)S(1)} %constant_dynamic-update-slice_fusion.2.after_ref.refs_0_), channel_id=1, source_target_pairs={{0,16},{4,20},{8,24},{12,28},{16,0},{20,4},{24,8},{28,12},{1,17},{... | collective-permute-start | bytes 688136 | tf_op jit(solution)/shard_map/ppermute | solution.py:718
  26.9 11.3 %collective-permute-start.4 = (bf16[128,896]{1,0:T(8,128)(2,1)S(1)}, bf16[128,896]{1,0:T(8,128)(2,1)S(1)}, u32[]{:S(2)}, u32[]{:S(2)}) collective-permute-start(bf16[128,896]{1,0:T(8,128)(2,1)S(1)} %constant_dynamic-update-slice_fusion.2.after_ref.refs_0_), channel_id=1, source_target_pairs={{0,8},{4,12},{8,16},{12,20},{16,24},{20,28},{24,0},{28,4},{1,9},{5... | collective-permute-start | bytes 688136 | tf_op jit(solution)/shard_map/ppermute | solution.py:718
  51.2 13.3 %collective-permute-start.10 = (bf16[32,3456]{1,0:T(8,128)(2,1)S(1)}, bf16[32,3456]{1,0:T(8,128)(2,1)S(1)}, u32[]{:S(2)}, u32[]{:S(2)}) collective-permute-start(bf16[32,3456]{1,0:T(8,128)(2,1)S(1)} %pad_maximum_fusion.3), channel_id=1, source_target_pairs={{0,8},{4,12},{8,16},{12,20},{16,24},{20,28},{24,0},{28,4},{1,9},{5... | collective-permute-start | bytes 663560 | tf_op jit(solution)/shard_map/ppermute | solution.py:718
  52.4 12.1 %collective-permute-start.11 = (bf16[32,3456]{1,0:T(8,128)(2,1)S(1)}, bf16[32,3456]{1,0:T(8,128)(2,1)S(1)}, u32[]{:S(2)}, u32[]{:S(2)}) collective-permute-start(bf16[32,3456]{1,0:T(8,128)(2,1)S(1)} %pad_maximum_fusion.4), channel_id=1, source_target_pairs={{0,16},{4,20},{8,24},{12,28},{16,0},{20,4},{24,8},{28,12},{1,17},{... | collective-permute-start | bytes 663560 | tf_op jit(solution)/shard_map/ppermute | solution.py:718
  53.0 11.5 %collective-permute-start.12 = (bf16[32,3456]{1,0:T(8,128)(2,1)S(1)}, bf16[32,3456]{1,0:T(8,128)(2,1)S(1)}, u32[]{:S(2)}, u32[]{:S(2)}) collective-permute-start(bf16[32,3456]{1,0:T(8,128)(2,1)S(1)} %pad_maximum_fusion.5), channel_id=1, source_target_pairs={{0,24},{4,28},{8,0},{12,4},{16,8},{20,12},{24,16},{28,20},{1,25},{... | collective-permute-start | bytes 663560 | tf_op jit(solution)/shard_map/ppermute | solution.py:718
  72.3 6.0 %collective-permute-start.17 = (bf16[32,2304]{1,0:T(8,128)(2,1)S(1)}, bf16[32,2304]{1,0:T(8,128)(2,1)S(1)}, u32[]{:S(2)}, u32[]{:S(2)}) collective-permute-start(bf16[32,2304]{1,0:T(8,128)(2,1)S(1)} %pad_maximum_fusion.10), channel_id=1, source_target_pairs={{0,1},{1,0},{2,3},{3,2},{4,5},{5,4},{6,7},{7,6},{8,9},{9,8},{10,11... | collective-permute-start | bytes 442376 | tf_op jit(solution)/shard_map/ppermute | solution.py:804
  72.4 18.3 %collective-permute-start.14 = (bf16[32,3072]{1,0:T(8,128)(2,1)S(1)}, bf16[32,3072]{1,0:T(8,128)(2,1)S(1)}, u32[]{:S(2)}, u32[]{:S(2)}) collective-permute-start(bf16[32,3072]{1,0:T(8,128)(2,1)S(1)} %pad_maximum_fusion.6), channel_id=1, source_target_pairs={{0,8},{4,12},{8,16},{12,20},{16,24},{20,28},{24,0},{28,4},{1,9},{5... | collective-permute-start | bytes 589832 | tf_op jit(solution)/shard_map/ppermute | solution.py:718
  72.7 18.0 %collective-permute-start.15 = (bf16[32,3072]{1,0:T(8,128)(2,1)S(1)}, bf16[32,3072]{1,0:T(8,128)(2,1)S(1)}, u32[]{:S(2)}, u32[]{:S(2)}) collective-permute-start(bf16[32,3072]{1,0:T(8,128)(2,1)S(1)} %pad_maximum_fusion.7), channel_id=1, source_target_pairs={{0,16},{4,20},{8,24},{12,28},{16,0},{20,4},{24,8},{28,12},{1,17},{... | collective-permute-start | bytes 589832 | tf_op jit(solution)/shard_map/ppermute | solution.py:718
  74.3 16.4 %collective-permute-start.16 = (bf16[32,3072]{1,0:T(8,128)(2,1)S(1)}, bf16[32,3072]{1,0:T(8,128)(2,1)S(1)}, u32[]{:S(2)}, u32[]{:S(2)}) collective-permute-start(bf16[32,3072]{1,0:T(8,128)(2,1)S(1)} %pad_maximum_fusion.8), channel_id=1, source_target_pairs={{0,24},{4,28},{8,0},{12,4},{16,8},{20,12},{24,16},{28,20},{1,25},{... | collective-permute-start | bytes 589832 | tf_op jit(solution)/shard_map/ppermute | solution.py:718
  78.3 12.2 %collective-permute-start.18 = (bf16[64,2304]{1,0:T(8,128)(2,1)S(1)}, bf16[64,2304]{1,0:T(8,128)(2,1)S(1)}, u32[]{:S(2)}, u32[]{:S(2)}) collective-permute-start(bf16[64,2304]{1,0:T(8,128)(2,1)S(1)} %pad_maximum_fusion.near_ref), channel_id=1, source_target_pairs={{0,3},{1,2},{2,1},{3,0},{4,7},{5,6},{6,5},{7,4},{8,11},{9,10},{10,... | collective-permute-start | bytes 884744 | tf_op jit(solution)/shard_map/ppermute | solution.py:804
  90.5 5.9 %collective-permute-start.19 = (bf16[128,768]{1,0:T(8,128)(2,1)S(1)}, bf16[128,768]{1,0:T(8,128)(2,1)S(1)}, u32[]{:S(2)}, u32[]{:S(2)}) collective-permute-start(bf16[128,768]{1,0:T(8,128)(2,1)S(1)} %pad_maximum_fusion.9.refs_9_), channel_id=1, source_target_pairs={{0,8},{4,12},{8,0},{12,4},{16,24},{20,28},{24,16},{28,20},{1,9},{5... | collective-permute-start | bytes 589832 | tf_op jit(solution)/shard_map/ppermute | solution.py:807
  96.5 14.4 %collective-permute-start.20 = (bf16[256,768]{1,0:T(8,128)(2,1)S(1)}, bf16[256,768]{1,0:T(8,128)(2,1)S(1)}, u32[]{:S(2)}, u32[]{:S(2)}) collective-permute-start(bf16[256,768]{1,0:T(8,128)(2,1)S(1)} %constant_dynamic-update-slice_fusion.7.low_chips), channel_id=1, source_target_pairs={{0,16},{4,20},{8,24},{12,28},{16,0},{20,4},{24,8},{28,12},{1,17},{... | collective-permute-start | bytes 1179656 | tf_op jit(solution)/shard_map/ppermute | solution.py:807
  98.0 12.3 %collective-permute-start.21 = (bf16[192,384]{1,0:T(8,128)(2,1)S(1)}, bf16[192,384]{1,0:T(8,128)(2,1)S(1)}, u32[]{:S(2)}, u32[]{:S(2)}) collective-permute-start(bf16[192,384]{1,0:T(8,128)(2,1)S(1)} %get-tuple-element.114), channel_id=1, source_target_pairs={{0,1},{1,2},{2,3},{3,0},{4,5},{5,6},{6,7},{7,4},{8,9},{9,10},{10,1... | collective-permute-start | bytes 442376 | tf_op jit(solution)/shard_map/ppermute | solution.py:721
  101.0 9.8 %collective-permute-start.22 = (bf16[192,384]{1,0:T(8,128)(2,1)S(1)}, bf16[192,384]{1,0:T(8,128)(2,1)S(1)}, u32[]{:S(2)}, u32[]{:S(2)}) collective-permute-start(bf16[192,384]{1,0:T(8,128)(2,1)S(1)} %get-tuple-element.115), channel_id=1, source_target_pairs={{0,2},{1,3},{2,0},{3,1},{4,6},{5,7},{6,4},{7,5},{8,10},{9,11},{10,... | collective-permute-start | bytes 442376 | tf_op jit(solution)/shard_map/ppermute | solution.py:721
  102.2 8.6 %collective-permute-start.23 = (bf16[192,384]{1,0:T(8,128)(2,1)S(1)}, bf16[192,384]{1,0:T(8,128)(2,1)S(1)}, u32[]{:S(2)}, u32[]{:S(2)}) collective-permute-start(bf16[192,384]{1,0:T(8,128)(2,1)S(1)} %get-tuple-element.116), channel_id=1, source_target_pairs={{0,3},{1,0},{2,1},{3,2},{4,7},{5,4},{6,5},{7,6},{8,11},{9,8},{10,9... | collective-permute-start | bytes 442376 | tf_op jit(solution)/shard_map/ppermute | solution.py:721
  112.0 14.1 %collective-permute-start.25 = (bf16[864,768]{1,0:T(8,128)(2,1)S(1)}, bf16[864,768]{1,0:T(8,128)(2,1)S(1)}, u32[]{:S(2)}, u32[]{:S(2)}) collective-permute-start(bf16[864,768]{1,0:T(8,128)(2,1)S(1)} %get-tuple-element.128), channel_id=1, source_target_pairs={{0,4},{4,0},{8,12},{12,8},{16,20},{20,16},{24,28},{28,24},{1,5},{5... | collective-permute-start | bytes 3981320 | tf_op jit(solution)/shard_map/ppermute | solution.py:715
  112.6 13.5 %collective-permute-start.26 = (f32[16,768]{1,0:T(8,128)S(1)}, f32[16,768]{1,0:T(8,128)S(1)}, u32[]{:S(2)}, u32[]{:S(2)}) collective-permute-start(f32[16,768]{1,0:T(8,128)S(1)} %get-tuple-element.129.own_ref), channel_id=1, source_target_pairs={{0,4},{4,0},{8,12},{12,8},{16,20},{20,16},{24,28},{28,24},{1,5},{5... | collective-permute-start | bytes 147464 | tf_op jit(solution)/shard_map/ppermute | solution.py:715
  115.5 14.7 %collective-permute-start.29 = (bf16[192,384]{1,0:T(8,128)(2,1)S(1)}, bf16[192,384]{1,0:T(8,128)(2,1)S(1)}, u32[]{:S(2)}, u32[]{:S(2)}) collective-permute-start(bf16[192,384]{1,0:T(8,128)(2,1)S(1)} %pad_maximum_fusion.11.refs_0_), channel_id=1, source_target_pairs={{0,3},{1,0},{2,1},{3,2},{4,7},{5,4},{6,5},{7,6},{8,11},{9,8},{10,9... | collective-permute-start | bytes 442376 | tf_op jit(solution)/shard_map/ppermute | solution.py:721
  120.3 12.8 %collective-permute-start.28 = (bf16[192,384]{1,0:T(8,128)(2,1)S(1)}, bf16[192,384]{1,0:T(8,128)(2,1)S(1)}, u32[]{:S(2)}, u32[]{:S(2)}) collective-permute-start(bf16[192,384]{1,0:T(8,128)(2,1)S(1)} %pad_maximum_fusion.11.refs_0_), channel_id=1, source_target_pairs={{0,2},{1,3},{2,0},{3,1},{4,6},{5,7},{6,4},{7,5},{8,10},{9,11},{10,... | collective-permute-start | bytes 442376 | tf_op jit(solution)/shard_map/ppermute | solution.py:721
  120.3 12.8 %collective-permute-start.27 = (bf16[192,384]{1,0:T(8,128)(2,1)S(1)}, bf16[192,384]{1,0:T(8,128)(2,1)S(1)}, u32[]{:S(2)}, u32[]{:S(2)}) collective-permute-start(bf16[192,384]{1,0:T(8,128)(2,1)S(1)} %pad_maximum_fusion.11.refs_0_), channel_id=1, source_target_pairs={{0,1},{1,2},{2,3},{3,0},{4,5},{5,6},{6,7},{7,4},{8,9},{9,10},{10,1... | collective-permute-start | bytes 442376 | tf_op jit(solution)/shard_map/ppermute | solution.py:721
  (39 other events, 409.7 us)

commit v3 on v2

--- a/solution.py
+++ b/solution.py
@@ -424,11 +424,16 @@
 
     columns = slope_ref.shape[1]
     at = pl.multiple_of(step * columns, columns)
-    pre = mm(low_ref[...], wback_ref[pl.ds(at, columns), :], NT) * slope_ref[...].astype(F32)
-    bias = jnp.sum(pre, axis=0, keepdims=True)
-    pre_low = pre.astype(BF)
-    gpl_ref[...] = pre_low
-    acc[...] += mm(pre_low, win_ref[:, pl.ds(at, columns)], NT)
+    strip = count // 2
+    bias = jnp.zeros((1, columns), F32)
+    spans = [slice(k * strip, (k + 1) * strip) for k in range(2)]
+    rising = [mm(low_ref[span, :], wback_ref[pl.ds(at, columns), :], NT) for span in spans]
+    for span, grown in zip(spans, rising):
+        pre = grown * slope_ref[span, :].astype(F32)
+        bias = bias + jnp.sum(pre, axis=0, keepdims=True)
+        pre_low = pre.astype(BF)
+        gpl_ref[span, :] = pre_low
+        acc[span, :] += mm(pre_low, win_ref[:, pl.ds(at, columns)], NT)
     for s in range(steps):
         @pl.when(step == s)
         def keep_bias():
@@ -821,7 +826,7 @@
         [shape_of((count, ff), BF), shape_of((count, width), BF), shape_of((count, width), BF),
          shape_of((chips * 2 * rows, width), BF), shape_of((16, width), F32), shape_of((near.shape[0], width), BF)],
         [pl.BlockSpec((count, fc), lambda s, ids: (0, s)), None, None, None, None, None],
-        [vm((count, width), F32), vm((count, width), BF)], grid=(steps,), vmem=30 if count <= 1024 else 60, work=(12e9, 18e6))
+        [vm((count, width), F32), vm((count, width), BF)], grid=(steps,), vmem=26 if count <= 1024 else 60, work=(12e9, 18e6))
 
     gq_column = jnp.concatenate([gq_near, far_z[:, 0:width]], axis=0)
 
@@ -830,7 +835,7 @@
         "share", functools.partial(share_kernel, heads, chips, depth, part), ids,
         late + early + [g_plane, gq_column], [None] * (2 * chips + 2),
         [shape_of((part, span), BF)] * depth + [shape_of(gq_column.shape, BF)], [None] * (depth + 1),
-        [vm((part, 2 * width), F32)], vmem=28 if count <= 1024 else 60, work=(1e9, 3e6))
+        [vm((part, 2 * width), F32)], vmem=24 if count <= 1024 else 60, work=(1e9, 3e6))
     masks = chip_masks(chips)
     gq_low = jnp.concatenate([gq_first, xor_chip(gq_column, masks[0])], axis=0)
     gq_low = double(gq_low, xor_chip, masks[1:-1])
@@ -849,7 +854,7 @@
          shape_of((in_rows + ghalf + half, width), BF)],
         [pl.BlockSpec((1, half, fc), lambda s, ids: (ids[0], 0, s)), out_block(ghalf, width), out_block(half, width), None],
         [vm((count, part), BF), vm((part, fc), F32), vm((fpart, width), F32), vm((part, width), F32)],
-        grid=(steps,), vmem=28 if count <= 1024 else 60, work=(4e9, 12e6))
+        grid=(steps,), vmem=24 if count <= 1024 else 60, work=(4e9, 12e6))
     gw_q, keep, send, small, sib = kernel_call(
         "query", functools.partial(query_kernel, chips, depth, rows, part), ids,
         [sib, near, far_z, gq_low, gq_high] + shares + [small], [ANY] + [None] * (depth + 5),

time: 136 us -> 135 us (level)
    unnamed x70 -> x36, local copies, waits for them, and re-layouts: 7.84 us -> 6.61 us
  transfers between devices with their start and end apart: 30 -> 30, of which waited for: 12 -> 13; matrix products, arithmetic and copies ran while one was open for 1% -> 1% of each run, Pallas kernels for 29% -> 29%
where the time goes in v3:
time: 135 us
  Pallas kernels  68.7 us (51%)
  starting transfers between devices  38.2 us (28%)
  waiting for transfers between devices  20 us (15%)
  local copies, waits for them, and re-layouts  6.79 us (5%)
    pallas_call x12, Pallas kernels, kernel_call(): pl.pallas_call(kernel, grid_spec=pltpu.PrefetchScalarGridSpec(num_scalar_...  68.7 us
    ppermute x9, starting transfers between devices, to_depth(): lax.ppermute(x, 'group', [(s, (s + k) % depth) for s in range(depth)])  18.9 us
    ppermute x9, starting transfers between devices, to_chip(): lax.ppermute(x, 'dp', [(s, (s // 2 + k) % chips * 2 + s % 2) for s in ran...  12 us
    ppermute x9, waiting for transfers between devices, to_depth(): lax.ppermute(x, 'group', [(s, (s + k) % depth) for s in range(depth)])  8.28 us
    unnamed x36, local copies, waits for them, and re-layouts  6.61 us
    ppermute x8, waiting for transfers between devices, swap(): return lax.ppermute(x, 'dp', [(k, k ^ 1) for k in range(n_dp)])  6.03 us
    ppermute x2, starting transfers between devices, xor_depth(): return lax.ppermute(x, 'group', [(s, s ^ mask) for s in range(depth)])  2.88 us
  transfers between devices with their start and end apart: 30, of which 13 were waited for; matrix products, arithmetic and copies ran while one was open for 1% of the time, Pallas kernels for 29%

profile of v3, /device:TPU:0, one launch (start us, length us, event | category | flops | bytes accessed | tf_op | source)
XLA Modules:
  0.0 135.0 jit_solution(711808947040170271)
XLA Ops:
  0.7 10.7 %attend.1 = (bf16[16,896]{1,0:T(8,128)(2,1)}, bf16[16,896]{1,0:T(8,128)(2,1)}, bf16[4,16,3456]{2,1,0:T(8,128)(2,1)}, bf16[4,16,3456]{2,1,0:T(8,128)(2,1)}, bf16[...) custom-call(s32[16]{0:T(128)} %qlen_ref.3, s32[4,4]{1,0:T(4,128)} %plen_ref.3, s32[16]{0:T(128)} %pos_ref.1, ...), custom_call_target="tpu_custom_call" | custom-call | flops 6000000000 | bytes 13000000 | tf_op jit(solution)/shard_map/attend/pallas_call | solution.py:685
  13.0 3.0 %collective-permute-start.1 = (bf16[32,896]{1,0:T(8,128)(2,1)S(1)}, bf16[32,896]{1,0:T(8,128)(2,1)S(1)}, u32[]{:S(2)}, u32[]{:S(2)}) collective-permute-start(bf16[32,896]{1,0:T(8,128)(2,1)S(1)} %get-tuple-element.157), channel_id=1, source_target_pairs={{0,1},{1,2},{2,3},{3,0},{4,5},{5,6},{6,7},{7,4},{8,9},{9,10},{10,1... | collective-permute-start | bytes 172040 | tf_op jit(solution)/shard_map/ppermute | solution.py:726
  16.0 2.0 %collective-permute-start.3 = (bf16[32,896]{1,0:T(8,128)(2,1)S(1)}, bf16[32,896]{1,0:T(8,128)(2,1)S(1)}, u32[]{:S(2)}, u32[]{:S(2)}) collective-permute-start(bf16[32,896]{1,0:T(8,128)(2,1)S(1)} %get-tuple-element.157), channel_id=1, source_target_pairs={{0,3},{1,0},{2,1},{3,2},{4,7},{5,4},{6,5},{7,6},{8,11},{9,8},{10,9... | collective-permute-start | bytes 172040 | tf_op jit(solution)/shard_map/ppermute | solution.py:726
  20.3 3.5 %collective-permute-done.2 = bf16[32,896]{1,0:T(8,128)(2,1)S(1)} collective-permute-done((bf16[32,896]{1,0:T(8,128)(2,1)S(1)}, bf16[32,896]{1,0:T(8,128)(2,1)S(1)}, u32[]{:S(2)}, u32[]{:S(2)}) %collective-permute-start.2) | collective-permute-done | bytes 57376 | tf_op jit(solution)/shard_map/ppermute | solution.py:726
  23.9 2.5 %collective-permute-start.6 = (bf16[128,896]{1,0:T(8,128)(2,1)S(1)}, bf16[128,896]{1,0:T(8,128)(2,1)S(1)}, u32[]{:S(2)}, u32[]{:S(2)}) collective-permute-start(bf16[128,896]{1,0:T(8,128)(2,1)S(1)} %constant_dynamic-update-slice_fusion.2.after_ref.refs_0_), channel_id=1, source_target_pairs={{0,24},{4,28},{8,0},{12,4},{16,8},{20,12},{24,16},{28,20},{1,25},{... | collective-permute-start | bytes 688136 | tf_op jit(solution)/shard_map/ppermute | solution.py:723
  30.3 6.5 %stage.1 = (bf16[768,3072]{1,0:T(8,128)(2,1)S(1)}, bf16[3072,768]{1,0:T(8,128)(2,1)S(1)}, bf16[768,768]{1,0:T(8,128)(2,1)S(1)}, bf16[2,1024,768]{2,1,0:T(8,128)(2,1)S(1)}, bf16[2,3,768,768]{3,2,1,0:T(8,128)(2,1)S(1)}) custom-call(s32[3]{0:T(128)S(1)} %pad_add_fusion.ids, bf16[128,896]{1,0:T(8,128)(2,1)S(1)} %constant_dynamic-update-slice_fusion.2.after_ref.refs_0_, ...), custom_call_target="tpu_custom_call" | custom-call | flops 5000000000 | bytes 10000000 | tf_op jit(solution)/shard_map/stage/pallas_call | solution.py:685
  38.3 11.3 %forward.1 = (bf16[512,768]{1,0:T(8,128)(2,1)S(1)}, bf16[512,3072]{1,0:T(8,128)(2,1)S(1)}, bf16[512,768]{1,0:T(8,128)(2,1)S(1)}, bf16[512,768]{1,0:T(8,128)(2,1)...) custom-call(s32[3]{0:T(128)S(1)} %pad_add_fusion.ids, ...), custom_call_target="tpu_custom_call", output_to_operand_aliasing={{7}: (11, {})} | custom-call | flops 10000000000 | bytes 18000000 | tf_op jit(solution)/shard_map/forward/pallas_call | solution.py:685
  53.2 1.9 %collective-permute-start.12 = (bf16[32,3456]{1,0:T(8,128)(2,1)S(1)}, bf16[32,3456]{1,0:T(8,128)(2,1)S(1)}, u32[]{:S(2)}, u32[]{:S(2)}) collective-permute-start(bf16[32,3456]{1,0:T(8,128)(2,1)S(1)} %pad_maximum_fusion.5), channel_id=1, source_target_pairs={{0,24},{4,28},{8,0},{12,4},{16,8},{20,12},{24,16},{28,20},{1,25},{... | collective-permute-start | bytes 663560 | tf_op jit(solution)/shard_map/ppermute | solution.py:723
  55.1 8.4 %loss.1 = (f32[512,768]{1,0:T(8,128)S(1)}, f32[1,16]{1,0:T(1,128)}, f32[16,1536]{1,0:T(8,128)S(1)}, f32[16,1536]{1,0:T(8,128)S(1)}, f32[8,768]{1,0:T(8,128)S(1)}...) custom-call(s32[3]{0:T(128)S(1)} %pad_add_fusion.ids, bf16[512,768]{1,0:T(8,128)(2,1)S(1)} %get-tuple-element.83.own_ref, ...), custom_call_target="tpu_custom_call" | custom-call | flops 8000000000 | bytes 16000000 | tf_op jit(solution)/shard_map/loss/pallas_call | solution.py:685
  64.8 4.5 %attend_back.1 = (bf16[4,16,3072]{2,1,0:T(8,128)(2,1)S(1)}, bf16[4,16,3072]{2,1,0:T(8,128)(2,1)S(1)}, bf16[2,192,1024]{2,1,0:T(8,128)(2,1)S(1)}, bf16[2,192,768]...) custom-call(s32[3]{0:T(128)S(1)} %pad_add_fusion.ids, ...), custom_call_target="tpu_custom_call" | custom-call | flops 6000000000 | bytes 16000000 | tf_op jit(solution)/shard_map/attend_back/pallas_call | solution.py:685
  73.7 2.5 %collective-permute-start.16 = (bf16[32,3072]{1,0:T(8,128)(2,1)S(1)}, bf16[32,3072]{1,0:T(8,128)(2,1)S(1)}, u32[]{:S(2)}, u32[]{:S(2)}) collective-permute-start(bf16[32,3072]{1,0:T(8,128)(2,1)S(1)} %pad_maximum_fusion.8), channel_id=1, source_target_pairs={{0,24},{4,28},{8,0},{12,4},{16,8},{20,12},{24,16},{28,20},{1,25},{... | collective-permute-start | bytes 589832 | tf_op jit(solution)/shard_map/ppermute | solution.py:723
  77.2 2.8 %collective-permute-start.18 = (bf16[64,2304]{1,0:T(8,128)(2,1)S(1)}, bf16[64,2304]{1,0:T(8,128)(2,1)S(1)}, u32[]{:S(2)}, u32[]{:S(2)}) collective-permute-start(bf16[64,2304]{1,0:T(8,128)(2,1)S(1)} %pad_maximum_fusion.near_ref), channel_id=1, source_target_pairs={{0,3},{1,2},{2,1},{3,0},{4,7},{5,6},{6,5},{7,4},{8,11},{9,10},{10,... | collective-permute-start | bytes 884744 | tf_op jit(solution)/shard_map/ppermute | solution.py:809
  80.0 9.0 %backward.1 = (bf16[512,3072]{1,0:T(8,128)(2,1)S(1)}, bf16[512,768]{1,0:T(8,128)(2,1)S(1)}, bf16[512,768]{1,0:T(8,128)(2,1)S(1)}, bf16[128,768]{1,0:T(8,128)(2,1...) custom-call(s32[3]{0:T(128)S(1)} %pad_add_fusion.ids, bf16[64,2304]{1,0:T(8,128)(2,1)S(1)} %pad_maximum_fusion.near_ref, ...), custom_call_target="tpu_custom_call" | custom-call | flops 12000000000 | bytes 18000000 | tf_op jit(solution)/shard_map/backward/pallas_call | solution.py:685
  89.9 2.8 %share.1 = (bf16[192,384]{1,0:T(8,128)(2,1)S(1)}, bf16[192,384]{1,0:T(8,128)(2,1)S(1)}, bf16[192,384]{1,0:T(8,128)(2,1)S(1)}, bf16[192,384]{1,0:T(8,128)(2,1)S(1)}, bf16[128,768]{1,0:T(8,128)(2,1)S(1)}) custom-call(s32[3]{0:T(128)S(1)} %pad_add_fusion.ids, bf16[32,3072]{1,0:T(8,128)(2,1)S(1)} %pad_maximum_fusion.1.refs_0_, ...), custom_call_target="tpu_custom_call" | custom-call | flops 1000000000 | bytes 3000000 | tf_op jit(solution)/shard_map/share/pallas_call | solution.py:685
  92.8 2.3 %collective-permute-done.19 = bf16[128,768]{1,0:T(8,128)(2,1)S(1)} collective-permute-done((bf16[128,768]{1,0:T(8,128)(2,1)S(1)}, bf16[128,768]{1,0:T(8,128)(2,1)S(1)}, u32[]{:S(2)}, u32[]{:S(2)}) %collective-permute-start.19) | collective-permute-done | bytes 196640 | tf_op jit(solution)/shard_map/ppermute | solution.py:812
  96.6 3.3 %collective-permute-start.21 = (bf16[192,384]{1,0:T(8,128)(2,1)S(1)}, bf16[192,384]{1,0:T(8,128)(2,1)S(1)}, u32[]{:S(2)}, u32[]{:S(2)}) collective-permute-start(bf16[192,384]{1,0:T(8,128)(2,1)S(1)} %get-tuple-element.114), channel_id=1, source_target_pairs={{0,1},{1,2},{2,3},{3,0},{4,5},{5,6},{6,7},{7,4},{8,9},{9,10},{10,1... | collective-permute-start | bytes 442376 | tf_op jit(solution)/shard_map/ppermute | solution.py:726
  101.1 2.9 %collective-permute-start.23 = (bf16[192,384]{1,0:T(8,128)(2,1)S(1)}, bf16[192,384]{1,0:T(8,128)(2,1)S(1)}, u32[]{:S(2)}, u32[]{:S(2)}) collective-permute-start(bf16[192,384]{1,0:T(8,128)(2,1)S(1)} %get-tuple-element.116), channel_id=1, source_target_pairs={{0,3},{1,0},{2,1},{3,2},{4,7},{5,4},{6,5},{7,6},{8,11},{9,8},{10,9... | collective-permute-start | bytes 442376 | tf_op jit(solution)/shard_map/ppermute | solution.py:726
  104.0 5.2 %weight.1 = (f32[2,96,3072]{2,1,0:T(8,128)}, f32[2,384,768]{2,1,0:T(8,128)}, f32[2,96,768]{2,1,0:T(8,128)}, bf16[864,768]{1,0:T(8,128)(2,1)S(1)}) custom-call(s32[3]{0:T(128)S(1)} %pad_add_fusion.ids, bf16[192,384]{1,0:T(8,128)(2,1)S(1)} %get-tuple-element.106.after_ref.refs_0_, bf16[64,2304]{1,0:T(8,128)(2,1)S(1)} %pad_maximum_fusion.near_ref, ...), custom_call_target="tpu_custom_call" | custom-call | flops 4000000000 | bytes 12000000 | tf_op jit(solution)/shard_map/weight/pallas_call | solution.py:685
  111.5 2.8 %collective-permute-done.24.after_ref.refs_5_ = bf16[96,1152]{1,0:T(8,128)(2,1)S(1)} collective-permute-done((bf16[96,1152]{1,0:T(8,128)(2,1)S(1)}, bf16[96,1152]{1,0:T(8,128)(2,1)S(1)}, u32[]{:S(2)}, u32[]{:S(2)}) %collective-permute-start.24) | collective-permute-done | bytes 221216 | tf_op jit(solution)/shard_map/ppermute | solution.py:720
  114.3 4.9 %collective-permute-start.29 = (bf16[192,384]{1,0:T(8,128)(2,1)S(1)}, bf16[192,384]{1,0:T(8,128)(2,1)S(1)}, u32[]{:S(2)}, u32[]{:S(2)}) collective-permute-start(bf16[192,384]{1,0:T(8,128)(2,1)S(1)} %pad_maximum_fusion.11.refs_0_), channel_id=1, source_target_pairs={{0,3},{1,0},{2,1},{3,2},{4,7},{5,4},{6,5},{7,6},{8,11},{9,8},{10,9... | collective-permute-start | bytes 442376 | tf_op jit(solution)/shard_map/ppermute | solution.py:726
  119.9 5.1 %token_grad.1 = (f32[1024,768]{1,0:T(8,128)}, f32[1024,768]{1,0:T(8,128)}) custom-call(s32[3]{0:T(128)S(1)} %pad_add_fusion.ids, bf16[96,1152]{1,0:T(8,128)(2,1)S(1)} %collective-permute-done.24.after_ref.refs_5_, s32[16]{0:T(128)S(1)} %copy-done.12, s32[4,4]{1,0:T(4,128)S(1)} %copy-done.11, bf16[2,192,1024]{2,1,0:T(8,128)(2,1)S(1)} %get-tuple-element.119.att_ref, ...), custom_call_target="tpu_custom_call" | custom-call | flops 2000000000 | bytes 9000000 | tf_op jit(solution)/shard_map/token_grad/pallas_call | solution.py:685
  125.0 1.9 %copy-done = f32[1024,768]{1,0:T(8,128)S(1)} copy-done((f32[1024,768]{1,0:T(8,128)S(1)}, f32[1024,768]{1,0:T(8,128)}, u32[]{:S(2)}) %copy-start) | copy-done | bytes 3145752
  126.9 2.2 %fill.1 = (f32[2,96,3072]{2,1,0:T(8,128)}, f32[2,384,768]{2,1,0:T(8,128)}, f32[2,96,768]{2,1,0:T(8,128)}, f32[2,2,768]{2,1,0:T(2,128)}, f32[2,768]{1,0:T(2,128)}...) custom-call(s32[3]{0:T(128)S(1)} %pad_add_fusion.ids, ...), custom_call_target="tpu_custom_call", output_to_operand_aliasing={{0}: (2, {}), {1}: (3, {}), {2}: (4, {})} | custom-call | flops 1000000 | bytes 8000000 | tf_op jit(solution)/shard_map/fill/pallas_call | solution.py:685
  129.0 3.0 %collective-permute-done.28.refs_2_ = bf16[192,384]{1,0:T(8,128)(2,1)S(1)} collective-permute-done((bf16[192,384]{1,0:T(8,128)(2,1)S(1)}, bf16[192,384]{1,0:T(8,128)(2,1)S(1)}, u32[]{:S(2)}, u32[]{:S(2)}) %collective-permute-start.28) | collective-permute-done | bytes 147488 | tf_op jit(solution)/shard_map/ppermute | solution.py:726
  (107 shorter events, 28.9 us)
Async XLA Ops:
  13.0 7.3 %collective-permute-start.1 = (bf16[32,896]{1,0:T(8,128)(2,1)S(1)}, bf16[32,896]{1,0:T(8,128)(2,1)S(1)}, u32[]{:S(2)}, u32[]{:S(2)}) collective-permute-start(bf16[32,896]{1,0:T(8,128)(2,1)S(1)} %get-tuple-element.157), channel_id=1, source_target_pairs={{0,1},{1,2},{2,3},{3,0},{4,5},{5,6},{6,7},{7,4},{8,9},{9,10},{10,1... | collective-permute-start | bytes 172040 | tf_op jit(solution)/shard_map/ppermute | solution.py:726
  16.0 7.8 %collective-permute-start.3 = (bf16[32,896]{1,0:T(8,128)(2,1)S(1)}, bf16[32,896]{1,0:T(8,128)(2,1)S(1)}, u32[]{:S(2)}, u32[]{:S(2)}) collective-permute-start(bf16[32,896]{1,0:T(8,128)(2,1)S(1)} %get-tuple-element.157), channel_id=1, source_target_pairs={{0,3},{1,0},{2,1},{3,2},{4,7},{5,4},{6,5},{7,6},{8,11},{9,8},{10,9... | collective-permute-start | bytes 172040 | tf_op jit(solution)/shard_map/ppermute | solution.py:726
  18.0 5.8 %collective-permute-start.2 = (bf16[32,896]{1,0:T(8,128)(2,1)S(1)}, bf16[32,896]{1,0:T(8,128)(2,1)S(1)}, u32[]{:S(2)}, u32[]{:S(2)}) collective-permute-start(bf16[32,896]{1,0:T(8,128)(2,1)S(1)} %get-tuple-element.157), channel_id=1, source_target_pairs={{0,2},{1,3},{2,0},{3,1},{4,6},{5,7},{6,4},{7,5},{8,10},{9,11},{10,... | collective-permute-start | bytes 172040 | tf_op jit(solution)/shard_map/ppermute | solution.py:726
  23.9 13.0 %collective-permute-start.6 = (bf16[128,896]{1,0:T(8,128)(2,1)S(1)}, bf16[128,896]{1,0:T(8,128)(2,1)S(1)}, u32[]{:S(2)}, u32[]{:S(2)}) collective-permute-start(bf16[128,896]{1,0:T(8,128)(2,1)S(1)} %constant_dynamic-update-slice_fusion.2.after_ref.refs_0_), channel_id=1, source_target_pairs={{0,24},{4,28},{8,0},{12,4},{16,8},{20,12},{24,16},{28,20},{1,25},{... | collective-permute-start | bytes 688136 | tf_op jit(solution)/shard_map/ppermute | solution.py:723
  26.4 11.8 %collective-permute-start.5 = (bf16[128,896]{1,0:T(8,128)(2,1)S(1)}, bf16[128,896]{1,0:T(8,128)(2,1)S(1)}, u32[]{:S(2)}, u32[]{:S(2)}) collective-permute-start(bf16[128,896]{1,0:T(8,128)(2,1)S(1)} %constant_dynamic-update-slice_fusion.2.after_ref.refs_0_), channel_id=1, source_target_pairs={{0,16},{4,20},{8,24},{12,28},{16,0},{20,4},{24,8},{28,12},{1,17},{... | collective-permute-start | bytes 688136 | tf_op jit(solution)/shard_map/ppermute | solution.py:723
  26.9 11.3 %collective-permute-start.4 = (bf16[128,896]{1,0:T(8,128)(2,1)S(1)}, bf16[128,896]{1,0:T(8,128)(2,1)S(1)}, u32[]{:S(2)}, u32[]{:S(2)}) collective-permute-start(bf16[128,896]{1,0:T(8,128)(2,1)S(1)} %constant_dynamic-update-slice_fusion.2.after_ref.refs_0_), channel_id=1, source_target_pairs={{0,8},{4,12},{8,16},{12,20},{16,24},{20,28},{24,0},{28,4},{1,9},{5... | collective-permute-start | bytes 688136 | tf_op jit(solution)/shard_map/ppermute | solution.py:723
  51.5 12.1 %collective-permute-start.10 = (bf16[32,3456]{1,0:T(8,128)(2,1)S(1)}, bf16[32,3456]{1,0:T(8,128)(2,1)S(1)}, u32[]{:S(2)}, u32[]{:S(2)}) collective-permute-start(bf16[32,3456]{1,0:T(8,128)(2,1)S(1)} %pad_maximum_fusion.3), channel_id=1, source_target_pairs={{0,8},{4,12},{8,16},{12,20},{16,24},{20,28},{24,0},{28,4},{1,9},{5... | collective-permute-start | bytes 663560 | tf_op jit(solution)/shard_map/ppermute | solution.py:723
  52.6 12.0 %collective-permute-start.11 = (bf16[32,3456]{1,0:T(8,128)(2,1)S(1)}, bf16[32,3456]{1,0:T(8,128)(2,1)S(1)}, u32[]{:S(2)}, u32[]{:S(2)}) collective-permute-start(bf16[32,3456]{1,0:T(8,128)(2,1)S(1)} %pad_maximum_fusion.4), channel_id=1, source_target_pairs={{0,16},{4,20},{8,24},{12,28},{16,0},{20,4},{24,8},{28,12},{1,17},{... | collective-permute-start | bytes 663560 | tf_op jit(solution)/shard_map/ppermute | solution.py:723
  53.2 11.4 %collective-permute-start.12 = (bf16[32,3456]{1,0:T(8,128)(2,1)S(1)}, bf16[32,3456]{1,0:T(8,128)(2,1)S(1)}, u32[]{:S(2)}, u32[]{:S(2)}) collective-permute-start(bf16[32,3456]{1,0:T(8,128)(2,1)S(1)} %pad_maximum_fusion.5), channel_id=1, source_target_pairs={{0,24},{4,28},{8,0},{12,4},{16,8},{20,12},{24,16},{28,20},{1,25},{... | collective-permute-start | bytes 663560 | tf_op jit(solution)/shard_map/ppermute | solution.py:723
  71.2 6.0 %collective-permute-start.17 = (bf16[32,2304]{1,0:T(8,128)(2,1)S(1)}, bf16[32,2304]{1,0:T(8,128)(2,1)S(1)}, u32[]{:S(2)}, u32[]{:S(2)}) collective-permute-start(bf16[32,2304]{1,0:T(8,128)(2,1)S(1)} %pad_maximum_fusion.10), channel_id=1, source_target_pairs={{0,1},{1,0},{2,3},{3,2},{4,5},{5,4},{6,7},{7,6},{8,9},{9,8},{10,11... | collective-permute-start | bytes 442376 | tf_op jit(solution)/shard_map/ppermute | solution.py:809
  71.3 18.5 %collective-permute-start.14 = (bf16[32,3072]{1,0:T(8,128)(2,1)S(1)}, bf16[32,3072]{1,0:T(8,128)(2,1)S(1)}, u32[]{:S(2)}, u32[]{:S(2)}) collective-permute-start(bf16[32,3072]{1,0:T(8,128)(2,1)S(1)} %pad_maximum_fusion.6), channel_id=1, source_target_pairs={{0,8},{4,12},{8,16},{12,20},{16,24},{20,28},{24,0},{28,4},{1,9},{5... | collective-permute-start | bytes 589832 | tf_op jit(solution)/shard_map/ppermute | solution.py:723
  72.1 17.8 %collective-permute-start.15 = (bf16[32,3072]{1,0:T(8,128)(2,1)S(1)}, bf16[32,3072]{1,0:T(8,128)(2,1)S(1)}, u32[]{:S(2)}, u32[]{:S(2)}) collective-permute-start(bf16[32,3072]{1,0:T(8,128)(2,1)S(1)} %pad_maximum_fusion.7), channel_id=1, source_target_pairs={{0,16},{4,20},{8,24},{12,28},{16,0},{20,4},{24,8},{28,12},{1,17},{... | collective-permute-start | bytes 589832 | tf_op jit(solution)/shard_map/ppermute | solution.py:723
  73.7 16.2 %collective-permute-start.16 = (bf16[32,3072]{1,0:T(8,128)(2,1)S(1)}, bf16[32,3072]{1,0:T(8,128)(2,1)S(1)}, u32[]{:S(2)}, u32[]{:S(2)}) collective-permute-start(bf16[32,3072]{1,0:T(8,128)(2,1)S(1)} %pad_maximum_fusion.8), channel_id=1, source_target_pairs={{0,24},{4,28},{8,0},{12,4},{16,8},{20,12},{24,16},{28,20},{1,25},{... | collective-permute-start | bytes 589832 | tf_op jit(solution)/shard_map/ppermute | solution.py:723
  77.2 11.9 %collective-permute-start.18 = (bf16[64,2304]{1,0:T(8,128)(2,1)S(1)}, bf16[64,2304]{1,0:T(8,128)(2,1)S(1)}, u32[]{:S(2)}, u32[]{:S(2)}) collective-permute-start(bf16[64,2304]{1,0:T(8,128)(2,1)S(1)} %pad_maximum_fusion.near_ref), channel_id=1, source_target_pairs={{0,3},{1,2},{2,1},{3,0},{4,7},{5,6},{6,5},{7,4},{8,11},{9,10},{10,... | collective-permute-start | bytes 884744 | tf_op jit(solution)/shard_map/ppermute | solution.py:809
  89.1 5.9 %collective-permute-start.19 = (bf16[128,768]{1,0:T(8,128)(2,1)S(1)}, bf16[128,768]{1,0:T(8,128)(2,1)S(1)}, u32[]{:S(2)}, u32[]{:S(2)}) collective-permute-start(bf16[128,768]{1,0:T(8,128)(2,1)S(1)} %pad_maximum_fusion.9.refs_9_), channel_id=1, source_target_pairs={{0,8},{4,12},{8,0},{12,4},{16,24},{20,28},{24,16},{28,20},{1,9},{5... | collective-permute-start | bytes 589832 | tf_op jit(solution)/shard_map/ppermute | solution.py:812
  95.1 14.6 %collective-permute-start.20 = (bf16[256,768]{1,0:T(8,128)(2,1)S(1)}, bf16[256,768]{1,0:T(8,128)(2,1)S(1)}, u32[]{:S(2)}, u32[]{:S(2)}) collective-permute-start(bf16[256,768]{1,0:T(8,128)(2,1)S(1)} %constant_dynamic-update-slice_fusion.7.low_chips), channel_id=1, source_target_pairs={{0,16},{4,20},{8,24},{12,28},{16,0},{20,4},{24,8},{28,12},{1,17},{... | collective-permute-start | bytes 1179656 | tf_op jit(solution)/shard_map/ppermute | solution.py:812
  96.6 12.6 %collective-permute-start.21 = (bf16[192,384]{1,0:T(8,128)(2,1)S(1)}, bf16[192,384]{1,0:T(8,128)(2,1)S(1)}, u32[]{:S(2)}, u32[]{:S(2)}) collective-permute-start(bf16[192,384]{1,0:T(8,128)(2,1)S(1)} %get-tuple-element.114), channel_id=1, source_target_pairs={{0,1},{1,2},{2,3},{3,0},{4,5},{5,6},{6,7},{7,4},{8,9},{9,10},{10,1... | collective-permute-start | bytes 442376 | tf_op jit(solution)/shard_map/ppermute | solution.py:726
  99.9 9.8 %collective-permute-start.22 = (bf16[192,384]{1,0:T(8,128)(2,1)S(1)}, bf16[192,384]{1,0:T(8,128)(2,1)S(1)}, u32[]{:S(2)}, u32[]{:S(2)}) collective-permute-start(bf16[192,384]{1,0:T(8,128)(2,1)S(1)} %get-tuple-element.115), channel_id=1, source_target_pairs={{0,2},{1,3},{2,0},{3,1},{4,6},{5,7},{6,4},{7,5},{8,10},{9,11},{10,... | collective-permute-start | bytes 442376 | tf_op jit(solution)/shard_map/ppermute | solution.py:726
  101.1 8.6 %collective-permute-start.23 = (bf16[192,384]{1,0:T(8,128)(2,1)S(1)}, bf16[192,384]{1,0:T(8,128)(2,1)S(1)}, u32[]{:S(2)}, u32[]{:S(2)}) collective-permute-start(bf16[192,384]{1,0:T(8,128)(2,1)S(1)} %get-tuple-element.116), channel_id=1, source_target_pairs={{0,3},{1,0},{2,1},{3,2},{4,7},{5,4},{6,5},{7,6},{8,11},{9,8},{10,9... | collective-permute-start | bytes 442376 | tf_op jit(solution)/shard_map/ppermute | solution.py:726
  110.8 14.1 %collective-permute-start.25 = (bf16[864,768]{1,0:T(8,128)(2,1)S(1)}, bf16[864,768]{1,0:T(8,128)(2,1)S(1)}, u32[]{:S(2)}, u32[]{:S(2)}) collective-permute-start(bf16[864,768]{1,0:T(8,128)(2,1)S(1)} %get-tuple-element.128), channel_id=1, source_target_pairs={{0,4},{4,0},{8,12},{12,8},{16,20},{20,16},{24,28},{28,24},{1,5},{5... | collective-permute-start | bytes 3981320 | tf_op jit(solution)/shard_map/ppermute | solution.py:720
  111.4 13.6 %collective-permute-start.26 = (f32[16,768]{1,0:T(8,128)S(1)}, f32[16,768]{1,0:T(8,128)S(1)}, u32[]{:S(2)}, u32[]{:S(2)}) collective-permute-start(f32[16,768]{1,0:T(8,128)S(1)} %get-tuple-element.129.own_ref), channel_id=1, source_target_pairs={{0,4},{4,0},{8,12},{12,8},{16,20},{20,16},{24,28},{28,24},{1,5},{5... | collective-permute-start | bytes 147464 | tf_op jit(solution)/shard_map/ppermute | solution.py:720
  114.3 14.7 %collective-permute-start.29 = (bf16[192,384]{1,0:T(8,128)(2,1)S(1)}, bf16[192,384]{1,0:T(8,128)(2,1)S(1)}, u32[]{:S(2)}, u32[]{:S(2)}) collective-permute-start(bf16[192,384]{1,0:T(8,128)(2,1)S(1)} %pad_maximum_fusion.11.refs_0_), channel_id=1, source_target_pairs={{0,3},{1,0},{2,1},{3,2},{4,7},{5,4},{6,5},{7,6},{8,11},{9,8},{10,9... | collective-permute-start | bytes 442376 | tf_op jit(solution)/shard_map/ppermute | solution.py:726
  119.2 12.8 %collective-permute-start.28 = (bf16[192,384]{1,0:T(8,128)(2,1)S(1)}, bf16[192,384]{1,0:T(8,128)(2,1)S(1)}, u32[]{:S(2)}, u32[]{:S(2)}) collective-permute-start(bf16[192,384]{1,0:T(8,128)(2,1)S(1)} %pad_maximum_fusion.11.refs_0_), channel_id=1, source_target_pairs={{0,2},{1,3},{2,0},{3,1},{4,6},{5,7},{6,4},{7,5},{8,10},{9,11},{10,... | collective-permute-start | bytes 442376 | tf_op jit(solution)/shard_map/ppermute | solution.py:726
  119.2 12.8 %collective-permute-start.27 = (bf16[192,384]{1,0:T(8,128)(2,1)S(1)}, bf16[192,384]{1,0:T(8,128)(2,1)S(1)}, u32[]{:S(2)}, u32[]{:S(2)}) collective-permute-start(bf16[192,384]{1,0:T(8,128)(2,1)S(1)} %pad_maximum_fusion.11.refs_0_), channel_id=1, source_target_pairs={{0,1},{1,2},{2,3},{3,0},{4,5},{5,6},{6,7},{7,4},{8,9},{9,10},{10,1... | collective-permute-start | bytes 442376 | tf_op jit(solution)/shard_map/ppermute | solution.py:726
  (22 other events, 176.2 us)

commit v4 on v3

--- a/solution.py
+++ b/solution.py
@@ -600,7 +600,7 @@
 
 def query_kernel(chips, depth, rows, part, ids, sib_in, near_ref, far_ref, low_chips, high_chips, *refs):
     shares = refs[:depth]
-    small_in, gw_ref, keep_ref, send_ref, small_ref, sib_out, x_all, gq_all, q_scr, share_scr = refs[depth:]
+    small_in, gw_ref, keep_ref, send_ref, rows_ref, sib_out, x_all, gq_all, q_scr, share_scr = refs[depth:]
     c, j, z = ids[0], ids[1], ids[2]
     for ref, first, lane, place in crossed_blocks((near_ref, far_ref), chips, depth, rows, c, j, z, part, chips * part):
         x_all[pl.ds(place, rows), :] = ref[first:first + rows, lane:lane + part]
@@ -617,8 +617,6 @@
     width = gq.shape[1]
     span = shares[0].shape[1]
     bias = jnp.sum(gq.astype(F32), axis=0, keepdims=True)
-    small_ref[...] = small_in[...]
-    small_ref[7:8, :] = bias
     total = shares[0][...].astype(F32)
     for k in range(1, depth):
         total = total + shares[k][...].astype(F32)
@@ -628,8 +626,10 @@
     sib = pl.ds(pl.multiple_of((1 - c) * half, half), half)
     keep_ref[...] = share_scr[own, :].astype(BF)
     gw_ref[...] = q_scr[own, :]
-    send_ref[:, 0:span] = share_scr[sib, :].astype(BF)
-    send_ref[:, span:] = q_scr[sib, :].astype(BF)
+    send_ref[...] = share_scr[sib, :].astype(BF)
+    rows_ref[0:half, :] = q_scr[sib, :]
+    rows_ref[half:, :] = small_in[...]
+    rows_ref[half + 7:half + 8, :] = bias
 
 
 def assemble_kernel(depth, ids, after_ref, *refs):
@@ -639,7 +639,7 @@
     half, width = own_ref.shape
     span = shards[0].shape[1]
     out_ref[c, :, 0:width] = own_ref[...]
-    out_ref[1 - c, :, 0:width] = far_ref[:, span:].astype(F32)
+    out_ref[1 - c, :, 0:width] = far_ref[0:half, :]
     for k in range(depth):
         at = pl.multiple_of(width + lax.rem(z - k + depth, depth) * span, 128)
         out_ref[c, :, pl.ds(at, span)] = shards[k][0:half, :].astype(F32)
@@ -656,7 +656,7 @@
     gback_ref[0] = sib_ref[in_rows:in_rows + ghalf, :].astype(F32)
     gout_ref[0] = sib_ref[in_rows + ghalf:, :].astype(F32)
     for e in range(2):
-        small = jnp.where(c == e, own_ref[...], other_ref[...])
+        small = jnp.where(c == e, own_ref[half:, :], other_ref[half:, :])
         gains_ref[e] = small[0:2]
         shifts_ref[e] = small[2:4]
         outb_ref[e:e + 1, :] = small[4:5]
@@ -855,16 +855,17 @@
         [pl.BlockSpec((1, half, fc), lambda s, ids: (ids[0], 0, s)), out_block(ghalf, width), out_block(half, width), None],
         [vm((count, part), BF), vm((part, fc), F32), vm((fpart, width), F32), vm((part, width), F32)],
         grid=(steps,), vmem=24 if count <= 1024 else 60, work=(4e9, 12e6))
-    gw_q, keep, send, small, sib = kernel_call(
+    gw_q, keep, send, rows_q, sib = kernel_call(
         "query", functools.partial(query_kernel, chips, depth, rows, part), ids,
         [sib, near, far_z, gq_low, gq_high] + shares + [small], [ANY] + [None] * (depth + 5),
-        [shape_of((half, width), F32), shape_of((half, span), BF), shape_of((half, span + width), BF), shape_of((16, width), F32),
+        [shape_of((half, width), F32), shape_of((half, span), BF), shape_of((half, span), BF), shape_of((half + 16, width), F32),
          shape_of(sib.shape, BF)],
         [None] * 4 + [ANY],
         [vm((count, part), BF), vm((count, width), BF), vm((part, width), F32), vm((part, span), F32)], vmem=20 if count <= 1024 else 60, aliases={1: 4}, work=(1e9, 3e6))
+    far = swap(send)
     sib_far = swap(sib)
-    far = swap(send)
-    shards = over_depth(jnp.concatenate([keep, far[:, 0:span]], axis=0))
+    far_q = swap(rows_q)
+    shards = over_depth(jnp.concatenate([keep, far], axis=0))
     gx = kernel_call(
         "token_grad", functools.partial(token_grad_kernel, pack, lengths, rows, heads), ids,
         [far, question_lengths, passage_lengths, att, probs, a_low, b_low, first_rows],
@@ -874,7 +875,7 @@
         grid=(tokens // 256,), vmem=24 if count <= 1024 else 60, work=(2e9, 9e6))
 
     gin, gback, gout, g_qv, g_outb, g_gains, g_shifts, g_inb, g_backb = kernel_call(
-        "fill", functools.partial(fill_kernel, in_rows), ids, [gx[0], gin, gback, gout, sib_far, small, swap(small)],
+        "fill", functools.partial(fill_kernel, in_rows), ids, [gx[0], gin, gback, gout, sib_far, rows_q, far_q],
         [ANY, ANY, ANY, ANY, None, None, None],
         [shape_of(gin.shape, F32), shape_of(gback.shape, F32), shape_of(gout.shape, F32), shape_of((2, 2, width), F32),
          shape_of((2, width), F32), shape_of((2, 2, width), F32), shape_of((2, 2, width), F32), shape_of((2, ff), F32),
@@ -883,7 +884,7 @@
         aliases={2: 0, 3: 1, 4: 2}, vmem=20 if count <= 1024 else 60, work=(1e6, 8e6))
 
     (g_qkv,) = kernel_call(
-        "assemble", functools.partial(assemble_kernel, depth), ids, [gout] + shards + [gw_q, far], [ANY] + [None] * (depth + 2),
+        "assemble", functools.partial(assemble_kernel, depth), ids, [gout] + shards + [gw_q, far_q], [ANY] + [None] * (depth + 2),
         [shape_of((2, half, 3 * width), F32)], [None], vmem=20 if count <= 1024 else 60, work=(1e6, 3e6))
 
     return (

time: 135 us -> 135 us (level)
    unnamed x36 -> x37, local copies, waits for them, and re-layouts: 6.61 us -> 6.62 us
where the time goes in v4:
time: 135 us
  Pallas kernels  68.7 us (51%)
  starting transfers between devices  38.2 us (28%)
  waiting for transfers between devices  19.8 us (15%)
  local copies, waits for them, and re-layouts  6.8 us (5%)
    pallas_call x12, Pallas kernels, kernel_call(): pl.pallas_call(kernel, grid_spec=pltpu.PrefetchScalarGridSpec(num_scalar_...  68.7 us
    ppermute x9, starting transfers between devices, to_depth(): lax.ppermute(x, 'group', [(s, (s + k) % depth) for s in range(depth)])  18.9 us
    ppermute x9, starting transfers between devices, to_chip(): lax.ppermute(x, 'dp', [(s, (s // 2 + k) % chips * 2 + s % 2) for s in ran...  12 us
    ppermute x9, waiting for transfers between devices, to_depth(): lax.ppermute(x, 'group', [(s, (s + k) % depth) for s in range(depth)])  8.3 us
    unnamed x37, local copies, waits for them, and re-layouts  6.62 us
    ppermute x8, waiting for transfers between devices, swap(): return lax.ppermute(x, 'dp', [(k, k ^ 1) for k in range(n_dp)])  5.78 us
    ppermute x2, starting transfers between devices, xor_depth(): return lax.ppermute(x, 'group', [(s, s ^ mask) for s in range(depth)])  2.89 us
  transfers between devices with their start and end apart: 30, of which 13 were waited for; matrix products, arithmetic and copies ran while one was open for 1% of the time, Pallas kernels for 29%

profile of v4, /device:TPU:0, one launch (start us, length us, event | category | flops | bytes accessed | tf_op | source)
XLA Modules:
  0.0 134.8 jit_solution(452193285478461154)
XLA Ops:
  0.7 10.7 %attend.1 = (bf16[16,896]{1,0:T(8,128)(2,1)}, bf16[16,896]{1,0:T(8,128)(2,1)}, bf16[4,16,3456]{2,1,0:T(8,128)(2,1)}, bf16[4,16,3456]{2,1,0:T(8,128)(2,1)}, bf16[...) custom-call(s32[16]{0:T(128)} %qlen_ref.3, s32[4,4]{1,0:T(4,128)} %plen_ref.3, s32[16]{0:T(128)} %pos_ref.1, ...), custom_call_target="tpu_custom_call" | custom-call | flops 6000000000 | bytes 13000000 | tf_op jit(solution)/shard_map/attend/pallas_call | solution.py:685
  13.0 3.0 %collective-permute-start.1 = (bf16[32,896]{1,0:T(8,128)(2,1)S(1)}, bf16[32,896]{1,0:T(8,128)(2,1)S(1)}, u32[]{:S(2)}, u32[]{:S(2)}) collective-permute-start(bf16[32,896]{1,0:T(8,128)(2,1)S(1)} %get-tuple-element.157), channel_id=1, source_target_pairs={{0,1},{1,2},{2,3},{3,0},{4,5},{5,6},{6,7},{7,4},{8,9},{9,10},{10,1... | collective-permute-start | bytes 172040 | tf_op jit(solution)/shard_map/ppermute | solution.py:726
  16.0 2.0 %collective-permute-start.3 = (bf16[32,896]{1,0:T(8,128)(2,1)S(1)}, bf16[32,896]{1,0:T(8,128)(2,1)S(1)}, u32[]{:S(2)}, u32[]{:S(2)}) collective-permute-start(bf16[32,896]{1,0:T(8,128)(2,1)S(1)} %get-tuple-element.157), channel_id=1, source_target_pairs={{0,3},{1,0},{2,1},{3,2},{4,7},{5,4},{6,5},{7,6},{8,11},{9,8},{10,9... | collective-permute-start | bytes 172040 | tf_op jit(solution)/shard_map/ppermute | solution.py:726
  20.3 3.5 %collective-permute-done.2 = bf16[32,896]{1,0:T(8,128)(2,1)S(1)} collective-permute-done((bf16[32,896]{1,0:T(8,128)(2,1)S(1)}, bf16[32,896]{1,0:T(8,128)(2,1)S(1)}, u32[]{:S(2)}, u32[]{:S(2)}) %collective-permute-start.2) | collective-permute-done | bytes 57376 | tf_op jit(solution)/shard_map/ppermute | solution.py:726
  23.9 2.5 %collective-permute-start.6 = (bf16[128,896]{1,0:T(8,128)(2,1)S(1)}, bf16[128,896]{1,0:T(8,128)(2,1)S(1)}, u32[]{:S(2)}, u32[]{:S(2)}) collective-permute-start(bf16[128,896]{1,0:T(8,128)(2,1)S(1)} %constant_dynamic-update-slice_fusion.2.after_ref.refs_0_), channel_id=1, source_target_pairs={{0,24},{4,28},{8,0},{12,4},{16,8},{20,12},{24,16},{28,20},{1,25},{... | collective-permute-start | bytes 688136 | tf_op jit(solution)/shard_map/ppermute | solution.py:723
  30.3 6.5 %stage.1 = (bf16[768,3072]{1,0:T(8,128)(2,1)S(1)}, bf16[3072,768]{1,0:T(8,128)(2,1)S(1)}, bf16[768,768]{1,0:T(8,128)(2,1)S(1)}, bf16[2,1024,768]{2,1,0:T(8,128)(2,1)S(1)}, bf16[2,3,768,768]{3,2,1,0:T(8,128)(2,1)S(1)}) custom-call(s32[3]{0:T(128)S(1)} %pad_add_fusion.ids, bf16[128,896]{1,0:T(8,128)(2,1)S(1)} %constant_dynamic-update-slice_fusion.2.after_ref.refs_0_, ...), custom_call_target="tpu_custom_call" | custom-call | flops 5000000000 | bytes 10000000 | tf_op jit(solution)/shard_map/stage/pallas_call | solution.py:685
  38.3 11.3 %forward.1 = (bf16[512,768]{1,0:T(8,128)(2,1)S(1)}, bf16[512,3072]{1,0:T(8,128)(2,1)S(1)}, bf16[512,768]{1,0:T(8,128)(2,1)S(1)}, bf16[512,768]{1,0:T(8,128)(2,1)...) custom-call(s32[3]{0:T(128)S(1)} %pad_add_fusion.ids, ...), custom_call_target="tpu_custom_call", output_to_operand_aliasing={{7}: (11, {})} | custom-call | flops 10000000000 | bytes 18000000 | tf_op jit(solution)/shard_map/forward/pallas_call | solution.py:685
  53.2 1.9 %collective-permute-start.12 = (bf16[32,3456]{1,0:T(8,128)(2,1)S(1)}, bf16[32,3456]{1,0:T(8,128)(2,1)S(1)}, u32[]{:S(2)}, u32[]{:S(2)}) collective-permute-start(bf16[32,3456]{1,0:T(8,128)(2,1)S(1)} %pad_maximum_fusion.5), channel_id=1, source_target_pairs={{0,24},{4,28},{8,0},{12,4},{16,8},{20,12},{24,16},{28,20},{1,25},{... | collective-permute-start | bytes 663560 | tf_op jit(solution)/shard_map/ppermute | solution.py:723
  55.1 8.4 %loss.1 = (f32[512,768]{1,0:T(8,128)S(1)}, f32[1,16]{1,0:T(1,128)}, f32[16,1536]{1,0:T(8,128)S(1)}, f32[16,1536]{1,0:T(8,128)S(1)}, f32[8,768]{1,0:T(8,128)S(1)}...) custom-call(s32[3]{0:T(128)S(1)} %pad_add_fusion.ids, bf16[512,768]{1,0:T(8,128)(2,1)S(1)} %get-tuple-element.83.own_ref, ...), custom_call_target="tpu_custom_call" | custom-call | flops 8000000000 | bytes 16000000 | tf_op jit(solution)/shard_map/loss/pallas_call | solution.py:685
  64.8 4.5 %attend_back.1 = (bf16[4,16,3072]{2,1,0:T(8,128)(2,1)S(1)}, bf16[4,16,3072]{2,1,0:T(8,128)(2,1)S(1)}, bf16[2,192,1024]{2,1,0:T(8,128)(2,1)S(1)}, bf16[2,192,768]...) custom-call(s32[3]{0:T(128)S(1)} %pad_add_fusion.ids, ...), custom_call_target="tpu_custom_call" | custom-call | flops 6000000000 | bytes 16000000 | tf_op jit(solution)/shard_map/attend_back/pallas_call | solution.py:685
  73.7 2.5 %collective-permute-start.16 = (bf16[32,3072]{1,0:T(8,128)(2,1)S(1)}, bf16[32,3072]{1,0:T(8,128)(2,1)S(1)}, u32[]{:S(2)}, u32[]{:S(2)}) collective-permute-start(bf16[32,3072]{1,0:T(8,128)(2,1)S(1)} %pad_maximum_fusion.8), channel_id=1, source_target_pairs={{0,24},{4,28},{8,0},{12,4},{16,8},{20,12},{24,16},{28,20},{1,25},{... | collective-permute-start | bytes 589832 | tf_op jit(solution)/shard_map/ppermute | solution.py:723
  77.2 2.8 %collective-permute-start.18 = (bf16[64,2304]{1,0:T(8,128)(2,1)S(1)}, bf16[64,2304]{1,0:T(8,128)(2,1)S(1)}, u32[]{:S(2)}, u32[]{:S(2)}) collective-permute-start(bf16[64,2304]{1,0:T(8,128)(2,1)S(1)} %pad_maximum_fusion.near_ref), channel_id=1, source_target_pairs={{0,3},{1,2},{2,1},{3,0},{4,7},{5,6},{6,5},{7,4},{8,11},{9,10},{10,... | collective-permute-start | bytes 884744 | tf_op jit(solution)/shard_map/ppermute | solution.py:809
  80.0 9.0 %backward.1 = (bf16[512,3072]{1,0:T(8,128)(2,1)S(1)}, bf16[512,768]{1,0:T(8,128)(2,1)S(1)}, bf16[512,768]{1,0:T(8,128)(2,1)S(1)}, bf16[128,768]{1,0:T(8,128)(2,1...) custom-call(s32[3]{0:T(128)S(1)} %pad_add_fusion.ids, bf16[64,2304]{1,0:T(8,128)(2,1)S(1)} %pad_maximum_fusion.near_ref, ...), custom_call_target="tpu_custom_call" | custom-call | flops 12000000000 | bytes 18000000 | tf_op jit(solution)/shard_map/backward/pallas_call | solution.py:685
  89.9 2.8 %share.1 = (bf16[192,384]{1,0:T(8,128)(2,1)S(1)}, bf16[192,384]{1,0:T(8,128)(2,1)S(1)}, bf16[192,384]{1,0:T(8,128)(2,1)S(1)}, bf16[192,384]{1,0:T(8,128)(2,1)S(1)}, bf16[128,768]{1,0:T(8,128)(2,1)S(1)}) custom-call(s32[3]{0:T(128)S(1)} %pad_add_fusion.ids, bf16[32,3072]{1,0:T(8,128)(2,1)S(1)} %pad_maximum_fusion.1.refs_0_, ...), custom_call_target="tpu_custom_call" | custom-call | flops 1000000000 | bytes 3000000 | tf_op jit(solution)/shard_map/share/pallas_call | solution.py:685
  92.8 2.3 %collective-permute-done.19 = bf16[128,768]{1,0:T(8,128)(2,1)S(1)} collective-permute-done((bf16[128,768]{1,0:T(8,128)(2,1)S(1)}, bf16[128,768]{1,0:T(8,128)(2,1)S(1)}, u32[]{:S(2)}, u32[]{:S(2)}) %collective-permute-start.19) | collective-permute-done | bytes 196640 | tf_op jit(solution)/shard_map/ppermute | solution.py:812
  96.6 3.3 %collective-permute-start.21 = (bf16[192,384]{1,0:T(8,128)(2,1)S(1)}, bf16[192,384]{1,0:T(8,128)(2,1)S(1)}, u32[]{:S(2)}, u32[]{:S(2)}) collective-permute-start(bf16[192,384]{1,0:T(8,128)(2,1)S(1)} %get-tuple-element.114), channel_id=1, source_target_pairs={{0,1},{1,2},{2,3},{3,0},{4,5},{5,6},{6,7},{7,4},{8,9},{9,10},{10,1... | collective-permute-start | bytes 442376 | tf_op jit(solution)/shard_map/ppermute | solution.py:726
  101.1 2.9 %collective-permute-start.23 = (bf16[192,384]{1,0:T(8,128)(2,1)S(1)}, bf16[192,384]{1,0:T(8,128)(2,1)S(1)}, u32[]{:S(2)}, u32[]{:S(2)}) collective-permute-start(bf16[192,384]{1,0:T(8,128)(2,1)S(1)} %get-tuple-element.116), channel_id=1, source_target_pairs={{0,3},{1,0},{2,1},{3,2},{4,7},{5,4},{6,5},{7,6},{8,11},{9,8},{10,9... | collective-permute-start | bytes 442376 | tf_op jit(solution)/shard_map/ppermute | solution.py:726
  104.0 5.2 %weight.1 = (f32[2,96,3072]{2,1,0:T(8,128)}, f32[2,384,768]{2,1,0:T(8,128)}, f32[2,96,768]{2,1,0:T(8,128)}, bf16[864,768]{1,0:T(8,128)(2,1)S(1)}) custom-call(s32[3]{0:T(128)S(1)} %pad_add_fusion.ids, bf16[192,384]{1,0:T(8,128)(2,1)S(1)} %get-tuple-element.106.after_ref.refs_0_, bf16[64,2304]{1,0:T(8,128)(2,1)S(1)} %pad_maximum_fusion.near_ref, ...), custom_call_target="tpu_custom_call" | custom-call | flops 4000000000 | bytes 12000000 | tf_op jit(solution)/shard_map/weight/pallas_call | solution.py:685
  111.5 2.6 %collective-permute-done.24.after_ref = bf16[96,384]{1,0:T(8,128)(2,1)S(1)} collective-permute-done((bf16[96,384]{1,0:T(8,128)(2,1)S(1)}, bf16[96,384]{1,0:T(8,128)(2,1)S(1)}, u32[]{:S(2)}, u32[]{:S(2)}) %collective-permute-start.24) | collective-permute-done | bytes 73760 | tf_op jit(solution)/shard_map/ppermute | solution.py:720
  114.1 4.9 %collective-permute-start.29 = (bf16[192,384]{1,0:T(8,128)(2,1)S(1)}, bf16[192,384]{1,0:T(8,128)(2,1)S(1)}, u32[]{:S(2)}, u32[]{:S(2)}) collective-permute-start(bf16[192,384]{1,0:T(8,128)(2,1)S(1)} %constant_dynamic-update-slice_fusion.9.refs_0_), channel_id=1, source_target_pairs={{0,3},{1,0},{2,1},{3,2},{4,7},{5,4},{6,5},{7,6},{8,11},{9,8},{10,9... | collective-permute-start | bytes 442376 | tf_op jit(solution)/shard_map/ppermute | solution.py:726
  119.6 5.1 %token_grad.1 = (f32[1024,768]{1,0:T(8,128)}, f32[1024,768]{1,0:T(8,128)}) custom-call(s32[3]{0:T(128)S(1)} %pad_add_fusion.ids, bf16[96,384]{1,0:T(8,128)(2,1)S(1)} %collective-permute-done.24.after_ref, s32[16]{0:T(128)S(1)} %copy-done.12, s32[4,4]{1,0:T(4,128)S(1)} %copy-done.11, bf16[2,192,1024]{2,1,0:T(8,128)(2,1)S(1)} %get-tuple-element.119.att_ref, ...), custom_call_target="tpu_custom_call" | custom-call | flops 2000000000 | bytes 9000000 | tf_op jit(solution)/shard_map/token_grad/pallas_call | solution.py:685
  124.8 1.9 %copy-done = f32[1024,768]{1,0:T(8,128)S(1)} copy-done((f32[1024,768]{1,0:T(8,128)S(1)}, f32[1024,768]{1,0:T(8,128)}, u32[]{:S(2)}) %copy-start) | copy-done | bytes 3145752
  126.6 2.2 %fill.1 = (f32[2,96,3072]{2,1,0:T(8,128)}, f32[2,384,768]{2,1,0:T(8,128)}, f32[2,96,768]{2,1,0:T(8,128)}, f32[2,2,768]{2,1,0:T(2,128)}, f32[2,768]{1,0:T(2,128)}...) custom-call(s32[3]{0:T(128)S(1)} %pad_add_fusion.ids, ...), custom_call_target="tpu_custom_call", output_to_operand_aliasing={{0}: (2, {}), {1}: (3, {}), {2}: (4, {})} | custom-call | flops 1000000 | bytes 8000000 | tf_op jit(solution)/shard_map/fill/pallas_call | solution.py:685
  128.8 3.0 %collective-permute-done.28.refs_2_ = bf16[192,384]{1,0:T(8,128)(2,1)S(1)} collective-permute-done((bf16[192,384]{1,0:T(8,128)(2,1)S(1)}, bf16[192,384]{1,0:T(8,128)(2,1)S(1)}, u32[]{:S(2)}, u32[]{:S(2)}) %collective-permute-start.28) | collective-permute-done | bytes 147488 | tf_op jit(solution)/shard_map/ppermute | solution.py:726
  (107 shorter events, 29.0 us)
Async XLA Ops:
  13.0 7.3 %collective-permute-start.1 = (bf16[32,896]{1,0:T(8,128)(2,1)S(1)}, bf16[32,896]{1,0:T(8,128)(2,1)S(1)}, u32[]{:S(2)}, u32[]{:S(2)}) collective-permute-start(bf16[32,896]{1,0:T(8,128)(2,1)S(1)} %get-tuple-element.157), channel_id=1, source_target_pairs={{0,1},{1,2},{2,3},{3,0},{4,5},{5,6},{6,7},{7,4},{8,9},{9,10},{10,1... | collective-permute-start | bytes 172040 | tf_op jit(solution)/shard_map/ppermute | solution.py:726
  16.0 7.8 %collective-permute-start.3 = (bf16[32,896]{1,0:T(8,128)(2,1)S(1)}, bf16[32,896]{1,0:T(8,128)(2,1)S(1)}, u32[]{:S(2)}, u32[]{:S(2)}) collective-permute-start(bf16[32,896]{1,0:T(8,128)(2,1)S(1)} %get-tuple-element.157), channel_id=1, source_target_pairs={{0,3},{1,0},{2,1},{3,2},{4,7},{5,4},{6,5},{7,6},{8,11},{9,8},{10,9... | collective-permute-start | bytes 172040 | tf_op jit(solution)/shard_map/ppermute | solution.py:726
  18.0 5.8 %collective-permute-start.2 = (bf16[32,896]{1,0:T(8,128)(2,1)S(1)}, bf16[32,896]{1,0:T(8,128)(2,1)S(1)}, u32[]{:S(2)}, u32[]{:S(2)}) collective-permute-start(bf16[32,896]{1,0:T(8,128)(2,1)S(1)} %get-tuple-element.157), channel_id=1, source_target_pairs={{0,2},{1,3},{2,0},{3,1},{4,6},{5,7},{6,4},{7,5},{8,10},{9,11},{10,... | collective-permute-start | bytes 172040 | tf_op jit(solution)/shard_map/ppermute | solution.py:726
  23.9 13.0 %collective-permute-start.6 = (bf16[128,896]{1,0:T(8,128)(2,1)S(1)}, bf16[128,896]{1,0:T(8,128)(2,1)S(1)}, u32[]{:S(2)}, u32[]{:S(2)}) collective-permute-start(bf16[128,896]{1,0:T(8,128)(2,1)S(1)} %constant_dynamic-update-slice_fusion.2.after_ref.refs_0_), channel_id=1, source_target_pairs={{0,24},{4,28},{8,0},{12,4},{16,8},{20,12},{24,16},{28,20},{1,25},{... | collective-permute-start | bytes 688136 | tf_op jit(solution)/shard_map/ppermute | solution.py:723
  26.4 11.8 %collective-permute-start.5 = (bf16[128,896]{1,0:T(8,128)(2,1)S(1)}, bf16[128,896]{1,0:T(8,128)(2,1)S(1)}, u32[]{:S(2)}, u32[]{:S(2)}) collective-permute-start(bf16[128,896]{1,0:T(8,128)(2,1)S(1)} %constant_dynamic-update-slice_fusion.2.after_ref.refs_0_), channel_id=1, source_target_pairs={{0,16},{4,20},{8,24},{12,28},{16,0},{20,4},{24,8},{28,12},{1,17},{... | collective-permute-start | bytes 688136 | tf_op jit(solution)/shard_map/ppermute | solution.py:723
  26.9 11.3 %collective-permute-start.4 = (bf16[128,896]{1,0:T(8,128)(2,1)S(1)}, bf16[128,896]{1,0:T(8,128)(2,1)S(1)}, u32[]{:S(2)}, u32[]{:S(2)}) collective-permute-start(bf16[128,896]{1,0:T(8,128)(2,1)S(1)} %constant_dynamic-update-slice_fusion.2.after_ref.refs_0_), channel_id=1, source_target_pairs={{0,8},{4,12},{8,16},{12,20},{16,24},{20,28},{24,0},{28,4},{1,9},{5... | collective-permute-start | bytes 688136 | tf_op jit(solution)/shard_map/ppermute | solution.py:723
  51.5 12.1 %collective-permute-start.10 = (bf16[32,3456]{1,0:T(8,128)(2,1)S(1)}, bf16[32,3456]{1,0:T(8,128)(2,1)S(1)}, u32[]{:S(2)}, u32[]{:S(2)}) collective-permute-start(bf16[32,3456]{1,0:T(8,128)(2,1)S(1)} %pad_maximum_fusion.3), channel_id=1, source_target_pairs={{0,8},{4,12},{8,16},{12,20},{16,24},{20,28},{24,0},{28,4},{1,9},{5... | collective-permute-start | bytes 663560 | tf_op jit(solution)/shard_map/ppermute | solution.py:723
  52.6 12.0 %collective-permute-start.11 = (bf16[32,3456]{1,0:T(8,128)(2,1)S(1)}, bf16[32,3456]{1,0:T(8,128)(2,1)S(1)}, u32[]{:S(2)}, u32[]{:S(2)}) collective-permute-start(bf16[32,3456]{1,0:T(8,128)(2,1)S(1)} %pad_maximum_fusion.4), channel_id=1, source_target_pairs={{0,16},{4,20},{8,24},{12,28},{16,0},{20,4},{24,8},{28,12},{1,17},{... | collective-permute-start | bytes 663560 | tf_op jit(solution)/shard_map/ppermute | solution.py:723
  53.2 11.4 %collective-permute-start.12 = (bf16[32,3456]{1,0:T(8,128)(2,1)S(1)}, bf16[32,3456]{1,0:T(8,128)(2,1)S(1)}, u32[]{:S(2)}, u32[]{:S(2)}) collective-permute-start(bf16[32,3456]{1,0:T(8,128)(2,1)S(1)} %pad_maximum_fusion.5), channel_id=1, source_target_pairs={{0,24},{4,28},{8,0},{12,4},{16,8},{20,12},{24,16},{28,20},{1,25},{... | collective-permute-start | bytes 663560 | tf_op jit(solution)/shard_map/ppermute | solution.py:723
  71.2 6.0 %collective-permute-start.17 = (bf16[32,2304]{1,0:T(8,128)(2,1)S(1)}, bf16[32,2304]{1,0:T(8,128)(2,1)S(1)}, u32[]{:S(2)}, u32[]{:S(2)}) collective-permute-start(bf16[32,2304]{1,0:T(8,128)(2,1)S(1)} %pad_maximum_fusion.10), channel_id=1, source_target_pairs={{0,1},{1,0},{2,3},{3,2},{4,5},{5,4},{6,7},{7,6},{8,9},{9,8},{10,11... | collective-permute-start | bytes 442376 | tf_op jit(solution)/shard_map/ppermute | solution.py:809
  71.3 18.6 %collective-permute-start.14 = (bf16[32,3072]{1,0:T(8,128)(2,1)S(1)}, bf16[32,3072]{1,0:T(8,128)(2,1)S(1)}, u32[]{:S(2)}, u32[]{:S(2)}) collective-permute-start(bf16[32,3072]{1,0:T(8,128)(2,1)S(1)} %pad_maximum_fusion.6), channel_id=1, source_target_pairs={{0,8},{4,12},{8,16},{12,20},{16,24},{20,28},{24,0},{28,4},{1,9},{5... | collective-permute-start | bytes 589832 | tf_op jit(solution)/shard_map/ppermute | solution.py:723
  72.1 17.8 %collective-permute-start.15 = (bf16[32,3072]{1,0:T(8,128)(2,1)S(1)}, bf16[32,3072]{1,0:T(8,128)(2,1)S(1)}, u32[]{:S(2)}, u32[]{:S(2)}) collective-permute-start(bf16[32,3072]{1,0:T(8,128)(2,1)S(1)} %pad_maximum_fusion.7), channel_id=1, source_target_pairs={{0,16},{4,20},{8,24},{12,28},{16,0},{20,4},{24,8},{28,12},{1,17},{... | collective-permute-start | bytes 589832 | tf_op jit(solution)/shard_map/ppermute | solution.py:723
  73.7 16.2 %collective-permute-start.16 = (bf16[32,3072]{1,0:T(8,128)(2,1)S(1)}, bf16[32,3072]{1,0:T(8,128)(2,1)S(1)}, u32[]{:S(2)}, u32[]{:S(2)}) collective-permute-start(bf16[32,3072]{1,0:T(8,128)(2,1)S(1)} %pad_maximum_fusion.8), channel_id=1, source_target_pairs={{0,24},{4,28},{8,0},{12,4},{16,8},{20,12},{24,16},{28,20},{1,25},{... | collective-permute-start | bytes 589832 | tf_op jit(solution)/shard_map/ppermute | solution.py:723
  77.2 11.9 %collective-permute-start.18 = (bf16[64,2304]{1,0:T(8,128)(2,1)S(1)}, bf16[64,2304]{1,0:T(8,128)(2,1)S(1)}, u32[]{:S(2)}, u32[]{:S(2)}) collective-permute-start(bf16[64,2304]{1,0:T(8,128)(2,1)S(1)} %pad_maximum_fusion.near_ref), channel_id=1, source_target_pairs={{0,3},{1,2},{2,1},{3,0},{4,7},{5,6},{6,5},{7,4},{8,11},{9,10},{10,... | collective-permute-start | bytes 884744 | tf_op jit(solution)/shard_map/ppermute | solution.py:809
  89.1 5.9 %collective-permute-start.19 = (bf16[128,768]{1,0:T(8,128)(2,1)S(1)}, bf16[128,768]{1,0:T(8,128)(2,1)S(1)}, u32[]{:S(2)}, u32[]{:S(2)}) collective-permute-start(bf16[128,768]{1,0:T(8,128)(2,1)S(1)} %pad_maximum_fusion.9.refs_9_), channel_id=1, source_target_pairs={{0,8},{4,12},{8,0},{12,4},{16,24},{20,28},{24,16},{28,20},{1,9},{5... | collective-permute-start | bytes 589832 | tf_op jit(solution)/shard_map/ppermute | solution.py:812
  95.1 14.6 %collective-permute-start.20 = (bf16[256,768]{1,0:T(8,128)(2,1)S(1)}, bf16[256,768]{1,0:T(8,128)(2,1)S(1)}, u32[]{:S(2)}, u32[]{:S(2)}) collective-permute-start(bf16[256,768]{1,0:T(8,128)(2,1)S(1)} %constant_dynamic-update-slice_fusion.7.low_chips), channel_id=1, source_target_pairs={{0,16},{4,20},{8,24},{12,28},{16,0},{20,4},{24,8},{28,12},{1,17},{... | collective-permute-start | bytes 1179656 | tf_op jit(solution)/shard_map/ppermute | solution.py:812
  96.6 12.6 %collective-permute-start.21 = (bf16[192,384]{1,0:T(8,128)(2,1)S(1)}, bf16[192,384]{1,0:T(8,128)(2,1)S(1)}, u32[]{:S(2)}, u32[]{:S(2)}) collective-permute-start(bf16[192,384]{1,0:T(8,128)(2,1)S(1)} %get-tuple-element.114), channel_id=1, source_target_pairs={{0,1},{1,2},{2,3},{3,0},{4,5},{5,6},{6,7},{7,4},{8,9},{9,10},{10,1... | collective-permute-start | bytes 442376 | tf_op jit(solution)/shard_map/ppermute | solution.py:726
  99.9 9.8 %collective-permute-start.22 = (bf16[192,384]{1,0:T(8,128)(2,1)S(1)}, bf16[192,384]{1,0:T(8,128)(2,1)S(1)}, u32[]{:S(2)}, u32[]{:S(2)}) collective-permute-start(bf16[192,384]{1,0:T(8,128)(2,1)S(1)} %get-tuple-element.115), channel_id=1, source_target_pairs={{0,2},{1,3},{2,0},{3,1},{4,6},{5,7},{6,4},{7,5},{8,10},{9,11},{10,... | collective-permute-start | bytes 442376 | tf_op jit(solution)/shard_map/ppermute | solution.py:726
  101.1 8.6 %collective-permute-start.23 = (bf16[192,384]{1,0:T(8,128)(2,1)S(1)}, bf16[192,384]{1,0:T(8,128)(2,1)S(1)}, u32[]{:S(2)}, u32[]{:S(2)}) collective-permute-start(bf16[192,384]{1,0:T(8,128)(2,1)S(1)} %get-tuple-element.116), channel_id=1, source_target_pairs={{0,3},{1,0},{2,1},{3,2},{4,7},{5,4},{6,5},{7,6},{8,11},{9,8},{10,9... | collective-permute-start | bytes 442376 | tf_op jit(solution)/shard_map/ppermute | solution.py:726
  110.8 13.9 %collective-permute-start.25 = (bf16[864,768]{1,0:T(8,128)(2,1)S(1)}, bf16[864,768]{1,0:T(8,128)(2,1)S(1)}, u32[]{:S(2)}, u32[]{:S(2)}) collective-permute-start(bf16[864,768]{1,0:T(8,128)(2,1)S(1)} %get-tuple-element.128), channel_id=1, source_target_pairs={{0,4},{4,0},{8,12},{12,8},{16,20},{20,16},{24,28},{28,24},{1,5},{5... | collective-permute-start | bytes 3981320 | tf_op jit(solution)/shard_map/ppermute | solution.py:720
  111.4 13.3 %collective-permute-start.26 = (f32[112,768]{1,0:T(8,128)S(1)}, f32[112,768]{1,0:T(8,128)S(1)}, u32[]{:S(2)}, u32[]{:S(2)}) collective-permute-start(f32[112,768]{1,0:T(8,128)S(1)} %get-tuple-element.129.own_ref), channel_id=1, source_target_pairs={{0,4},{4,0},{8,12},{12,8},{16,20},{20,16},{24,28},{28,24},{1,5},{5... | collective-permute-start | bytes 1032200 | tf_op jit(solution)/shard_map/ppermute | solution.py:720
  114.1 14.7 %collective-permute-start.29 = (bf16[192,384]{1,0:T(8,128)(2,1)S(1)}, bf16[192,384]{1,0:T(8,128)(2,1)S(1)}, u32[]{:S(2)}, u32[]{:S(2)}) collective-permute-start(bf16[192,384]{1,0:T(8,128)(2,1)S(1)} %constant_dynamic-update-slice_fusion.9.refs_0_), channel_id=1, source_target_pairs={{0,3},{1,0},{2,1},{3,2},{4,7},{5,4},{6,5},{7,6},{8,11},{9,8},{10,9... | collective-permute-start | bytes 442376 | tf_op jit(solution)/shard_map/ppermute | solution.py:726
  119.0 12.8 %collective-permute-start.28 = (bf16[192,384]{1,0:T(8,128)(2,1)S(1)}, bf16[192,384]{1,0:T(8,128)(2,1)S(1)}, u32[]{:S(2)}, u32[]{:S(2)}) collective-permute-start(bf16[192,384]{1,0:T(8,128)(2,1)S(1)} %constant_dynamic-update-slice_fusion.9.refs_0_), channel_id=1, source_target_pairs={{0,2},{1,3},{2,0},{3,1},{4,6},{5,7},{6,4},{7,5},{8,10},{9,11},{10,... | collective-permute-start | bytes 442376 | tf_op jit(solution)/shard_map/ppermute | solution.py:726
  119.0 12.8 %collective-permute-start.27 = (bf16[192,384]{1,0:T(8,128)(2,1)S(1)}, bf16[192,384]{1,0:T(8,128)(2,1)S(1)}, u32[]{:S(2)}, u32[]{:S(2)}) collective-permute-start(bf16[192,384]{1,0:T(8,128)(2,1)S(1)} %constant_dynamic-update-slice_fusion.9.refs_0_), channel_id=1, source_target_pairs={{0,1},{1,2},{2,3},{3,0},{4,5},{5,6},{6,7},{7,4},{8,9},{9,10},{10,1... | collective-permute-start | bytes 442376 | tf_op jit(solution)/shard_map/ppermute | solution.py:726
  (22 other events, 175.3 us)
